TPU v7x, 32 devices: a whole 2x2x4 slice. The times are simulated.
32 devices in a mesh: exp: 4 (over x, core), fsdp: 8 (over z, y).
Axes of the slice: x: 2, y: 2, z: 4, core: 2. Of those that a mesh axis runs over, the one named last changes fastest.
Arguments:
- tokens: bfloat16 [4096, 1536], P(('exp', 'fsdp')), may hold values from -6 to 6
- expert_ids: int32 [4096, 2], P(('exp', 'fsdp')), may hold values from 0 to 3, all different within a row; in each aligned block of 128 rows (0 to 127, 128 to 255, ...) at most 96 rows name the same one
- gates: float32 [4096, 2], P(('exp', 'fsdp')), may hold values from 0.1 to 1
- w_in: bfloat16 [4, 2048, 1536], P('exp', 'fsdp'), may hold values from -0.15625 to 0.15625
- w_out: bfloat16 [4, 2048, 1536], P('exp', 'fsdp'), may hold values from -0.125 to 0.125
- grad_y: bfloat16 [4096, 1536], P(('exp', 'fsdp')), may hold values from -6 to 6
Outputs:
- mixed: bfloat16 [4096, 1536], P(('exp', 'fsdp'))
- grad_tokens: bfloat16 [4096, 1536], P(('exp', 'fsdp'))
- grad_w_in: float32 [4, 2048, 1536], P('exp', 'fsdp')
- grad_w_out: float32 [4, 2048, 1536], P('exp', 'fsdp')
- grad_gates: float32 [4096, 2], P(('exp', 'fsdp'))
Inputs may be any that keep to these rules, and one draw needn't show every extreme that they name: `expert_ids`: each row names two different experts. Among the rows of one device no expert is named by more than 96 rows, and in some device some expert is named by exactly 96 rows.
All inputs are finite; a program needn't handle non-finite values.
Results may differ from a plain program's by a relative error of at most 0.0065.
Values may be sent and summed in bfloat16 or wider, within the bound.
No kernel may reach another device: no remote copies, remote signals or barrier semaphores. Data moves between devices by JAX's collectives and lax.ppermute only.
A program may use at most 192 MiB of HBM per device.

v0:
```python
import jax
import jax.numpy as jnp
from jax import lax
from jax.sharding import PartitionSpec as P

inv_sqrt_two = 0.7071067811865476
inv_sqrt_two_pi = 0.3989422804014327


def gelu_parts(values):
    cdf_part = 0.5 * (1.0 + jax.scipy.special.erf(values * inv_sqrt_two))
    return (
        values * cdf_part,
        cdf_part + values * jnp.exp(-0.5 * values * values) * inv_sqrt_two_pi,
    )


def contract_first(left, right):
    return lax.dot_general(
        left, right, (((0,), (0,)), ((), ())), preferred_element_type=jnp.float32
    )


def contract_last(left, right):
    return lax.dot_general(
        left, right, (((1,), (1,)), ((), ())), preferred_element_type=jnp.float32
    )


def shards(tokens, expert_ids, gates, w_in, w_out, grad_y):
    tok_rows, features = tokens.shape
    groups = lax.axis_size("exp")
    capacity = 3 * tok_rows // groups
    slot_count = 2 * tok_rows
    buffer_rows = groups * capacity
    flat_ids = expert_ids.reshape(-1)
    onehot = (flat_ids[:, None] == jnp.arange(groups, dtype=jnp.int32)[None, :]).astype(jnp.int32)
    slot_rank = jnp.sum((jnp.cumsum(onehot, axis=0) - 1) * onehot, axis=1)
    slot_index = flat_ids * capacity + slot_rank
    token_slots = jnp.repeat(tokens, 2, axis=0)
    grad_slots = (
        (gates[:, :, None] * grad_y[:, None, :]).astype(jnp.bfloat16).reshape(slot_count, features)
    )
    send_tokens = jnp.zeros((buffer_rows, features), jnp.bfloat16).at[slot_index].set(token_slots)
    send_grads = jnp.zeros((buffer_rows, features), jnp.bfloat16).at[slot_index].set(grad_slots)
    recv_tokens, recv_grads = (
        lax.all_to_all(
            send_tokens.reshape(groups, capacity, features),
            "exp",
            split_axis=0,
            concat_axis=0,
            tiled=True,
        ),
        lax.all_to_all(
            send_grads.reshape(groups, capacity, features),
            "exp",
            split_axis=0,
            concat_axis=0,
            tiled=True,
        ),
    )
    recv_tokens = recv_tokens.reshape(buffer_rows, features)
    recv_grads = recv_grads.reshape(buffer_rows, features)
    full_in, full_out = (
        lax.all_gather(w_in, "fsdp", axis=1, tiled=True),
        lax.all_gather(w_out, "fsdp", axis=1, tiled=True),
    )
    full_in = full_in[0]
    full_out = full_out[0]
    hidden_pre = contract_last(recv_tokens, full_in)
    act_full, slope_term = gelu_parts(hidden_pre)
    act_bf = act_full.astype(jnp.bfloat16)
    expert_out = jnp.dot(act_bf, full_out, preferred_element_type=jnp.float32).astype(jnp.bfloat16)
    expert_out = expert_out.reshape(groups, capacity, features)
    back_out = lax.all_to_all(expert_out, "exp", split_axis=0, concat_axis=0, tiled=True)
    again_in, again_out = (
        lax.all_gather(w_in, "fsdp", axis=1, tiled=True),
        lax.all_gather(w_out, "fsdp", axis=1, tiled=True),
    )
    back_in_weight = again_in[0]
    back_out_weight = again_out[0]
    grad_act = contract_last(recv_grads, back_out_weight)
    grad_hidden = (grad_act * slope_term).astype(jnp.bfloat16)
    input_grad = jnp.dot(grad_hidden, back_in_weight, preferred_element_type=jnp.float32).astype(
        jnp.bfloat16
    )
    input_grad = input_grad.reshape(groups, capacity, features)
    back_input = lax.all_to_all(input_grad, "exp", split_axis=0, concat_axis=0, tiled=True)
    out_three = (
        back_out.reshape(buffer_rows, features)[slot_index]
        .reshape(tok_rows, 2, features)
        .astype(jnp.float32)
    )
    mixed = jnp.sum(gates[:, :, None] * out_three, axis=1).astype(jnp.bfloat16)
    grad_gates = jnp.sum(grad_y.astype(jnp.float32)[:, None, :] * out_three, axis=-1)
    input_three = (
        back_input.reshape(buffer_rows, features)[slot_index]
        .reshape(tok_rows, 2, features)
        .astype(jnp.float32)
    )
    grad_tokens = jnp.sum(input_three, axis=1).astype(jnp.bfloat16)
    summed = lax.psum_scatter(
        jnp.concatenate(
            [contract_first(grad_hidden, recv_tokens), contract_first(act_bf, recv_grads)], axis=1
        ),
        "fsdp",
        scatter_dimension=0,
        tiled=True,
    )
    grad_in = summed[:, :features]
    grad_out = summed[:, features:]
    return (mixed, grad_tokens, grad_in[None], grad_out[None], grad_gates)


def solution(mesh):
    return jax.shard_map(
        shards,
        mesh=mesh,
        in_specs=(
            P(("exp", "fsdp"), None),
            P(("exp", "fsdp"), None),
            P(("exp", "fsdp"), None),
            P("exp", "fsdp", None),
            P("exp", "fsdp", None),
            P(("exp", "fsdp"), None),
        ),
        out_specs=(
            P(("exp", "fsdp"), None),
            P(("exp", "fsdp"), None),
            P("exp", "fsdp", None),
            P("exp", "fsdp", None),
            P(("exp", "fsdp"), None),
        ),
        check_vma=False,
    )
```

profile of v0, /device:TPU:0, one launch (start us, length us, event | category | flops | bytes accessed | tf_op | source)
XLA Modules:
  0.0 654.9 jit_solution(5956456060445289031)
XLA Ops:
  11.7 2.9 scatter_custom_fusion
  14.7 4.3 all-to-all-start
  21.2 3.0 scatter_custom_fusion.1
  24.2 11.3 %all-to-all-done = bf16[4,96,1536]{2,1,0:T(8,128)(2,1)} async-done(((bf16[4,96,1536]{2,1,0:T(8,128)(2,1)}), bf16[4,96,1536]{2,1,0:T(8,128)(2,1)}, u32[]{:S(2)}, u32[]{:S(2)}) %all-to-all-start) | async-done | bytes 1179680 | tf_op jit(solution)/shard_map/all_to_all | solution.py:47
  35.5 3.5 all-to-all-start.2
  39.1 73.0 %all-gather.3.cloned.1.call-done = bf16[1,2048,1536]{2,1,0:T(8,128)(2,1)} async-done(((bf16[1,256,1536]{2,1,0:T(8,128)(2,1)}), bf16[1,2048,1536]{2,1,0:T(8,128)(2,1)}) %all-gather.3.cloned.1.call-update) | async-done | bytes 6291472 | tf_op jit(solution)/shard_map/all_gather | solution.py:65
  112.0 7.5 %multiply_convert_fusion = (bf16[384,2048]{1,0:T(8,128)(2,1)S(1)}, f32[384,2048]{1,0:T(8,128)}) fusion(bf16[384,1536]{1,0:T(8,128)(2,1)} %bitcast.5, bf16[1,2048,1536]{2,1,0:T(8,128)(2,1)} %all-gather.3.cloned.1.call-done), kind=kOutput, calls=%fused_computation.20 | convolution fusion | flops 2419851264 | bytes 12189696 | tf_op jit(solution)/shard_map/dot_general | solution.py:25
  119.5 91.9 %all-gather.5.cloned.1.call-done = bf16[1,2048,1536]{2,1,0:T(8,128)(2,1)} async-done(((bf16[1,256,1536]{2,1,0:T(8,128)(2,1)}), bf16[1,2048,1536]{2,1,0:T(8,128)(2,1)}) %all-gather.5.cloned.1.call-update) | async-done | bytes 6291472 | tf_op jit(solution)/shard_map/all_gather | solution.py:66
  211.4 7.8 %fusion.13 = bf16[384,2048]{1,0:T(8,128)(2,1)S(1)} fusion(f32[384,2048]{1,0:T(8,128)} %get-tuple-element.25, bf16[384,1536]{1,0:T(8,128)(2,1)S(1)} %bitcast.59, bf16[1,2048,1536]{2,1,0:T(8,128)(2,1)} %all-gather.5.cloned.1.call-done), kind=kOutput, calls=%fused_computation.19 | convolution fusion | flops 2423783424 | bytes 12189696 | tf_op jit(solution)/shard_map/dot_general | solution.py:25
  219.3 5.3 fusion.29
  224.6 3.5 fusion.30
  228.0 12.2 %pad_maximum_fusion = f32[2048,3072]{0,1:T(8,128)} fusion(f32[2048,1536]{0,1:T(8,128)S(1)} %fusion.30, f32[2048,1536]{0,1:T(8,128)S(1)} %fusion.29), kind=kLoop, calls=%fused_computation.4 | loop fusion | flops 6291456 | bytes 50331648 | tf_op jit(solution)/shard_map/concatenate | solution.py:103
  240.2 6.4 fusion.19
  246.6 3.9 all-to-all-start.1
  250.5 6.4 fusion.16
  256.9 9.2 %all-to-all-done.1 = bf16[4,96,1536]{2,1,0:T(8,128)(2,1)S(1)} async-done(((bf16[4,96,1536]{2,1,0:T(8,128)(2,1)}), bf16[4,96,1536]{2,1,0:T(8,128)(2,1)S(1)}, u32[]{:S(2)}, u32[]{:S(2)}) %all-to-all-start.1) | async-done | bytes 1179680 | tf_op jit(solution)/shard_map/all_to_all | solution.py:75
  266.1 3.5 all-to-all-start.3
  269.8 2.1 gather_fusion
  271.9 13.6 %all-to-all-done.3 = bf16[4,96,1536]{2,1,0:T(8,128)(2,1)S(1)} async-done(((bf16[4,96,1536]{2,1,0:T(8,128)(2,1)}), bf16[4,96,1536]{2,1,0:T(8,128)(2,1)S(1)}, u32[]{:S(2)}, u32[]{:S(2)}) %all-to-all-start.3) | async-done | bytes 1179680 | tf_op jit(solution)/shard_map/all_to_all | solution.py:88
  287.6 2.2 reshape.118
  289.8 2.9 reduce_sum.44
  292.7 2.2 reshape.119
  294.9 3.5 multiply_reduce_fusion
  299.1 344.0 %reduce-scatter.2.cloned.1.call-done = f32[256,3072]{0,1:T(8,128)} async-done(((f32[2048,3072]{0,1:T(8,128)}), f32[256,3072]{0,1:T(8,128)}) %reduce-scatter.2.cloned.1.call-update) | async-done | bytes 3145744 | tf_op jit(solution)/shard_map/reduce_scatter | solution.py:102
  (52 shorter events, 14.9 us)
Async XLA Ops:
  7.2 1.5 copy-start.6
  7.2 3.7 copy-start.5
  7.2 104.8 %all-gather.3.cloned.1.call-start = ((), (), s32[]{:S(2)}) async-start(), calls=%async_computation.5 | async-start | bytes 7077888 | tf_op jit(solution)/shard_map/all_gather | solution.py:65
  7.9 203.5 %all-gather.5.cloned.1.call-start = ((), (), s32[]{:S(2)}) async-start(), calls=%async_computation.6 | async-start | bytes 7077888 | tf_op jit(solution)/shard_map/all_gather | solution.py:66
  11.7 7.2 %copy-start.7 = (f32[128,2]{0,1:T(2,128)S(1)}, f32[128,2]{0,1:T(2,128)}, u32[]{:S(2)}) copy-start(f32[128,2]{0,1:T(2,128)} %param.8) | copy-start | bytes 3076
  11.7 8.0 %copy-start.2 = (bf16[128,1536]{1,0:T(8,128)(2,1)S(1)}, bf16[128,1536]{1,0:T(8,128)(2,1)}, u32[]{:S(2)}) copy-start(bf16[128,1536]{1,0:T(8,128)(2,1)} %param.11) | copy-start | bytes 1179652
  14.7 20.8 %all-to-all-start = ((bf16[4,96,1536]{2,1,0:T(8,128)(2,1)}), bf16[4,96,1536]{2,1,0:T(8,128)(2,1)}, u32[]{:S(2)}, u32[]{:S(2)}) async-start(bf16[4,96,1536]{2,1,0:T(8,128)(2,1)} %bitcast.4), calls=%async_computation | async-start | bytes 2359296 | tf_op jit(solution)/shard_map/all_to_all | solution.py:47
  19.1 0.6 copy-start.3
  35.5 84.0 %all-to-all-start.2 = ((bf16[4,96,1536]{2,1,0:T(8,128)(2,1)}), bf16[4,96,1536]{2,1,0:T(8,128)(2,1)S(1)}, u32[]{:S(2)}, u32[]{:S(2)}) async-start(bf16[4,96,1536]{2,1,0:T(8,128)(2,1)} %bitcast.10), calls=%async_computation.2 | async-start | bytes 2359296 | tf_op jit(solution)/shard_map/all_to_all | solution.py:54
  39.0 604.1 %reduce-scatter.2.cloned.1.call-start = ((), (), s32[]{:S(2)}) async-start(), calls=%async_computation.7 | async-start | bytes 28311552 | tf_op jit(solution)/shard_map/reduce_scatter | solution.py:102
  219.2 5.3 copy-start
  246.6 3.9 copy-start.1
  246.6 19.5 %all-to-all-start.1 = ((bf16[4,96,1536]{2,1,0:T(8,128)(2,1)}), bf16[4,96,1536]{2,1,0:T(8,128)(2,1)S(1)}, u32[]{:S(2)}, u32[]{:S(2)}) async-start(bf16[4,96,1536]{2,1,0:T(8,128)(2,1)} %bitcast.62), calls=%async_computation.1 | async-start | bytes 2359296 | tf_op jit(solution)/shard_map/all_to_all | solution.py:75
  266.1 19.4 %all-to-all-start.3 = ((bf16[4,96,1536]{2,1,0:T(8,128)(2,1)}), bf16[4,96,1536]{2,1,0:T(8,128)(2,1)S(1)}, u32[]{:S(2)}, u32[]{:S(2)}) async-start(bf16[4,96,1536]{2,1,0:T(8,128)(2,1)} %bitcast.61), calls=%async_computation.3 | async-start | bytes 2359296 | tf_op jit(solution)/shard_map/all_to_all | solution.py:88
  289.8 5.1 copy-start.4
Sparse Core Ops, SparseCore 0:
  10.2 101.7 all-gather.2
  114.2 97.2 all-gather.4
  240.3 402.6 reduce-scatter.1
where the time goes:
time: 656 us; the launch traced here: 655 us
  waiting for transfers between devices  544 us (83%)
  matrix products  36.8 us (6%)
  other arithmetic  23 us (4%)
  local copies, waits for them, and re-layouts  21.4 us (3%)
  starting transfers between devices  15.3 us (2%)
  between operations  14 us (2%)
    reduce_scatter x1, waiting for transfers between devices, shards(): lax.psum_scatter(jnp.concatenate([contract_first(grad_hidden, recv_tokens...  344 us
    all_gather x1, waiting for transfers between devices, shards(): lax.all_gather(w_out, 'fsdp', axis=1, tiled=True)  91.9 us
    all_gather x1, waiting for transfers between devices, shards(): lax.all_gather(w_in, 'fsdp', axis=1, tiled=True)  73 us
    dot_general x2, matrix products, contract_last(): lax.dot_general(left, right, (((1,), (1,)), ((), ())), preferred_element_...  15.3 us
    all_to_all x1, waiting for transfers between devices, shards(): lax.all_to_all(input_grad, 'exp', split_axis=0, concat_axis=0, tiled=True)  13.6 us
  transfers between devices with their start and end apart: 7, of which 6 were waited for; matrix products, arithmetic and copies ran while one was open for 7% of the time, Pallas kernels for 0%

commit v1 on v0

v1 whole, which is shorter than its diff:
```python
import jax
import jax.numpy as jnp
from jax import lax
from jax.sharding import PartitionSpec as P

inv_sqrt_two = 0.7071067811865476
inv_sqrt_two_pi = 0.3989422804014327
AXES = ("exp", "fsdp")
CORES = 2
DEPTH = 4


def gelu_parts(values):
    cdf_part = 0.5 * (1.0 + jax.scipy.special.erf(values * inv_sqrt_two))
    return (
        values * cdf_part,
        cdf_part + values * jnp.exp(-0.5 * values * values) * inv_sqrt_two_pi,
    )


def contract_first(left, right):
    return lax.dot_general(
        left, right, (((0,), (0,)), ((), ())), preferred_element_type=jnp.float32
    )


def contract_last(left, right):
    return lax.dot_general(
        left, right, (((1,), (1,)), ((), ())), preferred_element_type=jnp.float32
    )


class Grid:
    def __init__(self, n_exp, n_fsdp):
        self.nx, self.ny = n_exp // CORES, n_fsdp // DEPTH

    def move(self, array, to):
        pairs = []
        for x in range(self.nx):
            for c in range(CORES):
                for z in range(DEPTH):
                    for y in range(self.ny):
                        tx, tc, tz, ty = to(x, c, z, y)
                        pairs.append((self.index(x, c, z, y), self.index(tx, tc, tz, ty)))
        return lax.ppermute(array, AXES, pairs)

    def index(self, x, c, z, y):
        return ((x * CORES + c) * DEPTH + z) * self.ny + y

    def from_x(self, array, step):
        return self.move(array, lambda x, c, z, y: ((x - step) % self.nx, c, z, y))

    def from_y(self, array, step):
        return self.move(array, lambda x, c, z, y: (x, c, z, (y - step) % self.ny))

    def to_x(self, array, step):
        return self.move(array, lambda x, c, z, y: ((x + step) % self.nx, c, z, y))

    def to_y(self, array, step):
        return self.move(array, lambda x, c, z, y: (x, c, z, (y + step) % self.ny))

    def swap_core(self, array):
        return self.move(array, lambda x, c, z, y: (x, 1 - c, z, y))

    def swap_far(self, array):
        return self.move(array, lambda x, c, z, y: (x, c, z ^ 2, y))

    def swap_near(self, array):
        return self.move(array, lambda x, c, z, y: (x, c, z ^ 1, y))


def wide(array):
    return array.astype(jnp.float32)


def total(parts):
    out = wide(parts[0])
    for part in parts[1:]:
        out = out + wide(part)
    return out


def shards(tokens, expert_ids, gates, w_in, w_out, grad_y):
    rows, features = tokens.shape
    n_exp, n_fsdp = lax.axis_size("exp"), lax.axis_size("fsdp")
    grid = Grid(n_exp, n_fsdp)
    nx, ny = grid.nx, grid.ny
    hidden = w_in.shape[1]
    bf = jnp.bfloat16
    own_expert = lax.axis_index("exp")

    far_tokens, far_grads = grid.swap_far(tokens), grid.swap_far(grad_y)
    w_in, w_out = w_in[0], w_out[0]
    near_in, near_out = grid.swap_near(w_in), grid.swap_near(w_out)

    ids_row = expert_ids.T[None, :, :]
    named = ids_row == jnp.arange(n_exp, dtype=jnp.int32)[:, None, None]
    gate_rows = jnp.sum(jnp.where(named, gates.T[None], 0.0), axis=1)
    gate_rows = jnp.stack([gate_rows, grid.swap_far(gate_rows)])
    gate_rows = jnp.stack([gate_rows] + [grid.from_x(gate_rows, s) for s in range(1, nx)])
    gate_rows = jnp.stack([gate_rows] + [grid.from_y(gate_rows, s) for s in range(1, ny)])

    def spread_tokens(base):
        along = [base] + [grid.from_x(base, s) for s in range(1, nx)]
        return [along] + [[grid.from_y(part, s) for part in along] for s in range(1, ny)]

    def spread_grads(base):
        along = [base] + [grid.from_y(base, s) for s in range(1, ny)]
        return [[part] + [grid.from_x(part, s) for s in range(1, nx)] for part in along]

    def flat(table):
        return jnp.concatenate([part for line in table for part in line], axis=0)

    half_tokens = [flat(spread_tokens(base)) for base in (tokens, far_tokens)]
    half_grads = [flat(spread_grads(base)) for base in (grad_y, far_grads)]

    core_in, core_out = grid.swap_core(w_in), grid.swap_core(w_out)
    core_near_in, core_near_out = grid.swap_core(near_in), grid.swap_core(near_out)
    all_in = jnp.concatenate([w_in, near_in, core_in, core_near_in], axis=0)
    all_out = jnp.concatenate([w_out, near_out, core_out, core_near_out], axis=0)
    expert_pair = jnp.stack([own_expert, own_expert ^ 1])

    mixed_parts, input_parts, score_parts, acts, hiddens = [], [], [], [], []
    for half in range(2):
        scale = jnp.take(gate_rows[:, :, half], expert_pair, axis=2)
        scale = jnp.moveaxis(scale, 2, -1).reshape(-1, 2)
        pre = contract_last(half_tokens[half], all_in)
        act, slope = gelu_parts(pre)
        back = contract_last(half_grads[half], all_out)
        spread = jnp.repeat(scale, 2 * hidden, axis=1)
        act_scaled = (act * spread).astype(bf)
        grad_hidden = (back * slope * spread).astype(bf)
        score = jnp.sum((act * back).reshape(-1, 2, 2 * hidden), axis=-1)
        acts.append(act_scaled)
        hiddens.append(grad_hidden)
        score_parts.append(score)
        mixed_parts.append(jnp.dot(act_scaled, all_out, preferred_element_type=jnp.float32).astype(bf))
        input_parts.append(jnp.dot(grad_hidden, all_in, preferred_element_type=jnp.float32).astype(bf))

    def table(array):
        return array.reshape((ny, nx, rows) + array.shape[1:])

    def gather_yx(array):
        part = table(array)
        lines = [
            total([part[0, xo]] + [grid.to_y(part[s, xo], s) for s in range(1, ny)]).astype(array.dtype)
            for xo in range(nx)
        ]
        return total([lines[0]] + [grid.to_x(lines[s], s) for s in range(1, nx)]).astype(array.dtype)

    def gather_xy(array):
        part = table(array)
        lines = [
            total([part[yo, 0]] + [grid.to_x(part[yo, s], s) for s in range(1, nx)]).astype(array.dtype)
            for yo in range(ny)
        ]
        return total([lines[0]] + [grid.to_y(lines[s], s) for s in range(1, ny)]).astype(array.dtype)

    def home(parts, gather):
        far = grid.swap_far(gather(parts[1]))
        return wide(gather(parts[0])) + wide(far)

    mixed = home(mixed_parts, gather_yx).astype(bf)
    grad_tokens = home(input_parts, gather_xy).astype(bf)

    def score_of(score):
        row = jnp.zeros((n_exp, score.shape[0]), jnp.float32).at[expert_pair].set(score.T)
        return row.reshape(n_exp, ny, nx, rows)

    scores = jnp.stack([score_of(s) for s in score_parts], axis=1)
    scores = total([scores[:, :, 0]] + [grid.to_y(scores[:, :, s], s) for s in range(1, ny)])
    scores = total([scores[:, :, 0]] + [grid.to_x(scores[:, :, s], s) for s in range(1, nx)])
    scores = scores[:, 0] + grid.swap_far(scores[:, 1])
    picked = jnp.sum(jnp.where(named, scores[:, None, :], 0.0), axis=0)
    grad_gates = picked.T

    both_tokens = jnp.concatenate(half_tokens, axis=0)
    both_grads = jnp.concatenate(half_grads, axis=0)
    both_acts = jnp.concatenate(acts, axis=0)
    both_hiddens = jnp.concatenate(hiddens, axis=0)
    span = 2 * hidden

    def weight_grad(left, right):
        other = contract_first(left[:, span:], right).astype(bf)
        mine = contract_first(left[:, :span], right)
        both = mine + wide(grid.swap_core(other))
        return both[:hidden] + wide(grid.swap_near(both[hidden:].astype(bf)))

    grad_in = weight_grad(both_hiddens, both_tokens)
    grad_out = weight_grad(both_acts, both_grads)
    return (mixed, grad_tokens, grad_in[None], grad_out[None], grad_gates)


def solution(mesh):
    rows = P(AXES, None)
    weights = P("exp", "fsdp", None)
    return jax.shard_map(
        shards,
        mesh=mesh,
        in_specs=(rows, rows, rows, weights, weights, rows),
        out_specs=(rows, rows, weights, weights, rows),
        check_vma=False,
    )
```

time: 656 us -> 291 us (0.44)
  waiting for transfers between devices: 544 us -> 157 us
  starting transfers between devices: 15.3 us -> 43.7 us
  local copies, waits for them, and re-layouts: 21.4 us -> 36.7 us
  between operations: 14 us -> 1.31 us
  other arithmetic: 23 us -> 14.8 us
    reduce_scatter x1 -> x0, waiting for transfers between devices: 344 us -> none  [shards(): lax.psum_scatter(jnp.concatenate([contract_first(grad_hidden, recv_tokens...]
    all_gather x2 -> x0, waiting for transfers between devices: 165 us -> none  [the longest x1 91.9 us: shards(): lax.all_gather(w_out, 'fsdp', axis=1, tiled=True)]
    ppermute x0 -> x44, waiting for transfers between devices: none -> 157 us  [move(): return lax.ppermute(array, AXES, pairs)]
    ppermute x0 -> x44, starting transfers between devices: none -> 43.7 us  [move(): return lax.ppermute(array, AXES, pairs)]
    all_to_all x4 -> x0, waiting for transfers between devices: 34.1 us -> none  [the longest x1 13.6 us: shards(): lax.all_to_all(input_grad, 'exp', split_axis=0, concat_axis=0, tiled=True)]
    unnamed x21 -> x91, local copies, waits for them, and re-layouts: 4.61 us -> 21.3 us
    all_to_all x4 -> x0, starting transfers between devices: 15.2 us -> none  [the longest x1 4.27 us: shards(): lax.all_to_all(send_tokens.reshape(groups, capacity, features), 'exp', sp...]
    concatenate x1 -> x0, other arithmetic: 12.2 us -> none  [shards(): jnp.concatenate([contract_first(grad_hidden, recv_tokens), contract_first...]
  transfers between devices with their start and end apart: 7 -> 44, of which waited for: 6 -> 25; matrix products, arithmetic and copies ran while one was open for 7% -> 18% of each run, Pallas kernels for 0% -> 0%
where the time goes in v1:
time: 291 us; the launch traced here: 289 us
  waiting for transfers between devices  157 us (54%)
  starting transfers between devices  43.7 us (15%)
  local copies, waits for them, and re-layouts  36.7 us (13%)
  matrix products  35.4 us (12%)
  other arithmetic  14.8 us (5%)
    ppermute x44, waiting for transfers between devices, move(): return lax.ppermute(array, AXES, pairs)  157 us
    ppermute x44, starting transfers between devices, move(): return lax.ppermute(array, AXES, pairs)  43.7 us
    unnamed x91, local copies, waits for them, and re-layouts  21.3 us
    dot_general x4, matrix products, contract_last(): lax.dot_general(left, right, (((1,), (1,)), ((), ())), preferred_element_...  17.5 us
    reshape x2, local copies, waits for them, and re-layouts, shards(): score = jnp.sum((act * back).reshape(-1, 2, 2 * hidden), axis=-1)  8.01 us
    dot_general x4, matrix products, contract_first(): lax.dot_general(left, right, (((0,), (0,)), ((), ())), preferred_element_...  7.34 us
    dot_general x2, matrix products, shards(): jnp.dot(grad_hidden, all_in, preferred_element_type=jnp.float32).astype(bf)  6.31 us
  transfers between devices with their start and end apart: 44, of which 25 were waited for; matrix products, arithmetic and copies ran while one was open for 18% of the time, Pallas kernels for 0%

profile of v1, /device:TPU:0, one launch (start us, length us, event | category | flops | bytes accessed | tf_op | source)
XLA Modules:
  0.0 289.3 jit_solution(5309220945933436443)
XLA Ops:
  22.2 7.1 %collective-permute-done.15 = bf16[128,1536]{1,0:T(8,128)(2,1)} collective-permute-done((bf16[128,1536]{1,0:T(8,128)(2,1)}, bf16[128,1536]{1,0:T(8,128)(2,1)}, u32[]{:S(2)}, u32[]{:S(2)}) %collective-permute-start.15) | collective-permute-done | bytes 393248 | tf_op jit(solution)/shard_map/ppermute | solution.py:45
  35.4 14.0 %collective-permute-done.29 = bf16[128,1536]{1,0:T(8,128)(2,1)S(1)} collective-permute-done((bf16[128,1536]{1,0:T(8,128)(2,1)S(1)}, bf16[128,1536]{1,0:T(8,128)(2,1)S(1)}, u32[]{:S(2)}, u32[]{:S(2)}) %collective-permute-start.29) | collective-permute-done | bytes 393248 | tf_op jit(solution)/shard_map/ppermute | solution.py:45
  54.6 13.8 %collective-permute-done.16 = bf16[128,1536]{1,0:T(8,128)(2,1)S(1)} collective-permute-done((bf16[128,1536]{1,0:T(8,128)(2,1)}, bf16[128,1536]{1,0:T(8,128)(2,1)S(1)}, u32[]{:S(2)}, u32[]{:S(2)}) %collective-permute-start.16) | collective-permute-done | bytes 393248 | tf_op jit(solution)/shard_map/ppermute | solution.py:45
  72.0 8.5 %collective-permute-done.17 = bf16[128,1536]{1,0:T(8,128)(2,1)S(1)} collective-permute-done((bf16[128,1536]{1,0:T(8,128)(2,1)}, bf16[128,1536]{1,0:T(8,128)(2,1)S(1)}, u32[]{:S(2)}, u32[]{:S(2)}) %collective-permute-start.17) | collective-permute-done | bytes 393248 | tf_op jit(solution)/shard_map/ppermute | solution.py:45
  81.1 7.9 %collective-permute-done.18 = bf16[128,1536]{1,0:T(8,128)(2,1)S(1)} collective-permute-done((bf16[128,1536]{1,0:T(8,128)(2,1)S(1)}, bf16[128,1536]{1,0:T(8,128)(2,1)S(1)}, u32[]{:S(2)}, u32[]{:S(2)}) %collective-permute-start.18) | collective-permute-done | bytes 393248 | tf_op jit(solution)/shard_map/ppermute | solution.py:45
  90.5 3.6 %fusion.24 = f32[512,1024]{1,0:T(8,128)S(1)} fusion(bf16[128,1536]{1,0:T(8,128)(2,1)S(1)} %collective-permute-done.18, bf16[128,1536]{1,0:T(8,128)(2,1)S(1)} %collective-permute-done.17, bf16[128,1536]{1,0:T(8,128)(2,1)S(1)} %collective-permute-done.16, bf16[128,1536]{1,0:T(8,128)(2,1)} %collective-permute-done.15, ...), kind=kOutput, calls=%fused_computation.52 | convolution fusion | flops 1629487104 | bytes 6815744 | tf_op jit(solution)/shard_map/dot_general | solution.py:28
  94.2 5.0 %collective-permute-done.32 = bf16[128,1536]{1,0:T(8,128)(2,1)S(1)} collective-permute-done((bf16[128,1536]{1,0:T(8,128)(2,1)S(1)}, bf16[128,1536]{1,0:T(8,128)(2,1)S(1)}, u32[]{:S(2)}, u32[]{:S(2)}) %collective-permute-start.32) | collective-permute-done | bytes 393248 | tf_op jit(solution)/shard_map/ppermute | solution.py:45
  99.3 3.9 %multiply_multiply_fusion.2 = (f32[512,1024]{1,0:T(8,128)}, f32[512,1024]{1,0:T(8,128)}) fusion(f32[512,1024]{1,0:T(8,128)S(1)} %fusion.24, bf16[256,1536]{1,0:T(8,128)(2,1)S(1)} %collective-permute-done.11, bf16[256,1536]{1,0:T(8,128)(2,1)S(1)} %collective-permute-done.10, bf16[256,1536]{1,0:T(8,128)(2,1)S(1)} %collective-permute-done.9, ...), kind=kOutput, calls=%fused_computation.82 | convolution fusion | flops 1632108544 | bytes 11010048 | tf_op jit(solution)/shard_map/dot_general | solution.py:28
  103.2 4.0 %reshape.158 = f32[512,2,512]{2,1,0:T(2,128)} reshape(f32[512,1024]{1,0:T(8,128)} %get-tuple-element.32) | data formatting | bytes 4194304 | tf_op jit(solution)/shard_map/reshape | solution.py:133
  110.3 4.3 %fusion.16 = f32[512,1024]{1,0:T(8,128)S(1)} fusion(bf16[128,1536]{1,0:T(8,128)(2,1)} %collective-permute-done.2, bf16[128,1536]{1,0:T(8,128)(2,1)} %copy-done.14, bf16[128,1536]{1,0:T(8,128)(2,1)} %collective-permute-done, bf16[128,1536]{1,0:T(8,128)(2,1)} %param.8, bf16[256,1536]{1,0:T(8,128)(2,1)} %copy-done.31, ...), kind=kOutput, calls=%fused_computation.44 | convolution fusion | flops 1629487104 | bytes 6815744 | tf_op jit(solution)/shard_map/dot_general | solution.py:28
  114.7 5.7 %multiply_multiply_fusion.3 = (f32[512,1024]{1,0:T(8,128)}, f32[512,1024]{1,0:T(8,128)}) fusion(f32[512,1024]{1,0:T(8,128)S(1)} %fusion.16, bf16[256,1536]{1,0:T(8,128)(2,1)S(1)} %copy-done.34, bf16[256,1536]{1,0:T(8,128)(2,1)S(1)} %copy-done.29, bf16[256,1536]{1,0:T(8,128)(2,1)S(1)} %copy-done.26, bf16[256,1536]{1,0:T(8,128)(2,1)S(1)} %bitcast.171, ...), kind=kOutput, calls=%fused_computation.83 | convolution fusion | flops 1632108544 | bytes 11010048 | tf_op jit(solution)/shard_map/dot_general | solution.py:28
  120.4 4.0 %reshape.157 = f32[512,2,512]{2,1,0:T(2,128)} reshape(f32[512,1024]{1,0:T(8,128)} %get-tuple-element.30) | data formatting | bytes 4194304 | tf_op jit(solution)/shard_map/reshape | solution.py:133
  138.2 3.5 %collective-permute-done.43 = f32[4,128]{1,0:T(4,128)S(1)} collective-permute-done((f32[4,128]{1,0:T(4,128)S(1)}, f32[4,128]{1,0:T(4,128)S(1)}, u32[]{:S(2)}, u32[]{:S(2)}) %collective-permute-start.43) | collective-permute-done | bytes 2080 | tf_op jit(solution)/shard_map/ppermute | solution.py:45
  143.9 3.5 %collective-permute-done.6 = f32[4,128]{1,0:T(4,128)S(1)} collective-permute-done((f32[4,128]{1,0:T(4,128)S(1)}, f32[4,128]{1,0:T(4,128)S(1)}, u32[]{:S(2)}, u32[]{:S(2)}) %collective-permute-start.6) | collective-permute-done | bytes 2080 | tf_op jit(solution)/shard_map/ppermute | solution.py:45
  187.2 6.8 %collective-permute-done.34 = bf16[128,1536]{1,0:T(8,128)(2,1)S(1)} collective-permute-done((bf16[128,1536]{1,0:T(8,128)(2,1)S(1)}, bf16[128,1536]{1,0:T(8,128)(2,1)S(1)}, u32[]{:S(2)}, u32[]{:S(2)}) %collective-permute-start.34) | collective-permute-done | bytes 393248 | tf_op jit(solution)/shard_map/ppermute | solution.py:45
  194.7 8.7 %collective-permute-done.13 = bf16[128,1536]{1,0:T(8,128)(2,1)S(1)} collective-permute-done((bf16[128,1536]{1,0:T(8,128)(2,1)S(1)}, bf16[128,1536]{1,0:T(8,128)(2,1)S(1)}, u32[]{:S(2)}, u32[]{:S(2)}) %collective-permute-start.13) | collective-permute-done | bytes 393248 | tf_op jit(solution)/shard_map/ppermute | solution.py:45
  204.0 8.7 %collective-permute-done.20 = bf16[128,1536]{1,0:T(8,128)(2,1)S(1)} collective-permute-done((bf16[128,1536]{1,0:T(8,128)(2,1)S(1)}, bf16[128,1536]{1,0:T(8,128)(2,1)S(1)}, u32[]{:S(2)}, u32[]{:S(2)}) %collective-permute-start.20) | collective-permute-done | bytes 393248 | tf_op jit(solution)/shard_map/ppermute | solution.py:45
  214.8 9.6 %collective-permute-done.35 = bf16[128,1536]{1,0:T(8,128)(2,1)S(1)} collective-permute-done((bf16[128,1536]{1,0:T(8,128)(2,1)S(1)}, bf16[128,1536]{1,0:T(8,128)(2,1)S(1)}, u32[]{:S(2)}, u32[]{:S(2)}) %collective-permute-start.35) | collective-permute-done | bytes 393248 | tf_op jit(solution)/shard_map/ppermute | solution.py:45
  226.1 4.3 %collective-permute-done.19 = bf16[128,1536]{1,0:T(8,128)(2,1)S(1)} collective-permute-done((bf16[128,1536]{1,0:T(8,128)(2,1)S(1)}, bf16[128,1536]{1,0:T(8,128)(2,1)S(1)}, u32[]{:S(2)}, u32[]{:S(2)}) %collective-permute-start.19) | collective-permute-done | bytes 393248 | tf_op jit(solution)/shard_map/ppermute | solution.py:45
  232.9 8.3 %collective-permute-done.28 = bf16[128,1536]{1,0:T(8,128)(2,1)S(1)} collective-permute-done((bf16[128,1536]{1,0:T(8,128)(2,1)S(1)}, bf16[128,1536]{1,0:T(8,128)(2,1)S(1)}, u32[]{:S(2)}, u32[]{:S(2)}) %collective-permute-start.28) | collective-permute-done | bytes 393248 | tf_op jit(solution)/shard_map/ppermute | solution.py:45
  242.8 10.6 %collective-permute-done.36 = bf16[128,1536]{1,0:T(8,128)(2,1)S(1)} collective-permute-done((bf16[128,1536]{1,0:T(8,128)(2,1)S(1)}, bf16[128,1536]{1,0:T(8,128)(2,1)S(1)}, u32[]{:S(2)}, u32[]{:S(2)}) %collective-permute-start.36) | collective-permute-done | bytes 393248 | tf_op jit(solution)/shard_map/ppermute | solution.py:45
  260.4 5.1 %collective-permute-done.22 = bf16[128,1536]{1,0:T(8,128)(2,1)S(1)} collective-permute-done((bf16[128,1536]{1,0:T(8,128)(2,1)S(1)}, bf16[128,1536]{1,0:T(8,128)(2,1)S(1)}, u32[]{:S(2)}, u32[]{:S(2)}) %collective-permute-start.22) | collective-permute-done | bytes 393248 | tf_op jit(solution)/shard_map/ppermute | solution.py:45
  266.5 13.0 %collective-permute-done.40 = bf16[256,1536]{1,0:T(8,128)(2,1)S(1)} collective-permute-done((bf16[256,1536]{1,0:T(8,128)(2,1)S(1)}, bf16[256,1536]{1,0:T(8,128)(2,1)S(1)}, u32[]{:S(2)}, u32[]{:S(2)}) %collective-permute-start.40) | collective-permute-done | bytes 786464 | tf_op jit(solution)/shard_map/ppermute | solution.py:45
  280.9 7.1 %collective-permute-done.38 = bf16[256,1536]{1,0:T(8,128)(2,1)S(1)} collective-permute-done((bf16[256,1536]{1,0:T(8,128)(2,1)S(1)}, bf16[256,1536]{1,0:T(8,128)(2,1)S(1)}, u32[]{:S(2)}, u32[]{:S(2)}) %collective-permute-start.38) | collective-permute-done | bytes 786464 | tf_op jit(solution)/shard_map/ppermute | solution.py:45
  (218 shorter events, 116.9 us)
Async XLA Ops:
  0.6 50.3 %collective-permute-start.3 = (bf16[256,1536]{1,0:T(8,128)(2,1)}, bf16[256,1536]{1,0:T(8,128)(2,1)}, u32[]{:S(2)}, u32[]{:S(2)}) collective-permute-start(bf16[256,1536]{1,0:T(8,128)(2,1)} %bitcast.162), channel_id=1, source_target_pairs={{0,2},{1,3},{2,0},{3,1},{4,6},{5,7},{6,4},{7,5},{8,10},{9,11},{10,... | collective-permute-start | bytes 2359304 | tf_op jit(solution)/shard_map/ppermute | solution.py:45
  3.7 48.7 %collective-permute-start.4 = (bf16[256,1536]{1,0:T(8,128)(2,1)}, bf16[256,1536]{1,0:T(8,128)(2,1)}, u32[]{:S(2)}, u32[]{:S(2)}) collective-permute-start(bf16[256,1536]{1,0:T(8,128)(2,1)} %bitcast.163), channel_id=1, source_target_pairs={{0,8},{1,9},{2,10},{3,11},{4,12},{5,13},{6,14},{7,15},{8,0},{9,1},... | collective-permute-start | bytes 2359304 | tf_op jit(solution)/shard_map/ppermute | solution.py:45
  6.7 22.5 %collective-permute-start.15 = (bf16[128,1536]{1,0:T(8,128)(2,1)}, bf16[128,1536]{1,0:T(8,128)(2,1)}, u32[]{:S(2)}, u32[]{:S(2)}) collective-permute-start(bf16[128,1536]{1,0:T(8,128)(2,1)} %param.8), channel_id=1, source_target_pairs={{0,4},{1,5},{2,6},{3,7},{4,0},{5,1},{6,2},{7,3},{8,12},{9,13},{10,... | collective-permute-start | bytes 1179656 | tf_op jit(solution)/shard_map/ppermute | solution.py:45
  15.6 17.1 %collective-permute-start = (bf16[128,1536]{1,0:T(8,128)(2,1)}, bf16[128,1536]{1,0:T(8,128)(2,1)}, u32[]{:S(2)}, u32[]{:S(2)}) collective-permute-start(bf16[128,1536]{1,0:T(8,128)(2,1)} %param.8), channel_id=1, source_target_pairs={{0,16},{1,17},{2,18},{3,19},{4,20},{5,21},{6,22},{7,23},{8,24},{9,... | collective-permute-start | bytes 1179656 | tf_op jit(solution)/shard_map/ppermute | solution.py:45
  29.3 20.2 %collective-permute-start.29 = (bf16[128,1536]{1,0:T(8,128)(2,1)S(1)}, bf16[128,1536]{1,0:T(8,128)(2,1)S(1)}, u32[]{:S(2)}, u32[]{:S(2)}) collective-permute-start(bf16[128,1536]{1,0:T(8,128)(2,1)S(1)} %copy-done.8), channel_id=1, source_target_pairs={{0,4},{1,5},{2,6},{3,7},{4,0},{5,1},{6,2},{7,3},{8,12},{9,13},{10,... | collective-permute-start | bytes 1179656 | tf_op jit(solution)/shard_map/ppermute | solution.py:45
  32.7 35.7 %collective-permute-start.9 = (bf16[256,1536]{1,0:T(8,128)(2,1)}, bf16[256,1536]{1,0:T(8,128)(2,1)S(1)}, u32[]{:S(2)}, u32[]{:S(2)}) collective-permute-start(bf16[256,1536]{1,0:T(8,128)(2,1)} %bitcast.168), channel_id=1, source_target_pairs={{0,2},{1,3},{2,0},{3,1},{4,6},{5,7},{6,4},{7,5},{8,10},{9,11},{10,... | collective-permute-start | bytes 2359304 | tf_op jit(solution)/shard_map/ppermute | solution.py:45
  32.9 20.1 %collective-permute-start.25 = (bf16[128,1536]{1,0:T(8,128)(2,1)}, bf16[128,1536]{1,0:T(8,128)(2,1)S(1)}, u32[]{:S(2)}, u32[]{:S(2)}) collective-permute-start(bf16[128,1536]{1,0:T(8,128)(2,1)} %collective-permute-done.24), channel_id=1, source_target_pairs={{0,16},{1,17},{2,18},{3,19},{4,20},{5,21},{6,22},{7,23},{8,24},{9,... | collective-permute-start | bytes 1179656 | tf_op jit(solution)/shard_map/ppermute | solution.py:45
  49.4 19.5 %collective-permute-start.31 = (bf16[128,1536]{1,0:T(8,128)(2,1)S(1)}, bf16[128,1536]{1,0:T(8,128)(2,1)S(1)}, u32[]{:S(2)}, u32[]{:S(2)}) collective-permute-start(bf16[128,1536]{1,0:T(8,128)(2,1)S(1)} %collective-permute-done.29), channel_id=1, source_target_pairs={{0,1},{1,0},{2,3},{3,2},{4,5},{5,4},{6,7},{7,6},{8,9},{9,8},{10,11... | collective-permute-start | bytes 1179656 | tf_op jit(solution)/shard_map/ppermute | solution.py:45
  51.0 19.5 %collective-permute-start.30 = (bf16[128,1536]{1,0:T(8,128)(2,1)S(1)}, bf16[128,1536]{1,0:T(8,128)(2,1)S(1)}, u32[]{:S(2)}, u32[]{:S(2)}) collective-permute-start(bf16[128,1536]{1,0:T(8,128)(2,1)S(1)} %collective-permute-done.29), channel_id=1, source_target_pairs={{0,16},{1,17},{2,18},{3,19},{4,20},{5,21},{6,22},{7,23},{8,24},{9,... | collective-permute-start | bytes 1179656 | tf_op jit(solution)/shard_map/ppermute | solution.py:45
  53.0 37.5 %collective-permute-start.5 = (bf16[256,1536]{1,0:T(8,128)(2,1)}, bf16[256,1536]{1,0:T(8,128)(2,1)S(1)}, u32[]{:S(2)}, u32[]{:S(2)}) collective-permute-start(bf16[256,1536]{1,0:T(8,128)(2,1)} %collective-permute-done.3), channel_id=1, source_target_pairs={{0,8},{1,9},{2,10},{3,11},{4,12},{5,13},{6,14},{7,15},{8,0},{9,1},... | collective-permute-start | bytes 2359304 | tf_op jit(solution)/shard_map/ppermute | solution.py:45
  68.4 25.8 %collective-permute-start.10 = (bf16[256,1536]{1,0:T(8,128)(2,1)}, bf16[256,1536]{1,0:T(8,128)(2,1)S(1)}, u32[]{:S(2)}, u32[]{:S(2)}) collective-permute-start(bf16[256,1536]{1,0:T(8,128)(2,1)} %bitcast.169), channel_id=1, source_target_pairs={{0,8},{1,9},{2,10},{3,11},{4,12},{5,13},{6,14},{7,15},{8,0},{9,1},... | collective-permute-start | bytes 2359304 | tf_op jit(solution)/shard_map/ppermute | solution.py:45
  69.0 20.0 %collective-permute-start.18 = (bf16[128,1536]{1,0:T(8,128)(2,1)S(1)}, bf16[128,1536]{1,0:T(8,128)(2,1)S(1)}, u32[]{:S(2)}, u32[]{:S(2)}) collective-permute-start(bf16[128,1536]{1,0:T(8,128)(2,1)S(1)} %collective-permute-done.16), channel_id=1, source_target_pairs={{0,1},{1,0},{2,3},{3,2},{4,5},{5,4},{6,7},{7,6},{8,9},{9,8},{10,11... | collective-permute-start | bytes 1179656 | tf_op jit(solution)/shard_map/ppermute | solution.py:45
  70.5 28.8 %collective-permute-start.11 = (bf16[256,1536]{1,0:T(8,128)(2,1)S(1)}, bf16[256,1536]{1,0:T(8,128)(2,1)S(1)}, u32[]{:S(2)}, u32[]{:S(2)}) collective-permute-start(bf16[256,1536]{1,0:T(8,128)(2,1)S(1)} %collective-permute-done.9), channel_id=1, source_target_pairs={{0,8},{1,9},{2,10},{3,11},{4,12},{5,13},{6,14},{7,15},{8,0},{9,1},... | collective-permute-start | bytes 2359304 | tf_op jit(solution)/shard_map/ppermute | solution.py:45
  80.6 29.7 %collective-permute-start.2 = (bf16[128,1536]{1,0:T(8,128)(2,1)}, bf16[128,1536]{1,0:T(8,128)(2,1)}, u32[]{:S(2)}, u32[]{:S(2)}) collective-permute-start(bf16[128,1536]{1,0:T(8,128)(2,1)} %collective-permute-done), channel_id=1, source_target_pairs={{0,1},{1,0},{2,3},{3,2},{4,5},{5,4},{6,7},{7,6},{8,9},{9,8},{10,11... | collective-permute-start | bytes 1179656 | tf_op jit(solution)/shard_map/ppermute | solution.py:45
  167.9 86.5 %collective-permute-start.39 = (bf16[512,1536]{1,0:T(8,128)(2,1)S(1)}, bf16[512,1536]{1,0:T(8,128)(2,1)S(1)}, u32[]{:S(2)}, u32[]{:S(2)}) collective-permute-start(bf16[512,1536]{1,0:T(8,128)(2,1)S(1)} %convolution_convert_fusion), channel_id=1, source_target_pairs={{0,8},{1,9},{2,10},{3,11},{4,12},{5,13},{6,14},{7,15},{8,0},{9,1},... | collective-permute-start | bytes 4718600 | tf_op jit(solution)/shard_map/ppermute | solution.py:45
  169.8 88.2 %collective-permute-start.37 = (bf16[512,1536]{1,0:T(8,128)(2,1)S(1)}, bf16[512,1536]{1,0:T(8,128)(2,1)S(1)}, u32[]{:S(2)}, u32[]{:S(2)}) collective-permute-start(bf16[512,1536]{1,0:T(8,128)(2,1)S(1)} %convolution_convert_fusion.1), channel_id=1, source_target_pairs={{0,8},{1,9},{2,10},{3,11},{4,12},{5,13},{6,14},{7,15},{8,0},{9,1},... | collective-permute-start | bytes 4718600 | tf_op jit(solution)/shard_map/ppermute | solution.py:45
  179.3 34.0 %collective-permute-start.33 = (bf16[128,1536]{1,0:T(8,128)(2,1)S(1)}, bf16[128,1536]{1,0:T(8,128)(2,1)S(1)}, u32[]{:S(2)}, u32[]{:S(2)}) collective-permute-start(bf16[128,1536]{1,0:T(8,128)(2,1)S(1)} %get-tuple-element.16), channel_id=1, source_target_pairs={{0,16},{1,17},{2,18},{3,19},{4,20},{5,21},{6,22},{7,23},{8,24},{9,... | collective-permute-start | bytes 1179656 | tf_op jit(solution)/shard_map/ppermute | solution.py:45
  185.7 46.7 %collective-permute-start.26 = (bf16[128,1536]{1,0:T(8,128)(2,1)S(1)}, bf16[128,1536]{1,0:T(8,128)(2,1)S(1)}, u32[]{:S(2)}, u32[]{:S(2)}) collective-permute-start(bf16[128,1536]{1,0:T(8,128)(2,1)S(1)} %get-tuple-element.14), channel_id=1, source_target_pairs={{0,16},{1,17},{2,18},{3,19},{4,20},{5,21},{6,22},{7,23},{8,24},{9,... | collective-permute-start | bytes 1179656 | tf_op jit(solution)/shard_map/ppermute | solution.py:45
  213.3 17.1 %collective-permute-start.19 = (bf16[128,1536]{1,0:T(8,128)(2,1)S(1)}, bf16[128,1536]{1,0:T(8,128)(2,1)S(1)}, u32[]{:S(2)}, u32[]{:S(2)}) collective-permute-start(bf16[128,1536]{1,0:T(8,128)(2,1)S(1)} %get-tuple-element.20), channel_id=1, source_target_pairs={{0,1},{1,0},{2,3},{3,2},{4,5},{5,4},{6,7},{7,6},{8,9},{9,8},{10,11... | collective-permute-start | bytes 1179656 | tf_op jit(solution)/shard_map/ppermute | solution.py:45
  232.2 21.2 %collective-permute-start.36 = (bf16[128,1536]{1,0:T(8,128)(2,1)S(1)}, bf16[128,1536]{1,0:T(8,128)(2,1)S(1)}, u32[]{:S(2)}, u32[]{:S(2)}) collective-permute-start(bf16[128,1536]{1,0:T(8,128)(2,1)S(1)} %add_convert_fusion.1), channel_id=1, source_target_pairs={{0,4},{1,5},{2,6},{3,7},{4,0},{5,1},{6,2},{7,3},{8,12},{9,13},{10,... | collective-permute-start | bytes 1179656 | tf_op jit(solution)/shard_map/ppermute | solution.py:45
  232.4 28.0 %collective-permute-start.12 = (bf16[128,1536]{1,0:T(8,128)(2,1)S(1)}, bf16[128,1536]{1,0:T(8,128)(2,1)S(1)}, u32[]{:S(2)}, u32[]{:S(2)}) collective-permute-start(bf16[128,1536]{1,0:T(8,128)(2,1)S(1)} %get-tuple-element.18), channel_id=1, source_target_pairs={{0,1},{1,0},{2,3},{3,2},{4,5},{5,4},{6,7},{7,6},{8,9},{9,8},{10,11... | collective-permute-start | bytes 1179656 | tf_op jit(solution)/shard_map/ppermute | solution.py:45
  241.3 19.1 %collective-permute-start.14 = (bf16[128,1536]{1,0:T(8,128)(2,1)S(1)}, bf16[128,1536]{1,0:T(8,128)(2,1)S(1)}, u32[]{:S(2)}, u32[]{:S(2)}) collective-permute-start(bf16[128,1536]{1,0:T(8,128)(2,1)S(1)} %fusion.60), channel_id=1, source_target_pairs={{0,16},{1,17},{2,18},{3,19},{4,20},{5,21},{6,22},{7,23},{8,24},{9,... | collective-permute-start | bytes 1179656 | tf_op jit(solution)/shard_map/ppermute | solution.py:45
  256.3 23.2 %collective-permute-start.40 = (bf16[256,1536]{1,0:T(8,128)(2,1)S(1)}, bf16[256,1536]{1,0:T(8,128)(2,1)S(1)}, u32[]{:S(2)}, u32[]{:S(2)}) collective-permute-start(bf16[256,1536]{1,0:T(8,128)(2,1)S(1)} %slice.238), channel_id=1, source_target_pairs={{0,2},{1,3},{2,0},{3,1},{4,6},{5,7},{6,4},{7,5},{8,10},{9,11},{10,... | collective-permute-start | bytes 2359304 | tf_op jit(solution)/shard_map/ppermute | solution.py:45
  260.0 28.0 %collective-permute-start.38 = (bf16[256,1536]{1,0:T(8,128)(2,1)S(1)}, bf16[256,1536]{1,0:T(8,128)(2,1)S(1)}, u32[]{:S(2)}, u32[]{:S(2)}) collective-permute-start(bf16[256,1536]{1,0:T(8,128)(2,1)S(1)} %slice.239), channel_id=1, source_target_pairs={{0,2},{1,3},{2,0},{3,1},{4,6},{5,7},{6,4},{7,5},{8,10},{9,11},{10,... | collective-permute-start | bytes 2359304 | tf_op jit(solution)/shard_map/ppermute | solution.py:45
  (57 other events, 769.2 us)

commit v2 on v1

v2 whole, which is shorter than its diff:
```python
import jax
import jax.numpy as jnp
from jax import lax
from jax.sharding import PartitionSpec as P

inv_sqrt_two = 0.7071067811865476
inv_sqrt_two_pi = 0.3989422804014327
AXES = ("exp", "fsdp")
CORES = 2
DEPTH = 4


def gelu_parts(values):
    cdf_part = 0.5 * (1.0 + jax.scipy.special.erf(values * inv_sqrt_two))
    return (
        values * cdf_part,
        cdf_part + values * jnp.exp(-0.5 * values * values) * inv_sqrt_two_pi,
    )


def contract_first(left, right):
    return lax.dot_general(
        left, right, (((0,), (0,)), ((), ())), preferred_element_type=jnp.float32
    )


def contract_last(left, right):
    return lax.dot_general(
        left, right, (((1,), (1,)), ((), ())), preferred_element_type=jnp.float32
    )


class Grid:
    def __init__(self, n_exp, n_fsdp):
        self.nx, self.ny = n_exp // CORES, n_fsdp // DEPTH

    def move(self, array, to):
        pairs = []
        for x in range(self.nx):
            for c in range(CORES):
                for z in range(DEPTH):
                    for y in range(self.ny):
                        tx, tc, tz, ty = to(x, c, z, y)
                        pairs.append((self.index(x, c, z, y), self.index(tx, tc, tz, ty)))
        return lax.ppermute(array, AXES, pairs)

    def index(self, x, c, z, y):
        return ((x * CORES + c) * DEPTH + z) * self.ny + y

    def from_x(self, array, step):
        return self.move(array, lambda x, c, z, y: ((x - step) % self.nx, c, z, y))

    def from_y(self, array, step):
        return self.move(array, lambda x, c, z, y: (x, c, z, (y - step) % self.ny))

    def to_x(self, array, step):
        return self.move(array, lambda x, c, z, y: ((x + step) % self.nx, c, z, y))

    def to_y(self, array, step):
        return self.move(array, lambda x, c, z, y: (x, c, z, (y + step) % self.ny))

    def swap_core(self, array):
        return self.move(array, lambda x, c, z, y: (x, 1 - c, z, y))

    def swap_far(self, array):
        return self.move(array, lambda x, c, z, y: (x, c, z ^ 2, y))

    def swap_near(self, array):
        return self.move(array, lambda x, c, z, y: (x, c, z ^ 1, y))


def wide(array):
    return array.astype(jnp.float32)


def total(parts):
    out = wide(parts[0])
    for part in parts[1:]:
        out = out + wide(part)
    return out


def tie(*groups):
    return lax.optimization_barrier(groups)


def shards(tokens, expert_ids, gates, w_in, w_out, grad_y):
    rows, features = tokens.shape
    n_exp, n_fsdp = lax.axis_size("exp"), lax.axis_size("fsdp")
    grid = Grid(n_exp, n_fsdp)
    nx, ny = grid.nx, grid.ny
    hidden = w_in.shape[1]
    bf = jnp.bfloat16
    own_expert = lax.axis_index("exp")

    far = jnp.concatenate([tokens, grad_y], axis=0)
    far, tokens, grad_y = tie(far, tokens, grad_y)
    far = grid.swap_far(far)
    own_weights = jnp.concatenate([w_in[0], w_out[0]], axis=0)
    near_weights = grid.swap_near(own_weights)

    ids_row = expert_ids.T[None, :, :]
    named = ids_row == jnp.arange(n_exp, dtype=jnp.int32)[:, None, None]
    gate_rows = jnp.sum(jnp.where(named, gates.T[None], 0.0), axis=1)

    def tok_first(tok):
        return [tok] + [grid.from_x(tok, s) for s in range(1, nx)]

    def grad_first(grad):
        return [grad] + [grid.from_y(grad, s) for s in range(1, ny)]

    def tok_second(line):
        line = jnp.concatenate(line, axis=0)
        return jnp.concatenate([line] + [grid.from_y(line, s) for s in range(1, ny)], axis=0)

    def grad_second(line):
        line = jnp.concatenate(line, axis=0)
        pieces = [line] + [grid.from_x(line, s) for s in range(1, nx)]
        return jnp.concatenate(
            [pieces[xo][yo * rows : (yo + 1) * rows] for yo in range(ny) for xo in range(nx)],
            axis=0,
        )

    gates_y = jnp.stack([gate_rows] + [grid.from_y(gate_rows, s) for s in range(1, ny)])
    tok_line, grad_line, gates_y = tie(tok_first(tokens), grad_first(grad_y), gates_y)
    gates_x = jnp.stack([gates_y] + [grid.from_x(gates_y, s) for s in range(1, nx)], axis=1)
    near_half = (tok_second(tok_line), grad_second(grad_line))
    far, gates_x = tie(far, gates_x)
    far_tok, far_grad = tok_first(far[:rows]), grad_first(far[rows:])
    near_half, gates_x, own_weights = tie(near_half, gates_x, own_weights)
    gates_z = jnp.stack([gates_x, grid.swap_far(gates_x)], axis=2)
    other_own = grid.swap_core(own_weights)
    far_tok, far_grad, other_own = tie(far_tok, far_grad, other_own)
    far_half = (tok_second(far_tok), grad_second(far_grad))
    halves = (near_half, far_half)

    other_near, gates_z = tie(grid.swap_core(near_weights), gates_z)
    four = (own_weights, near_weights, other_own, other_near)
    all_in = jnp.concatenate([part[:hidden] for part in four], axis=0)
    all_out = jnp.concatenate([part[hidden:] for part in four], axis=0)
    expert_pair = jnp.stack([own_expert, own_expert ^ 1])
    span = 2 * hidden
    pair_gates = jnp.take(gates_z, expert_pair, axis=3)

    def mixed_first(array):
        line = array.reshape(ny, nx * rows, features)
        return [line[0]] + [grid.to_y(line[s], s) for s in range(1, ny)]

    def mixed_second(line):
        line = total(line).astype(bf).reshape(nx, rows, features)
        return [line[0]] + [grid.to_x(line[s], s) for s in range(1, nx)]

    def input_first(array):
        part = array.reshape(ny, nx, rows, features)
        line = [part[:, s].reshape(ny * rows, features) for s in range(nx)]
        return [line[0]] + [grid.to_x(line[s], s) for s in range(1, nx)]

    def input_second(line):
        line = total(line).astype(bf).reshape(ny, rows, features)
        return [line[0]] + [grid.to_y(line[s], s) for s in range(1, ny)]

    mixed_parts, input_parts, acts, hiddens, products = [], [], [], [], []
    for half in range(2):
        tok, grad = halves[half]
        if half == 1:
            near_mixed, near_input = mixed_first(mixed_parts[0]), input_first(input_parts[0])
        scale = [pair_gates[:, :, half, e].reshape(-1, 1) for e in range(2)]
        pre = contract_last(tok, all_in)
        act, slope = gelu_parts(pre)
        back = contract_last(grad, all_out)
        column = lax.broadcasted_iota(jnp.int32, (1, 2 * span), 1)
        factor = jnp.where(column < span, scale[0], scale[1])
        act_scaled = (act * factor).astype(bf)
        grad_hidden = (back * slope * factor).astype(bf)
        products.append(act * back)
        acts.append(act_scaled)
        hiddens.append(grad_hidden)
        mixed_parts.append(jnp.dot(act_scaled, all_out, preferred_element_type=jnp.float32).astype(bf))
        input_parts.append(jnp.dot(grad_hidden, all_in, preferred_element_type=jnp.float32).astype(bf))

    far_mixed, far_input = mixed_first(mixed_parts[1]), input_first(input_parts[1])

    both_tokens = jnp.concatenate([half[0] for half in halves], axis=0)
    both_grads = jnp.concatenate([half[1] for half in halves], axis=0)
    both_acts = jnp.concatenate(acts, axis=0)
    both_hiddens = jnp.concatenate(hiddens, axis=0)
    other = jnp.concatenate(
        [
            contract_first(both_hiddens[:, span:], both_tokens).astype(bf),
            contract_first(both_acts[:, span:], both_grads).astype(bf),
        ],
        axis=0,
    )
    other = grid.swap_core(other)
    other = wide(other)
    sum_in = contract_first(both_hiddens[:, :span], both_tokens) + other[:span]
    sum_out = contract_first(both_acts[:, :span], both_grads) + other[span:]

    near_sums = jnp.concatenate([sum_in[hidden:], sum_out[hidden:]], axis=0).astype(bf)
    far_mixed, far_input, near_mixed, near_input, near_sums = tie(
        far_mixed, far_input, near_mixed, near_input, near_sums
    )
    far_mixed, far_input = mixed_second(far_mixed), input_second(far_input)
    near_mixed, near_input = mixed_second(near_mixed), input_second(near_input)
    near_sums = wide(grid.swap_near(near_sums))

    scores = jnp.stack(
        [
            jnp.sum(p[:, e * span : (e + 1) * span], axis=1).reshape(ny, nx, rows)
            for p in products
            for e in range(2)
        ],
        axis=2,
    ).reshape(ny, nx, 2, 2, rows)
    experts = jnp.arange(n_exp, dtype=jnp.int32)[:, None]
    scores = sum(
        jnp.where(experts == expert_pair[e], scores[:, :, :, e][:, :, :, None, :], 0.0)
        for e in range(2)
    )
    scores = scores[:, :, 0] + grid.swap_far(scores[:, :, 1])
    scores = total([scores[0]] + [grid.to_y(scores[s], s) for s in range(1, ny)])
    scores = total([scores[0]] + [grid.to_x(scores[s], s) for s in range(1, nx)])
    grad_gates = jnp.sum(jnp.where(named, scores[:, None, :], 0.0), axis=0).T

    far_sums = jnp.concatenate([total(far_mixed), total(far_input)], axis=0).astype(bf)
    far_sums = wide(grid.swap_far(far_sums))
    mixed = (total(near_mixed) + far_sums[:rows]).astype(bf)
    grad_tokens = (total(near_input) + far_sums[rows:]).astype(bf)
    grad_in = sum_in[:hidden] + near_sums[:hidden]
    grad_out = sum_out[:hidden] + near_sums[hidden:]
    return (mixed, grad_tokens, grad_in[None], grad_out[None], grad_gates)


def solution(mesh):
    rows = P(AXES, None)
    weights = P("exp", "fsdp", None)
    return jax.shard_map(
        shards,
        mesh=mesh,
        in_specs=(rows, rows, rows, weights, weights, rows),
        out_specs=(rows, rows, weights, weights, rows),
        check_vma=False,
    )
```

time: 291 us -> 192 us (0.66)
  waiting for transfers between devices: 157 us -> 96.9 us
  local copies, waits for them, and re-layouts: 36.7 us -> 17.4 us
  starting transfers between devices: 43.7 us -> 29.4 us
  matrix products: 35.4 us -> 28.5 us
    ppermute x44 -> x29, waiting for transfers between devices: 157 us -> 96.9 us  [move(): return lax.ppermute(array, AXES, pairs)]
    unnamed x91 -> x56, local copies, waits for them, and re-layouts: 21.3 us -> 4.36 us
    ppermute x44 -> x29, starting transfers between devices: 43.7 us -> 29.4 us  [move(): return lax.ppermute(array, AXES, pairs)]
    slice x3 -> x18, local copies, waits for them, and re-layouts: 0.17 us -> 9.34 us  [the longest x4 8.53 us: shards(): all_out = jnp.concatenate([part[hidden:] for part in four], axis=0)]
    reshape x4 -> x0, local copies, waits for them, and re-layouts: 8.3 us -> none  [the longest x2 8.01 us: shards(): score = jnp.sum((act * back).reshape(-1, 2, 2 * hidden), axis=-1)]
    concatenate x0 -> x11, other arithmetic: none -> 6.48 us  [the longest x1 2.61 us: shards(): own_weights = jnp.concatenate([w_in[0], w_out[0]], axis=0)]
    dot_general x4, matrix products: 17.5 us -> 12.5 us  [contract_last(): lax.dot_general(left, right, (((1,), (1,)), ((), ())), preferred_element_...]
    reduce_sum x3 -> x4, other arithmetic: 5.77 us -> 1.78 us  [the longest x1 0.76 us: shards(): gate_rows = jnp.sum(jnp.where(named, gates.T[None], 0.0), axis=1)]
  transfers between devices with their start and end apart: 44 -> 29, of which waited for: 25 -> 11; matrix products, arithmetic and copies ran while one was open for 18% -> 30% of each run, Pallas kernels for 0% -> 0%
where the time goes in v2:
time: 192 us; the launch traced here: 191 us
  waiting for transfers between devices  96.9 us (50%)
  starting transfers between devices  29.4 us (15%)
  matrix products  28.5 us (15%)
  local copies, waits for them, and re-layouts  17.4 us (9%)
  other arithmetic  17.4 us (9%)
    ppermute x29, waiting for transfers between devices, move(): return lax.ppermute(array, AXES, pairs)  96.9 us
    ppermute x29, starting transfers between devices, move(): return lax.ppermute(array, AXES, pairs)  29.4 us
    dot_general x4, matrix products, contract_last(): lax.dot_general(left, right, (((1,), (1,)), ((), ())), preferred_element_...  12.5 us
    slice x4, local copies, waits for them, and re-layouts, shards(): all_out = jnp.concatenate([part[hidden:] for part in four], axis=0)  8.53 us
    dot_general x4, matrix products, contract_first(): lax.dot_general(left, right, (((0,), (0,)), ((), ())), preferred_element_...  7.57 us
    unnamed x56, local copies, waits for them, and re-layouts  4.36 us
    dot_general x2, matrix products, shards(): jnp.dot(act_scaled, all_out, preferred_element_type=jnp.float32).astype(bf)  4.22 us
    dot_general x2, matrix products, shards(): jnp.dot(grad_hidden, all_in, preferred_element_type=jnp.float32).astype(bf)  4.19 us
  transfers between devices with their start and end apart: 29, of which 11 were waited for; matrix products, arithmetic and copies ran while one was open for 30% of the time, Pallas kernels for 0%

profile of v2, /device:TPU:0, one launch (start us, length us, event | category | flops | bytes accessed | tf_op | source)
XLA Modules:
  0.0 191.1 jit_solution(10468330751337649632)
XLA Ops:
  1.4 3.0 %collective-permute-start.3 = (f32[4,128]{1,0:T(4,128)S(1)}, f32[4,128]{1,0:T(4,128)S(1)}, u32[]{:S(2)}, u32[]{:S(2)}) collective-permute-start(f32[4,128]{1,0:T(4,128)S(1)} %select_reduce_fusion.1), channel_id=1, source_target_pairs={{0,1},{1,0},{2,3},{3,2},{4,5},{5,4},{6,7},{7,6},{8,9},{9,8},{10,11... | collective-permute-start | bytes 6152 | tf_op jit(solution)/shard_map/ppermute | solution.py:45
  7.7 2.6 %collective-permute-start = (bf16[256,1536]{1,0:T(8,128)(2,1)S(1)}, bf16[256,1536]{1,0:T(8,128)(2,1)S(1)}, u32[]{:S(2)}, u32[]{:S(2)}) collective-permute-start(bf16[256,1536]{1,0:T(8,128)(2,1)S(1)} %pad_maximum_fusion.11), channel_id=1, source_target_pairs={{0,4},{1,5},{2,6},{3,7},{4,0},{5,1},{6,2},{7,3},{8,12},{9,13},{10,... | collective-permute-start | bytes 2359304 | tf_op jit(solution)/shard_map/ppermute | solution.py:45
  10.2 2.6 %pad_maximum_fusion.5 = bf16[512,1536]{1,0:T(8,128)(2,1)} fusion(bf16[256,1536]{1,0:T(8,128)(2,1)} %bitcast.84, bf16[256,1536]{1,0:T(8,128)(2,1)} %bitcast.85), kind=kLoop, calls=%fused_computation.46 | loop fusion | flops 3145728 | bytes 3145728 | tf_op jit(solution)/shard_map/concatenate | solution.py:99
  20.8 14.9 %collective-permute-done.4 = f32[2,4,128]{2,1,0:T(4,128)S(1)} collective-permute-done((f32[2,4,128]{2,1,0:T(4,128)S(1)}, f32[2,4,128]{2,1,0:T(4,128)S(1)}, u32[]{:S(2)}, u32[]{:S(2)}) %collective-permute-start.4) | collective-permute-done | bytes 4128 | tf_op jit(solution)/shard_map/ppermute | solution.py:45
  35.7 8.3 %collective-permute-done = bf16[256,1536]{1,0:T(8,128)(2,1)S(1)} collective-permute-done((bf16[256,1536]{1,0:T(8,128)(2,1)S(1)}, bf16[256,1536]{1,0:T(8,128)(2,1)S(1)}, u32[]{:S(2)}, u32[]{:S(2)}) %collective-permute-start) | collective-permute-done | bytes 786464 | tf_op jit(solution)/shard_map/ppermute | solution.py:45
  46.7 3.3 %fusion.54 = (bf16[256,1536]{1,0:T(8,128)(2,1)}, bf16[256,1536]{1,0:T(8,128)(2,1)}) fusion(bf16[512,1536]{1,0:T(8,128)(2,1)} %pad_maximum_fusion.5), kind=kLoop, calls=%fused_computation.137 | loop fusion | bytes 3145728 | tf_op jit(solution)/shard_map/slice | solution.py:140
  50.2 10.0 %collective-permute-done.13 = f32[2,2,4,128]{3,2,1,0:T(4,128)S(1)} collective-permute-done((f32[2,2,4,128]{3,2,1,0:T(4,128)S(1)}, f32[2,2,4,128]{3,2,1,0:T(4,128)S(1)}, u32[]{:S(2)}, u32[]{:S(2)}) %collective-permute-start.13) | collective-permute-done | bytes 8224 | tf_op jit(solution)/shard_map/ppermute | solution.py:45
  60.2 3.9 %collective-permute-done.11 = bf16[512,1536]{1,0:T(8,128)(2,1)} collective-permute-done((bf16[512,1536]{1,0:T(8,128)(2,1)}, bf16[512,1536]{1,0:T(8,128)(2,1)}, u32[]{:S(2)}, u32[]{:S(2)}) %collective-permute-start.11) | collective-permute-done | bytes 1572896 | tf_op jit(solution)/shard_map/ppermute | solution.py:45
  64.1 2.6 %fusion.55 = (bf16[256,1536]{1,0:T(8,128)(2,1)}, bf16[256,1536]{1,0:T(8,128)(2,1)}) fusion(bf16[512,1536]{1,0:T(8,128)(2,1)} %collective-permute-done.11), kind=kLoop, calls=%fused_computation.138 | loop fusion | bytes 3145728 | tf_op jit(solution)/shard_map/slice | solution.py:140
  77.3 4.3 %fusion.49 = f32[512,1024]{1,0:T(8,128)S(1)} fusion(bf16[512,1536]{1,0:T(8,128)(2,1)} %copy-done.4, bf16[256,1536]{1,0:T(8,128)(2,1)} %get-tuple-element.94, bf16[256,1536]{1,0:T(8,128)(2,1)} %get-tuple-element.92, bf16[256,1536]{1,0:T(8,128)(2,1)} %get-tuple-element.90, bf16[256,1536]{1,0:T(8,128)(2,1)} %get-tuple-element.88), kind=kOutput, calls=%fused_computation.132 | convolution fusion | flops 1623195648 | bytes 6815744 | tf_op jit(solution)/shard_map/dot_general | solution.py:28
  81.7 2.6 %multiply_multiply_fusion.2 = (f32[512,1024]{1,0:T(8,128)S(1)}, bf16[512,1024]{1,0:T(8,128)(2,1)S(1)}, bf16[512,1024]{1,0:T(8,128)(2,1)S(1)}) fusion(f32[512,1024]{1,0:T(8,128)S(1)} %fusion.49, f32[512]{0:T(512)S(1)} %bitcast.106, f32[512]{0:T(512)S(1)} %bitcast.105, pred[1024]{0:T(1024)(128)(4,1)S(1)} %copy-done.24, bf16[512,1536]{1,0:T(8,128)(2,1)S(1)} %copy-done.3, ...), kind=kOutput, calls=%fused_computation.76 | convolution fusion | flops 1631584256 | bytes 11015168 | tf_op jit(solution)/shard_map/dot_general | solution.py:28
  84.3 2.2 %convolution_convert_fusion.2 = bf16[512,1536]{1,0:T(8,128)(2,1)S(1)} fusion(bf16[512,1024]{1,0:T(8,128)(2,1)S(1)} %get-tuple-element.70, bf16[256,1536]{1,0:T(8,128)(2,1)S(1)} %copy-done.20, bf16[256,1536]{1,0:T(8,128)(2,1)S(1)} %copy-done.18, bf16[256,1536]{1,0:T(8,128)(2,1)S(1)} %copy-done.16, bf16[256,1536]{1,0:T(8,128)(2,1)S(1)} %copy-done.14), kind=kOutput, calls=%fused_computation.14 | convolution fusion | flops 1623982080 | bytes 5767168 | tf_op jit(solution)/shard_map/dot_general | solution.py:179
  88.2 2.0 %convolution_convert_fusion.3 = bf16[512,1536]{1,0:T(8,128)(2,1)S(1)} fusion(bf16[512,1024]{1,0:T(8,128)(2,1)S(1)} %get-tuple-element.76, bf16[256,1536]{1,0:T(8,128)(2,1)S(1)} %copy-done.19, bf16[256,1536]{1,0:T(8,128)(2,1)S(1)} %copy-done.17, bf16[256,1536]{1,0:T(8,128)(2,1)S(1)} %copy-done.15, bf16[256,1536]{1,0:T(8,128)(2,1)S(1)} %copy-done.13), kind=kOutput, calls=%fused_computation.15 | convolution fusion | flops 1623982080 | bytes 5767168 | tf_op jit(solution)/shard_map/dot_general | solution.py:178
  94.4 3.0 %fusion.16 = f32[512,1024]{1,0:T(8,128)S(1)} fusion(bf16[256,1536]{1,0:T(8,128)(2,1)} %collective-permute-done.10, bf16[128,1536]{1,0:T(8,128)(2,1)S(1)} %copy-done.12, bf16[128,1536]{1,0:T(8,128)(2,1)S(1)} %get-tuple-element.46, bf16[256,1536]{1,0:T(8,128)(2,1)S(1)} %copy-done.20, bf16[256,1536]{1,0:T(8,128)(2,1)S(1)} %copy-done.18, ...), kind=kOutput, calls=%fused_computation.47 | convolution fusion | flops 1627914240 | bytes 6815744 | tf_op jit(solution)/shard_map/dot_general | solution.py:28
  97.4 2.6 %multiply_multiply_fusion.3 = (f32[512,1024]{1,0:T(8,128)S(1)}, bf16[512,1024]{1,0:T(8,128)(2,1)S(1)}, bf16[512,1024]{1,0:T(8,128)(2,1)S(1)}) fusion(f32[512,1024]{1,0:T(8,128)S(1)} %fusion.16, f32[512]{0:T(512)S(1)} %bitcast.103, f32[512]{0:T(512)S(1)} %bitcast.104, pred[1024]{0:T(1024)(128)(4,1)S(1)} %copy-done.24, bf16[256,1536]{1,0:T(8,128)(2,1)S(1)} %copy-done.19, ...), kind=kOutput, calls=%fused_computation.77 | convolution fusion | flops 1637875712 | bytes 11015168 | tf_op jit(solution)/shard_map/dot_general | solution.py:28
  106.5 2.0 %convolution_convert_fusion.4 = bf16[512,1536]{1,0:T(8,128)(2,1)S(1)} fusion(bf16[512,1024]{1,0:T(8,128)(2,1)S(1)} %get-tuple-element.72, bf16[256,1536]{1,0:T(8,128)(2,1)S(1)} %copy-done.20, bf16[256,1536]{1,0:T(8,128)(2,1)S(1)} %copy-done.18, bf16[256,1536]{1,0:T(8,128)(2,1)S(1)} %copy-done.16, bf16[256,1536]{1,0:T(8,128)(2,1)S(1)} %copy-done.14), kind=kOutput, calls=%fused_computation.16 | convolution fusion | flops 1623982080 | bytes 5767168 | tf_op jit(solution)/shard_map/dot_general | solution.py:179
  108.5 2.2 %convolution_convert_fusion.5 = bf16[512,1536]{1,0:T(8,128)(2,1)S(1)} fusion(bf16[512,1024]{1,0:T(8,128)(2,1)S(1)} %get-tuple-element.75, bf16[256,1536]{1,0:T(8,128)(2,1)S(1)} %copy-done.19, bf16[256,1536]{1,0:T(8,128)(2,1)S(1)} %copy-done.17, bf16[256,1536]{1,0:T(8,128)(2,1)S(1)} %copy-done.15, bf16[256,1536]{1,0:T(8,128)(2,1)S(1)} %copy-done.13), kind=kOutput, calls=%fused_computation.17 | convolution fusion | flops 1623982080 | bytes 5767168 | tf_op jit(solution)/shard_map/dot_general | solution.py:178
  112.2 2.9 %collective-permute-done.27 = f32[2,4,128]{2,1,0:T(4,128)S(1)} collective-permute-done((f32[2,4,128]{2,1,0:T(4,128)S(1)}, f32[2,4,128]{2,1,0:T(4,128)S(1)}, u32[]{:S(2)}, u32[]{:S(2)}) %collective-permute-start.27) | collective-permute-done | bytes 4128 | tf_op jit(solution)/shard_map/ppermute | solution.py:45
  120.8 9.4 %collective-permute-done.16 = bf16[256,1536]{1,0:T(8,128)(2,1)S(1)} collective-permute-done((bf16[256,1536]{1,0:T(8,128)(2,1)S(1)}, bf16[256,1536]{1,0:T(8,128)(2,1)S(1)}, u32[]{:S(2)}, u32[]{:S(2)}) %collective-permute-start.16) | collective-permute-done | bytes 786464 | tf_op jit(solution)/shard_map/ppermute | solution.py:45
  130.2 2.8 %collective-permute-done.14 = bf16[256,1536]{1,0:T(8,128)(2,1)S(1)} collective-permute-done((bf16[256,1536]{1,0:T(8,128)(2,1)S(1)}, bf16[256,1536]{1,0:T(8,128)(2,1)S(1)}, u32[]{:S(2)}, u32[]{:S(2)}) %collective-permute-start.14) | collective-permute-done | bytes 786464 | tf_op jit(solution)/shard_map/ppermute | solution.py:45
  133.0 2.5 %collective-permute-start.25 = (bf16[512,1536]{1,0:T(8,128)(2,1)S(1)}, bf16[512,1536]{1,0:T(8,128)(2,1)S(1)}, u32[]{:S(2)}, u32[]{:S(2)}) collective-permute-start(bf16[512,1536]{1,0:T(8,128)(2,1)S(1)} %pad_maximum_fusion.6), channel_id=1, source_target_pairs={{0,2},{1,3},{2,0},{3,1},{4,6},{5,7},{6,4},{7,5},{8,10},{9,11},{10,... | collective-permute-start | bytes 4718600 | tf_op jit(solution)/shard_map/ppermute | solution.py:45
  139.0 13.8 %collective-permute-done.21 = bf16[128,1536]{1,0:T(8,128)(2,1)S(1)} collective-permute-done((bf16[128,1536]{1,0:T(8,128)(2,1)S(1)}, bf16[128,1536]{1,0:T(8,128)(2,1)S(1)}, u32[]{:S(2)}, u32[]{:S(2)}) %collective-permute-start.21) | collective-permute-done | bytes 393248 | tf_op jit(solution)/shard_map/ppermute | solution.py:45
  158.8 28.2 %collective-permute-done.23 = bf16[256,1536]{1,0:T(8,128)(2,1)S(1)} collective-permute-done((bf16[256,1536]{1,0:T(8,128)(2,1)S(1)}, bf16[256,1536]{1,0:T(8,128)(2,1)S(1)}, u32[]{:S(2)}, u32[]{:S(2)}) %collective-permute-start.23) | collective-permute-done | bytes 786464 | tf_op jit(solution)/shard_map/ppermute | solution.py:45
  188.8 2.2 %fusion.14 = (f32[1,256,1536]{2,1,0:T(8,128)}, f32[1,256,1536]{2,1,0:T(8,128)}) fusion(f32[512,1536]{1,0:T(8,128)S(1)} %convert_element_type.141, f32[512,1536]{1,0:T(8,128)S(1)} %convolution_add_fusion, f32[512,1536]{1,0:T(8,128)S(1)} %convolution_add_fusion.1), kind=kLoop, calls=%fused_computation.39 | loop fusion | flops 786432 | bytes 9437184 | tf_op jit(solution)/shard_map/broadcast_in_dim | solution.py:231
  (168 shorter events, 55.5 us)
Async XLA Ops:
  1.4 15.5 %collective-permute-start.3 = (f32[4,128]{1,0:T(4,128)S(1)}, f32[4,128]{1,0:T(4,128)S(1)}, u32[]{:S(2)}, u32[]{:S(2)}) collective-permute-start(f32[4,128]{1,0:T(4,128)S(1)} %select_reduce_fusion.1), channel_id=1, source_target_pairs={{0,1},{1,0},{2,3},{3,2},{4,5},{5,4},{6,7},{7,6},{8,9},{9,8},{10,11... | collective-permute-start | bytes 6152 | tf_op jit(solution)/shard_map/ppermute | solution.py:45
  5.6 11.4 %collective-permute-start.1 = (bf16[128,1536]{1,0:T(8,128)(2,1)}, bf16[128,1536]{1,0:T(8,128)(2,1)S(1)}, u32[]{:S(2)}, u32[]{:S(2)}) collective-permute-start(bf16[128,1536]{1,0:T(8,128)(2,1)} %param.6), channel_id=1, source_target_pairs={{0,16},{1,17},{2,18},{3,19},{4,20},{5,21},{6,22},{7,23},{8,24},{9,... | collective-permute-start | bytes 1179656 | tf_op jit(solution)/shard_map/ppermute | solution.py:45
  7.2 10.5 %collective-permute-start.2 = (bf16[128,1536]{1,0:T(8,128)(2,1)}, bf16[128,1536]{1,0:T(8,128)(2,1)S(1)}, u32[]{:S(2)}, u32[]{:S(2)}) collective-permute-start(bf16[128,1536]{1,0:T(8,128)(2,1)} %param.11), channel_id=1, source_target_pairs={{0,1},{1,0},{2,3},{3,2},{4,5},{5,4},{6,7},{7,6},{8,9},{9,8},{10,11... | collective-permute-start | bytes 1179656 | tf_op jit(solution)/shard_map/ppermute | solution.py:45
  7.7 36.3 %collective-permute-start = (bf16[256,1536]{1,0:T(8,128)(2,1)S(1)}, bf16[256,1536]{1,0:T(8,128)(2,1)S(1)}, u32[]{:S(2)}, u32[]{:S(2)}) collective-permute-start(bf16[256,1536]{1,0:T(8,128)(2,1)S(1)} %pad_maximum_fusion.11), channel_id=1, source_target_pairs={{0,4},{1,5},{2,6},{3,7},{4,0},{5,1},{6,2},{7,3},{8,12},{9,13},{10,... | collective-permute-start | bytes 2359304 | tf_op jit(solution)/shard_map/ppermute | solution.py:45
  12.9 51.2 %collective-permute-start.11 = (bf16[512,1536]{1,0:T(8,128)(2,1)}, bf16[512,1536]{1,0:T(8,128)(2,1)}, u32[]{:S(2)}, u32[]{:S(2)}) collective-permute-start(bf16[512,1536]{1,0:T(8,128)(2,1)} %pad_maximum_fusion.5), channel_id=1, source_target_pairs={{0,2},{1,3},{2,0},{3,1},{4,6},{5,7},{6,4},{7,5},{8,10},{9,11},{10,... | collective-permute-start | bytes 4718600 | tf_op jit(solution)/shard_map/ppermute | solution.py:45
  17.7 28.4 %collective-permute-start.8 = (bf16[256,1536]{1,0:T(8,128)(2,1)S(1)}, bf16[256,1536]{1,0:T(8,128)(2,1)S(1)}, u32[]{:S(2)}, u32[]{:S(2)}) collective-permute-start(bf16[256,1536]{1,0:T(8,128)(2,1)S(1)} %pad_maximum_fusion.13), channel_id=1, source_target_pairs={{0,16},{1,17},{2,18},{3,19},{4,20},{5,21},{6,22},{7,23},{8,24},{9,... | collective-permute-start | bytes 2359304 | tf_op jit(solution)/shard_map/ppermute | solution.py:45
  18.3 17.3 %collective-permute-start.4 = (f32[2,4,128]{2,1,0:T(4,128)S(1)}, f32[2,4,128]{2,1,0:T(4,128)S(1)}, u32[]{:S(2)}, u32[]{:S(2)}) collective-permute-start(f32[2,4,128]{2,1,0:T(4,128)S(1)} %pad_maximum_fusion.20), channel_id=1, source_target_pairs={{0,16},{1,17},{2,18},{3,19},{4,20},{5,21},{6,22},{7,23},{8,24},{9,... | collective-permute-start | bytes 12296 | tf_op jit(solution)/shard_map/ppermute | solution.py:45
  19.9 26.5 %collective-permute-start.7 = (bf16[256,1536]{1,0:T(8,128)(2,1)S(1)}, bf16[256,1536]{1,0:T(8,128)(2,1)S(1)}, u32[]{:S(2)}, u32[]{:S(2)}) collective-permute-start(bf16[256,1536]{1,0:T(8,128)(2,1)S(1)} %pad_maximum_fusion.12), channel_id=1, source_target_pairs={{0,1},{1,0},{2,3},{3,2},{4,5},{5,4},{6,7},{7,6},{8,9},{9,8},{10,11... | collective-permute-start | bytes 2359304 | tf_op jit(solution)/shard_map/ppermute | solution.py:45
  44.0 22.7 %collective-permute-start.5 = (bf16[128,1536]{1,0:T(8,128)(2,1)S(1)}, bf16[128,1536]{1,0:T(8,128)(2,1)S(1)}, u32[]{:S(2)}, u32[]{:S(2)}) collective-permute-start(bf16[128,1536]{1,0:T(8,128)(2,1)S(1)} %get-tuple-element.46), channel_id=1, source_target_pairs={{0,16},{1,17},{2,18},{3,19},{4,20},{5,21},{6,22},{7,23},{8,24},{9,... | collective-permute-start | bytes 1179656 | tf_op jit(solution)/shard_map/ppermute | solution.py:45
  44.6 22.2 %collective-permute-start.6 = (bf16[128,1536]{1,0:T(8,128)(2,1)S(1)}, bf16[128,1536]{1,0:T(8,128)(2,1)S(1)}, u32[]{:S(2)}, u32[]{:S(2)}) collective-permute-start(bf16[128,1536]{1,0:T(8,128)(2,1)S(1)} %get-tuple-element.52), channel_id=1, source_target_pairs={{0,1},{1,0},{2,3},{3,2},{4,5},{5,4},{6,7},{7,6},{8,9},{9,8},{10,11... | collective-permute-start | bytes 1179656 | tf_op jit(solution)/shard_map/ppermute | solution.py:45
  46.5 13.7 %collective-permute-start.13 = (f32[2,2,4,128]{3,2,1,0:T(4,128)S(1)}, f32[2,2,4,128]{3,2,1,0:T(4,128)S(1)}, u32[]{:S(2)}, u32[]{:S(2)}) collective-permute-start(f32[2,2,4,128]{3,2,1,0:T(4,128)S(1)} %pad_maximum_fusion.18), channel_id=1, source_target_pairs={{0,4},{1,5},{2,6},{3,7},{4,0},{5,1},{6,2},{7,3},{8,12},{9,13},{10,... | collective-permute-start | bytes 24584 | tf_op jit(solution)/shard_map/ppermute | solution.py:45
  46.5 20.2 %collective-permute-start.9 = (bf16[512,1536]{1,0:T(8,128)(2,1)}, bf16[512,1536]{1,0:T(8,128)(2,1)S(1)}, u32[]{:S(2)}, u32[]{:S(2)}) collective-permute-start(bf16[512,1536]{1,0:T(8,128)(2,1)} %pad_maximum_fusion.5), channel_id=1, source_target_pairs={{0,8},{1,9},{2,10},{3,11},{4,12},{5,13},{6,14},{7,15},{8,0},{9,1},... | collective-permute-start | bytes 4718600 | tf_op jit(solution)/shard_map/ppermute | solution.py:45
  67.9 23.3 %collective-permute-start.15 = (bf16[256,1536]{1,0:T(8,128)(2,1)}, bf16[256,1536]{1,0:T(8,128)(2,1)}, u32[]{:S(2)}, u32[]{:S(2)}) collective-permute-start(bf16[256,1536]{1,0:T(8,128)(2,1)} %pad_maximum_fusion.15), channel_id=1, source_target_pairs={{0,16},{1,17},{2,18},{3,19},{4,20},{5,21},{6,22},{7,23},{8,24},{9,... | collective-permute-start | bytes 2359304 | tf_op jit(solution)/shard_map/ppermute | solution.py:45
  69.3 25.1 %collective-permute-start.10 = (bf16[256,1536]{1,0:T(8,128)(2,1)}, bf16[256,1536]{1,0:T(8,128)(2,1)}, u32[]{:S(2)}, u32[]{:S(2)}) collective-permute-start(bf16[256,1536]{1,0:T(8,128)(2,1)} %pad_maximum_fusion.14), channel_id=1, source_target_pairs={{0,1},{1,0},{2,3},{3,2},{4,5},{5,4},{6,7},{7,6},{8,9},{9,8},{10,11... | collective-permute-start | bytes 2359304 | tf_op jit(solution)/shard_map/ppermute | solution.py:45
  86.6 34.1 %collective-permute-start.18 = (bf16[256,1536]{1,0:T(8,128)(2,1)S(1)}, bf16[256,1536]{1,0:T(8,128)(2,1)S(1)}, u32[]{:S(2)}, u32[]{:S(2)}) collective-permute-start(bf16[256,1536]{1,0:T(8,128)(2,1)S(1)} %bitcast.86), channel_id=1, source_target_pairs={{0,16},{1,17},{2,18},{3,19},{4,20},{5,21},{6,22},{7,23},{8,24},{9,... | collective-permute-start | bytes 2359304 | tf_op jit(solution)/shard_map/ppermute | solution.py:45
  90.3 30.4 %collective-permute-start.17 = (bf16[256,1536]{1,0:T(8,128)(2,1)S(1)}, bf16[256,1536]{1,0:T(8,128)(2,1)S(1)}, u32[]{:S(2)}, u32[]{:S(2)}) collective-permute-start(bf16[256,1536]{1,0:T(8,128)(2,1)S(1)} %get-tuple-element.81), channel_id=1, source_target_pairs={{0,1},{1,0},{2,3},{3,2},{4,5},{5,4},{6,7},{7,6},{8,9},{9,8},{10,11... | collective-permute-start | bytes 2359304 | tf_op jit(solution)/shard_map/ppermute | solution.py:45
  110.9 19.4 %collective-permute-start.16 = (bf16[256,1536]{1,0:T(8,128)(2,1)S(1)}, bf16[256,1536]{1,0:T(8,128)(2,1)S(1)}, u32[]{:S(2)}, u32[]{:S(2)}) collective-permute-start(bf16[256,1536]{1,0:T(8,128)(2,1)S(1)} %bitcast.87), channel_id=1, source_target_pairs={{0,16},{1,17},{2,18},{3,19},{4,20},{5,21},{6,22},{7,23},{8,24},{9,... | collective-permute-start | bytes 2359304 | tf_op jit(solution)/shard_map/ppermute | solution.py:45
  115.2 17.9 %collective-permute-start.14 = (bf16[256,1536]{1,0:T(8,128)(2,1)S(1)}, bf16[256,1536]{1,0:T(8,128)(2,1)S(1)}, u32[]{:S(2)}, u32[]{:S(2)}) collective-permute-start(bf16[256,1536]{1,0:T(8,128)(2,1)S(1)} %get-tuple-element.85), channel_id=1, source_target_pairs={{0,1},{1,0},{2,3},{3,2},{4,5},{5,4},{6,7},{7,6},{8,9},{9,8},{10,11... | collective-permute-start | bytes 2359304 | tf_op jit(solution)/shard_map/ppermute | solution.py:45
  133.0 55.4 %collective-permute-start.25 = (bf16[512,1536]{1,0:T(8,128)(2,1)S(1)}, bf16[512,1536]{1,0:T(8,128)(2,1)S(1)}, u32[]{:S(2)}, u32[]{:S(2)}) collective-permute-start(bf16[512,1536]{1,0:T(8,128)(2,1)S(1)} %pad_maximum_fusion.6), channel_id=1, source_target_pairs={{0,2},{1,3},{2,0},{3,1},{4,6},{5,7},{6,4},{7,5},{8,10},{9,11},{10,... | collective-permute-start | bytes 4718600 | tf_op jit(solution)/shard_map/ppermute | solution.py:45
  135.7 51.5 %collective-permute-start.20 = (bf16[128,1536]{1,0:T(8,128)(2,1)S(1)}, bf16[128,1536]{1,0:T(8,128)(2,1)S(1)}, u32[]{:S(2)}, u32[]{:S(2)}) collective-permute-start(bf16[128,1536]{1,0:T(8,128)(2,1)S(1)} %slice.283), channel_id=1, source_target_pairs={{0,16},{1,17},{2,18},{3,19},{4,20},{5,21},{6,22},{7,23},{8,24},{9,... | collective-permute-start | bytes 1179656 | tf_op jit(solution)/shard_map/ppermute | solution.py:45
  137.8 15.0 %collective-permute-start.21 = (bf16[128,1536]{1,0:T(8,128)(2,1)S(1)}, bf16[128,1536]{1,0:T(8,128)(2,1)S(1)}, u32[]{:S(2)}, u32[]{:S(2)}) collective-permute-start(bf16[128,1536]{1,0:T(8,128)(2,1)S(1)} %slice.285), channel_id=1, source_target_pairs={{0,16},{1,17},{2,18},{3,19},{4,20},{5,21},{6,22},{7,23},{8,24},{9,... | collective-permute-start | bytes 1179656 | tf_op jit(solution)/shard_map/ppermute | solution.py:45
  138.4 14.6 %collective-permute-start.22 = (bf16[128,1536]{1,0:T(8,128)(2,1)S(1)}, bf16[128,1536]{1,0:T(8,128)(2,1)S(1)}, u32[]{:S(2)}, u32[]{:S(2)}) collective-permute-start(bf16[128,1536]{1,0:T(8,128)(2,1)S(1)} %slice.287), channel_id=1, source_target_pairs={{0,1},{1,0},{2,3},{3,2},{4,5},{5,4},{6,7},{7,6},{8,9},{9,8},{10,11... | collective-permute-start | bytes 1179656 | tf_op jit(solution)/shard_map/ppermute | solution.py:45
  153.1 34.0 %collective-permute-start.23 = (bf16[256,1536]{1,0:T(8,128)(2,1)S(1)}, bf16[256,1536]{1,0:T(8,128)(2,1)S(1)}, u32[]{:S(2)}, u32[]{:S(2)}) collective-permute-start(bf16[256,1536]{1,0:T(8,128)(2,1)S(1)} %pad_maximum_fusion.16), channel_id=1, source_target_pairs={{0,4},{1,5},{2,6},{3,7},{4,0},{5,1},{6,2},{7,3},{8,12},{9,13},{10,... | collective-permute-start | bytes 2359304 | tf_op jit(solution)/shard_map/ppermute | solution.py:45
  154.0 33.3 %collective-permute-start.24 = (bf16[128,1536]{1,0:T(8,128)(2,1)S(1)}, bf16[128,1536]{1,0:T(8,128)(2,1)S(1)}, u32[]{:S(2)}, u32[]{:S(2)}) collective-permute-start(bf16[128,1536]{1,0:T(8,128)(2,1)S(1)} %slice.290), channel_id=1, source_target_pairs={{0,1},{1,0},{2,3},{3,2},{4,5},{5,4},{6,7},{7,6},{8,9},{9,8},{10,11... | collective-permute-start | bytes 1179656 | tf_op jit(solution)/shard_map/ppermute | solution.py:45
  (30 other events, 173.7 us)

commit v3 on v1

v3 whole, which is shorter than its diff:
```python
import functools

import jax
import jax.numpy as jnp
from jax import lax
from jax.experimental import pallas as pl
from jax.experimental.pallas import tpu as pltpu
from jax.sharding import PartitionSpec as P

inv_sqrt_two = 0.7071067811865476
inv_sqrt_two_pi = 0.3989422804014327
AXES = ("exp", "fsdp")
CORES = 2
DEPTH = 4


def contract_first(left, right):
    return lax.dot_general(
        left, right, (((0,), (0,)), ((), ())), preferred_element_type=jnp.float32
    )


def contract_last(left, right):
    return lax.dot_general(
        left, right, (((1,), (1,)), ((), ())), preferred_element_type=jnp.float32
    )


def gelu_parts(values):
    cdf_part = 0.5 * (1.0 + lax.erf(values * inv_sqrt_two))
    return (
        values * cdf_part,
        cdf_part + values * jnp.exp(-0.5 * values * values) * inv_sqrt_two_pi,
    )


class Copies:
    def __init__(self, sems):
        self.sems, self.all = sems, []

    def start(self, source, target):
        copy = pltpu.make_async_copy(source, target, self.sems.at[len(self.all)])
        copy.start()
        self.all.append(copy)
        return copy


def hidden_part(tok, grad, weight, scale, act_ref, hid_ref, columns):
    hidden = weight.shape[0] // 2
    pre = contract_last(tok, weight[:hidden, :])
    back = contract_last(grad, weight[hidden:, :])
    full, slope = gelu_parts(pre)
    act_ref[:, columns] = (full * scale).astype(jnp.bfloat16)
    hid_ref[:, columns] = (back * slope * scale).astype(jnp.bfloat16)
    return jnp.sum(full * back, axis=1, keepdims=True)


def gate_of(gate, expert):
    here = lax.broadcasted_iota(jnp.int32, gate.shape, 1) == expert
    return here, jnp.sum(jnp.where(here, gate, 0.0), axis=1, keepdims=True)


def decode(code, rows):
    wide_code = code.astype(jnp.float32)
    return (wide_code[:, :rows] + wide_code[:, rows:]).T


def far_kernel(plan, *refs):
    count, rows = plan
    refs = list(refs)
    take = lambda number: [refs.pop(0) for _ in range(number)]
    (first_ref,), pieces, weights_in = take(1), take(count), take(4)
    (act_out, hid_out), pieces_out = take(2), take(count)
    (tok, grad, coded_rows, extra), values = take(4), take(2)
    weights, stages, (sems_in, sems_out) = take(4), take(2), take(2)
    hidden = weights[0].shape[0] // 2
    tile = 2 * rows
    loads, stores = Copies(sems_in), Copies(sems_out)
    weight_ready, ready = [loads.start(weights_in[0], weights[0])], []

    def load_tile(t):
        group = []
        for b in (2 * t, 2 * t + 1):
            at = pl.ds(b * rows, rows)
            group.append(loads.start(pieces[b].at[pl.ds(0, rows)], tok.at[at]))
            group.append(loads.start(pieces[b].at[pl.ds(rows, rows)], grad.at[at]))
            source = pieces[b].at[pl.ds(2 * rows, SPARE), pl.ds(0, 2 * rows)]
            group.append(loads.start(source, coded_rows.at[b]))
        ready.append(group)

    load_tile(0)
    for i in range(1, 4):
        weight_ready.append(loads.start(weights_in[i], weights[i]))
    for t in range(1, count // 2):
        load_tile(t)
    first = first_ref[0]
    extra[...] = jnp.zeros_like(extra)
    staged, pending = [[], []], []
    for t in range(count // 2):
        span = pl.ds(t * tile, tile)
        for copy in ready[t]:
            copy.wait()
        gate = jnp.concatenate([decode(coded_rows[2 * t + k], rows) for k in range(2)], axis=0)
        total = 0.0
        for e in range(2):
            here, scale = gate_of(gate, first ^ e)
            part = 0.0
            for i in (2 * e, 2 * e + 1):
                if t == 0:
                    weight_ready[i].wait()
                part = part + hidden_part(
                    tok[span, :],
                    grad[span, :],
                    weights[i],
                    scale,
                    values[0].at[span],
                    values[1].at[span],
                    slice(i * hidden, (i + 1) * hidden),
                )
            total = total + jnp.where(here, part, 0.0)
        for value, target in zip(values, (act_out, hid_out)):
            source = value.at[span, pl.ds(0, 2 * hidden)]
            pending.append(stores.start(source, target.at[span]))
        for k in range(2):
            b = 2 * t + k
            encode(total[k * rows : (k + 1) * rows, :], extra, b, rows)
            pending.append(stores.start(extra.at[b], pieces_out[b].at[pl.ds(2 * rows, SPARE)]))
        for copy in staged[t % 2]:
            copy.wait()
        staged[t % 2] = []
        for kind, (stage, low) in enumerate(zip(stages, (hidden, 0))):
            lefts = [values[kind].at[span, pl.ds(i * hidden, hidden)] for i in range(4)]
            stage[t % 2] = partial_output(lefts, weights, low)
            for k in range(2):
                source = stage.at[t % 2, pl.ds(k * rows, rows)]
                target = pieces_out[2 * t + k].at[pl.ds(kind * rows, rows)]
                staged[t % 2].append(stores.start(source, target))
    for copy in pending + staged[0] + staged[1]:
        copy.wait()


def encode(score, extra, b, rows):
    rest = score.T
    high = rest.astype(jnp.bfloat16)
    extra[b, :, pl.ds(0, rows)] = high
    extra[b, :, pl.ds(rows, rows)] = (rest - high.astype(jnp.float32)).astype(jnp.bfloat16)


def partial_output(lefts, weights, low):
    hidden = weights[0].shape[0] // 2
    out = 0.0
    for left, weight in zip(lefts, weights):
        out = out + jnp.dot(
            left[...], weight[low : low + hidden, :], preferred_element_type=jnp.float32
        )
    return out.astype(jnp.bfloat16)


def split(stack, count, rows):
    step = 2 * rows + SPARE
    return [stack.at[pl.ds(b * step, step)] for b in range(count)]


def load_blocks(loads, blocks, slot, tok, grad, coded_rows, rows):
    started = []
    for k, block in enumerate(blocks):
        at = pl.ds(k * rows, rows)
        started.append(loads.start(block.at[pl.ds(0, rows)], tok.at[slot, at]))
        started.append(loads.start(block.at[pl.ds(rows, rows)], grad.at[slot, at]))
        if coded_rows is not None:
            source = block.at[pl.ds(2 * rows, SPARE), pl.ds(0, 2 * rows)]
            started.append(loads.start(source, coded_rows.at[slot, k]))
    return started


def add_sums(totals, acts, hids, tok, grad, slot, empty, results=None):
    hidden = totals.shape[1]
    for which, (left, right) in enumerate(((hids, tok), (acts, grad))):
        for k in range(2):
            out = contract_first(left[slot, :, k * hidden : (k + 1) * hidden], right[slot])
            if not empty:
                out = out + totals[2 * which + k]
            if results is None or k == 0:
                totals[2 * which + k] = out
            else:
                results[which] = out.astype(jnp.bfloat16)


def sums_kernel(plan, *refs):
    count, rows = plan
    refs = list(refs)
    take = lambda number: [refs.pop(0) for _ in range(number)]
    (first_ref,), near, far, (near_over,) = take(1), take(count), take(count), take(1)
    far_over, far_values = take(count), take(2)
    weights_in, near_values, keep_out, near_sums, (score,) = take(2), take(2), take(2), take(2), take(1)
    tok, grad, coded_rows, acts, hids, totals, results = take(7)
    weights, (sems_in, sems_out) = take(2), take(2)
    group = 4
    tile = group * rows
    hidden = weights[0].shape[0] // 2
    loads, stores = Copies(sems_in), Copies(sems_out)
    lists = [near, far, split(near_over, count, rows), far_over]
    steps = [
        (kind, g, blocks[g * group : (g + 1) * group])
        for kind, blocks in enumerate(lists)
        for g in range(count // group)
    ]

    def load(n):
        kind, g, blocks = steps[n]
        codes = None if kind == 1 else coded_rows
        started = load_blocks(loads, blocks, n % 2, tok, grad, codes, rows)
        if kind == 1:
            for source, target in zip(far_values, (acts, hids)):
                source = source.at[pl.ds(g * tile, tile)]
                started.append(loads.start(source, target.at[n % 2]))
        return started

    weight_ready = [loads.start(weights_in[0], weights[0])]
    ready = load(0)
    weight_ready.append(loads.start(weights_in[1], weights[1]))
    first = first_ref[0]
    saved = [[], []]
    for n, (kind, g, blocks) in enumerate(steps):
        slot = n % 2
        for copy in saved[1 - slot]:
            copy.wait()
        saved[1 - slot] = []
        coming = load(n + 1) if n + 1 < len(steps) else []
        for copy in ready:
            copy.wait()
        ready = coming
        if kind != 1:
            gate = jnp.concatenate([decode(coded_rows[slot, k], rows) for k in range(group)], axis=0)
            here, scale = gate_of(gate, first)
            part = 0.0
            for k in range(2):
                if n == 0:
                    weight_ready[k].wait()
                columns = slice(k * hidden, (k + 1) * hidden)
                part = part + hidden_part(
                    tok[slot], grad[slot], weights[k], scale, acts.at[slot], hids.at[slot], columns
                )
        if kind == 0:
            span = pl.ds(g * tile, tile)
            score[span, :] = jnp.where(here, part, 0.0)
            saved[slot] = [
                stores.start(acts.at[slot], near_values[0].at[span]),
                stores.start(hids.at[slot], near_values[1].at[span]),
            ]
        last = n + 1 == len(steps)
        add_sums(totals, acts, hids, tok, grad, slot, n == 0, results if last else None)
    tail = [stores.start(totals.at[2 * which], keep_out[which]) for which in range(2)]
    tail += [stores.start(results.at[which], near_sums[which]) for which in range(2)]
    for copy in saved[0] + saved[1] + tail:
        copy.wait()


def near_kernel(plan, *refs):
    count, rows = plan
    refs = list(refs)
    take = lambda number: [refs.pop(0) for _ in range(number)]
    (first_ref, score), near, values_in, weights_in = take(2), take(count), take(2), take(4)
    pieces_out = take(count)
    tok, grad, coded_rows, extra, acts, hids, others, outs = take(8)
    weights, (sems_in, sems_out) = take(4), take(2)
    hidden = weights[0].shape[0] // 2
    group = 4
    tile = group * rows
    loads, stores = Copies(sems_in), Copies(sems_out)

    def load(g):
        blocks, span = near[g * group : (g + 1) * group], pl.ds(g * tile, tile)
        started = load_blocks(loads, blocks, g % 2, tok, grad, coded_rows, rows)
        for source, target in zip(values_in, (acts, hids)):
            started.append(loads.start(source.at[span], target.at[g % 2]))
        return started

    weight_ready = {2: loads.start(weights_in[2], weights[2])}
    ready = load(0)
    for i in (3, 0, 1):
        weight_ready[i] = loads.start(weights_in[i], weights[i])
    first = first_ref[0]
    extra[...] = jnp.zeros_like(extra)
    out_copies = []
    for g in range(count // group):
        slot = g % 2
        coming = load(g + 1) if (g + 1) * group < count else []
        for copy in ready + out_copies:
            copy.wait()
        ready, out_copies = coming, []
        gate = jnp.concatenate([decode(coded_rows[slot, k], rows) for k in range(group)], axis=0)
        here, scale = gate_of(gate, first ^ 1)
        part = 0.0
        for k in range(2):
            if g == 0:
                weight_ready[2 + k].wait()
            columns = slice(k * hidden, (k + 1) * hidden)
            part = part + hidden_part(
                tok[slot], grad[slot], weights[2 + k], scale, others.at[0], others.at[1], columns
            )
        total = score[pl.ds(g * tile, tile), :] + jnp.where(here, part, 0.0)
        if g == 0:
            weight_ready[0].wait()
            weight_ready[1].wait()
        for k in range(group):
            b = g * group + k
            encode(total[k * rows : (k + 1) * rows, :], extra, b, rows)
            out_copies.append(stores.start(extra.at[b], pieces_out[b].at[pl.ds(2 * rows, SPARE)]))
        for which, (mine, low) in enumerate(((acts, hidden), (hids, 0))):
            lefts = [mine.at[slot, :, pl.ds(k * hidden, hidden)] for k in range(2)]
            lefts += [others.at[which, :, pl.ds(k * hidden, hidden)] for k in range(2)]
            outs[which] = partial_output(lefts, weights, low)
            for k in range(group):
                source = outs.at[which, pl.ds(k * rows, rows)]
                target = pieces_out[g * group + k].at[pl.ds(which * rows, rows)]
                out_copies.append(stores.start(source, target))
    for copy in out_copies:
        copy.wait()


ANYWHERE = pl.BlockSpec(memory_space=pl.ANY)
IN_VMEM = pl.BlockSpec(memory_space=pltpu.VMEM)
IN_SMEM = pl.BlockSpec(memory_space=pltpu.SMEM)
SPARE = 16


def kernel_params(flops=10**11):
    return dict(
        compiler_params=pltpu.CompilerParams(vmem_limit_bytes=58 * 2**20),
        cost_estimate=pl.CostEstimate(flops=flops, bytes_accessed=flops // 10**3, transcendentals=0),
    )


def far_call(rows, first, pieces, weights):
    count, features = len(pieces), pieces[0].shape[1]
    hidden = weights[0].shape[0] // 2
    height = count * rows
    bf = jnp.bfloat16
    shape = jax.ShapeDtypeStruct
    outs = pl.pallas_call(
        functools.partial(far_kernel, (count, rows)),
        out_shape=[shape((height, 2 * hidden), bf)] * 2
        + [shape((2 * rows + SPARE, features), bf)] * count,
        in_specs=[IN_SMEM] + [ANYWHERE] * (count + 4),
        out_specs=[ANYWHERE] * (2 + count),
        scratch_shapes=[pltpu.VMEM((height, features), bf)] * 2
        + [pltpu.VMEM((count, SPARE, 2 * rows), bf)]
        + [pltpu.VMEM((count, SPARE, features), bf)]
        + [pltpu.VMEM((height, 4 * hidden), bf)] * 2
        + [pltpu.VMEM((2 * hidden, features), bf)] * 4
        + [pltpu.VMEM((2, 2 * rows, features), bf)] * 2
        + [pltpu.SemaphoreType.DMA((3 * count + 4,)), pltpu.SemaphoreType.DMA((4 * count,))],
        **kernel_params(),
    )(first, *pieces, *weights)
    return outs[:2], outs[2:]


def sums_call(rows, first, near, far, near_over, far_over, far_values, weights):
    count, features = len(near), near[0].shape[1]
    hidden = weights[0].shape[0] // 2
    height, tile = count * rows, 4 * rows
    bf, f32 = jnp.bfloat16, jnp.float32
    shape = jax.ShapeDtypeStruct
    outs = pl.pallas_call(
        functools.partial(sums_kernel, (count, rows)),
        out_shape=[shape((height, 2 * hidden), bf)] * 2
        + [shape((hidden, features), f32)] * 2
        + [shape((hidden, features), bf)] * 2
        + [shape((height, SPARE), f32)],
        in_specs=[IN_SMEM] + [ANYWHERE] * (3 * count + 5),
        out_specs=[ANYWHERE] * 6 + [IN_VMEM],
        scratch_shapes=[pltpu.VMEM((2, tile, features), bf)] * 2
        + [pltpu.VMEM((2, 4, SPARE, 2 * rows), bf)]
        + [pltpu.VMEM((2, tile, 2 * hidden), bf)] * 2
        + [pltpu.VMEM((4, hidden, features), f32)]
        + [pltpu.VMEM((2, hidden, features), bf)]
        + [pltpu.VMEM((2 * hidden, features), bf)] * 2
        + [pltpu.SemaphoreType.DMA((12 * count + 2,)), pltpu.SemaphoreType.DMA((count + 4,))],
        **kernel_params(),
    )(first, *near, *far, near_over, *far_over, *far_values, *weights)
    return outs[:2], outs[2:4], outs[4:6], outs[6]


def near_call(rows, first, score, near, values, weights):
    count, features = len(near), near[0].shape[1]
    hidden = weights[0].shape[0] // 2
    tile = 4 * rows
    bf = jnp.bfloat16
    return pl.pallas_call(
        functools.partial(near_kernel, (count, rows)),
        out_shape=[jax.ShapeDtypeStruct((2 * rows + SPARE, features), bf)] * count,
        in_specs=[IN_SMEM, IN_VMEM] + [ANYWHERE] * (count + 6),
        out_specs=[ANYWHERE] * count,
        scratch_shapes=[pltpu.VMEM((2, tile, features), bf)] * 2
        + [pltpu.VMEM((2, 4, SPARE, 2 * rows), bf)]
        + [pltpu.VMEM((count, SPARE, features), bf)]
        + [pltpu.VMEM((2, tile, 2 * hidden), bf)] * 3
        + [pltpu.VMEM((2, tile, features), bf)]
        + [pltpu.VMEM((2 * hidden, features), bf)] * 4
        + [pltpu.SemaphoreType.DMA((4 * count + 4,)), pltpu.SemaphoreType.DMA((3 * count,))],
        **kernel_params(1000),
    )(first, score, *near, *values, *weights)


def coded(rows_of, features):
    high = lax.reduce_precision(rows_of, 8, 7)
    both = jnp.concatenate([high, rows_of - high], axis=1).astype(jnp.bfloat16)
    return jnp.pad(both, ((0, SPARE - both.shape[0]), (0, features - both.shape[1])))


class Grid:
    def __init__(self, n_exp, n_fsdp):
        self.nx, self.ny = n_exp // CORES, n_fsdp // DEPTH

    def move(self, array, to):
        pairs = []
        for x in range(self.nx):
            for c in range(CORES):
                for z in range(DEPTH):
                    for y in range(self.ny):
                        tx, tc, tz, ty = to(x, c, z, y)
                        pairs.append((self.index(x, c, z, y), self.index(tx, tc, tz, ty)))
        return lax.ppermute(array, AXES, pairs)

    def index(self, x, c, z, y):
        return ((x * CORES + c) * DEPTH + z) * self.ny + y

    def spread(self, array, dx, dy):
        if dx == dy == 0:
            return array
        return self.move(
            array, lambda x, c, z, y: ((x - dx) % self.nx, c, z, (y - dy) % self.ny)
        )

    def collect(self, array, dx, dy):
        if dx == dy == 0:
            return array
        return self.move(
            array, lambda x, c, z, y: ((x + dx) % self.nx, c, z, (y + dy) % self.ny)
        )

    def swap_core(self, array):
        return self.move(array, lambda x, c, z, y: (x, 1 - c, z, y))

    def swap_far(self, array):
        return self.move(array, lambda x, c, z, y: (x, c, z ^ 2, y))

    def swap_near(self, array):
        return self.move(array, lambda x, c, z, y: (x, c, z ^ 1, y))


def wide(array):
    return array.astype(jnp.float32)


def total(parts):
    out = wide(parts[0])
    for part in parts[1:]:
        out = out + wide(part)
    return out


def tie(*groups):
    return lax.optimization_barrier(groups)


def shards(tokens, expert_ids, gates, w_in, w_out, grad_y):
    rows, features = tokens.shape
    n_exp, n_fsdp = lax.axis_size("exp"), lax.axis_size("fsdp")
    grid = Grid(n_exp, n_fsdp)
    steps = [(xo, yo) for yo in range(grid.ny) for xo in range(grid.nx)]
    bf = jnp.bfloat16
    first = jnp.reshape(lax.axis_index("exp"), (1,))

    ids_row = expert_ids.T[None, :, :]
    named = ids_row == jnp.arange(n_exp, dtype=jnp.int32)[:, None, None]
    gate_rows = jnp.sum(jnp.where(named, gates.T[None], 0.0), axis=1)

    own = jnp.concatenate([tokens, grad_y, coded(gate_rows, features)], axis=0)
    far = grid.swap_far(own)
    own_weights = jnp.concatenate([w_in[0], w_out[0]], axis=0)
    near_weights = grid.swap_near(own_weights)
    near_pieces = [grid.spread(own, *step) for step in steps]
    near_pieces, far, core_weights = tie(near_pieces, far, own_weights)
    far_pieces = [grid.spread(far, *step) for step in steps]
    near_over = grid.swap_core(jnp.concatenate(near_pieces, axis=0))
    other_own = grid.swap_core(core_weights)
    far_pieces, other_own = tie(far_pieces, other_own)
    other_near = grid.swap_core(near_weights)
    weights = [own_weights, near_weights, other_own, other_near]
    far_values, far_out = far_call(rows, first, far_pieces, weights)

    far_home = [grid.collect(part, *step) for part, step in zip(far_out, steps)]
    far_over = [grid.swap_core(piece) for piece in far_pieces]
    near_values, keep, near_sums, score = sums_call(
        rows, first, near_pieces, far_pieces, near_over, far_over, far_values, weights[:2]
    )
    near_out = near_call(rows, first, score, near_pieces, near_values, weights)
    far_home, near_out, _ = tie(far_home, near_out, near_sums)
    near_sums = [grid.swap_near(part) for part in near_sums]
    far_home = total(far_home)

    def score_of(home):
        return home[2 * rows :, :rows] + home[2 * rows :, rows : 2 * rows]

    far_home = jnp.concatenate(
        [far_home[: 2 * rows].astype(bf), coded(score_of(far_home), features)], axis=0
    )
    far_home = grid.swap_far(far_home)
    near_home = total([grid.collect(part, *step) for part, step in zip(near_out, steps)])

    home = near_home + wide(far_home)
    mixed, grad_tokens = home[:rows].astype(bf), home[rows : 2 * rows].astype(bf)
    score = score_of(home)[:n_exp]
    grad_gates = jnp.sum(jnp.where(named, score[:, None, :], 0.0), axis=0).T
    grad_in, grad_out = [mine + wide(theirs) for mine, theirs in zip(keep, near_sums)]
    return (mixed, grad_tokens, grad_in[None], grad_out[None], grad_gates)


def solution(mesh):
    rows = P(AXES, None)
    weights = P("exp", "fsdp", None)
    return jax.shard_map(
        shards,
        mesh=mesh,
        in_specs=(rows, rows, rows, weights, weights, rows),
        out_specs=(rows, rows, weights, weights, rows),
        check_vma=False,
    )
```

time: 291 us -> 194 us (0.67)
  waiting for transfers between devices: 157 us -> 111 us
  Pallas kernels: 0 us -> 42 us
  matrix products: 35.4 us -> 0 us
  local copies, waits for them, and re-layouts: 36.7 us -> 2.06 us
  starting transfers between devices: 43.7 us -> 26.3 us
  other arithmetic: 14.8 us -> 11.6 us
    ppermute x44 -> x24, waiting for transfers between devices: 157 us -> 111 us  [move(): return lax.ppermute(array, AXES, pairs)]
    pallas_call x0 -> x3, Pallas kernels: none -> 42 us  [the longest x1 19.1 us: sums_call(): pl.pallas_call(functools.partial(sums_kernel, (count, rows)), out_shape=[...]
    dot_general x12 -> x0, matrix products: 35.4 us -> none  [the longest x4 17.5 us: contract_last(): lax.dot_general(left, right, (((1,), (1,)), ((), ())), preferred_element_...]
    unnamed x91 -> x42, local copies, waits for them, and re-layouts: 21.3 us -> 1.05 us
    ppermute x44 -> x24, starting transfers between devices: 43.7 us -> 26.3 us  [move(): return lax.ppermute(array, AXES, pairs)]
    reshape x4 -> x0, local copies, waits for them, and re-layouts: 8.3 us -> none  [the longest x2 8.01 us: shards(): score = jnp.sum((act * back).reshape(-1, 2, 2 * hidden), axis=-1)]
    concatenate x0 -> x6, other arithmetic: none -> 7.36 us  [the longest x1 5.69 us: shards(): near_over = grid.swap_core(jnp.concatenate(near_pieces, axis=0))]
    reduce_sum x3 -> x2, other arithmetic: 5.77 us -> 0.59 us  [the longest x1 0.58 us: shards(): grad_gates = jnp.sum(jnp.where(named, score[:, None, :], 0.0), axis=0).T]
  transfers between devices with their start and end apart: 44 -> 24, of which waited for: 25 -> 11; matrix products, arithmetic and copies ran while one was open for 18% -> 5% of each run, Pallas kernels for 0% -> 22%
where the time goes in v3:
time: 194 us
  waiting for transfers between devices  111 us (57%)
  Pallas kernels  42 us (22%)
  starting transfers between devices  26.3 us (14%)
  other arithmetic  11.6 us (6%)
  local copies, waits for them, and re-layouts  2.06 us (1%)
    ppermute x24, waiting for transfers between devices, move(): return lax.ppermute(array, AXES, pairs)  111 us
    ppermute x24, starting transfers between devices, move(): return lax.ppermute(array, AXES, pairs)  26.3 us
    pallas_call x1, Pallas kernels, sums_call(): pl.pallas_call(functools.partial(sums_kernel, (count, rows)), out_shape=[...  19.1 us
    pallas_call x1, Pallas kernels, far_call(): pl.pallas_call(functools.partial(far_kernel, (count, rows)), out_shape=[s...  11.5 us
    pallas_call x1, Pallas kernels, near_call(): pl.pallas_call(functools.partial(near_kernel, (count, rows)), out_shape=[...  11.4 us
    concatenate x1, other arithmetic, shards(): near_over = grid.swap_core(jnp.concatenate(near_pieces, axis=0))  5.69 us
  transfers between devices with their start and end apart: 24, of which 11 were waited for; matrix products, arithmetic and copies ran while one was open for 5% of the time, Pallas kernels for 22%

profile of v3, /device:TPU:0, one launch (start us, length us, event | category | flops | bytes accessed | tf_op | source)
XLA Modules:
  0.0 194.1 jit_solution(787372524324125921)
XLA Ops:
  0.7 1.5 pad_maximum_fusion.1.refs_5_.refs_16_.refs_8_
  2.2 3.1 %collective-permute-start.8 = (bf16[512,1536]{1,0:T(8,128)(2,1)S(1)}, bf16[512,1536]{1,0:T(8,128)(2,1)}, u32[]{:S(2)}, u32[]{:S(2)}) collective-permute-start(bf16[512,1536]{1,0:T(8,128)(2,1)S(1)} %pad_maximum_fusion.1.refs_5_.refs_16_.refs_8_), channel_id=1, source_target_pairs={{0,2},{1,3},{2,0},{3,1},{4,6},{5,7},{6,4},{7,5},{8,10},{9,11},{10,... | collective-permute-start | bytes 4718600 | tf_op jit(solution)/shard_map/ppermute | solution.py:424
  5.5 1.6 collective-permute-start
  7.0 1.5 collective-permute-start.1
  9.0 2.6 %collective-permute-start.3 = (bf16[272,1536]{1,0:T(8,128)(2,1)S(1)}, bf16[272,1536]{1,0:T(8,128)(2,1)}, u32[]{:S(2)}, u32[]{:S(2)}) collective-permute-start(bf16[272,1536]{1,0:T(8,128)(2,1)S(1)} %pad_maximum_fusion.2.refs_1_.refs_2_), channel_id=1, source_target_pairs={{0,4},{1,5},{2,6},{3,7},{4,0},{5,1},{6,2},{7,3},{8,12},{9,13},{10,... | collective-permute-start | bytes 2506760 | tf_op jit(solution)/shard_map/ppermute | solution.py:424
  11.6 15.4 %collective-permute-done.refs_2_.refs_3_ = bf16[272,1536]{1,0:T(8,128)(2,1)S(1)} collective-permute-done((bf16[272,1536]{1,0:T(8,128)(2,1)S(1)}, bf16[272,1536]{1,0:T(8,128)(2,1)S(1)}, u32[]{:S(2)}, u32[]{:S(2)}) %collective-permute-start) | collective-permute-done | bytes 835616 | tf_op jit(solution)/shard_map/ppermute | solution.py:424
  27.0 17.7 %collective-permute-done.1.refs_3_.refs_4_ = bf16[272,1536]{1,0:T(8,128)(2,1)S(1)} collective-permute-done((bf16[272,1536]{1,0:T(8,128)(2,1)S(1)}, bf16[272,1536]{1,0:T(8,128)(2,1)S(1)}, u32[]{:S(2)}, u32[]{:S(2)}) %collective-permute-start.1) | collective-permute-done | bytes 835616 | tf_op jit(solution)/shard_map/ppermute | solution.py:424
  44.7 12.2 %collective-permute-done.3.refs_1_.refs_5_ = bf16[272,1536]{1,0:T(8,128)(2,1)} collective-permute-done((bf16[272,1536]{1,0:T(8,128)(2,1)S(1)}, bf16[272,1536]{1,0:T(8,128)(2,1)}, u32[]{:S(2)}, u32[]{:S(2)}) %collective-permute-start.3) | collective-permute-done | bytes 835616 | tf_op jit(solution)/shard_map/ppermute | solution.py:424
  57.7 1.7 collective-permute-start.4
  59.5 1.5 collective-permute-start.5
  61.3 5.7 %pad_maximum_fusion = bf16[1088,1536]{1,0:T(8,128)(2,1)} fusion(bf16[272,1536]{1,0:T(8,128)(2,1)} %copy-done.4, bf16[272,1536]{1,0:T(8,128)(2,1)} %copy-done.3, bf16[272,1536]{1,0:T(8,128)(2,1)S(1)} %collective-permute-done.refs_2_.refs_3_, bf16[272,1536]{1,0:T(8,128)(2,1)S(1)} %pad_maximum_fusion.2.refs_1_.refs_2_), kind=kLoop, calls=%fused_computation | loop fusion | flops 13369344 | bytes 6684672 | tf_op jit(solution)/shard_map/concatenate | solution.py:487
  67.0 12.5 %collective-permute-done.4.refs_2_.refs_6_ = bf16[272,1536]{1,0:T(8,128)(2,1)} collective-permute-done((bf16[272,1536]{1,0:T(8,128)(2,1)}, bf16[272,1536]{1,0:T(8,128)(2,1)}, u32[]{:S(2)}, u32[]{:S(2)}) %collective-permute-start.4) | collective-permute-done | bytes 835616 | tf_op jit(solution)/shard_map/ppermute | solution.py:424
  79.5 18.8 %collective-permute-done.5.refs_3_.refs_7_ = bf16[272,1536]{1,0:T(8,128)(2,1)} collective-permute-done((bf16[272,1536]{1,0:T(8,128)(2,1)}, bf16[272,1536]{1,0:T(8,128)(2,1)}, u32[]{:S(2)}, u32[]{:S(2)}) %collective-permute-start.5) | collective-permute-done | bytes 835616 | tf_op jit(solution)/shard_map/ppermute | solution.py:424
  99.4 11.5 %shard_map.101 = (bf16[512,512]{1,0:T(8,128)(2,1)}, bf16[512,512]{1,0:T(8,128)(2,1)}, bf16[272,1536]{1,0:T(8,128)(2,1)}, bf16[272,1536]{1,0:T(8,128)(2,1)}, bf16...) custom-call(s32[1]{0:T(128)} %bitcast.refs_0_, bf16[272,1536]{1,0:T(8,128)(2,1)} %collective-permute-done.3.refs_1_.refs_5_, ...), custom_call_target="tpu_custom_call" | custom-call | flops 99999997952 | bytes 100000000 | tf_op jit(solution)/shard_map/pallas_call | solution.py:341
  113.1 1.4 collective-permute-start.12
  115.5 19.1 %shard_map.102 = (bf16[512,512]{1,0:T(8,128)(2,1)}, bf16[512,512]{1,0:T(8,128)(2,1)}, f32[256,1536]{1,0:T(8,128)}, f32[256,1536]{1,0:T(8,128)}, bf16[256,1536]{1...) custom-call(s32[1]{0:T(128)} %bitcast.refs_0_, bf16[272,1536]{1,0:T(8,128)(2,1)} %copy-done, ...), custom_call_target="tpu_custom_call" | custom-call | flops 99999997952 | bytes 100000000 | tf_op jit(solution)/shard_map/pallas_call | solution.py:365
  134.6 2.7 %collective-permute-start.22 = (bf16[256,1536]{1,0:T(8,128)(2,1)}, bf16[256,1536]{1,0:T(8,128)(2,1)S(1)}, u32[]{:S(2)}, u32[]{:S(2)}) collective-permute-start(bf16[256,1536]{1,0:T(8,128)(2,1)} %get-tuple-element.65), channel_id=1, source_target_pairs={{0,2},{1,3},{2,0},{3,1},{4,6},{5,7},{6,4},{7,5},{8,10},{9,11},{10,... | collective-permute-start | bytes 2359304 | tf_op jit(solution)/shard_map/ppermute | solution.py:424
  137.4 11.4 %shard_map.103 = (bf16[272,1536]{1,0:T(8,128)(2,1)}, bf16[272,1536]{1,0:T(8,128)(2,1)}, bf16[272,1536]{1,0:T(8,128)(2,1)}, bf16[272,1536]{1,0:T(8,128)(2,1)}) custom-call(s32[1]{0:T(128)} %bitcast.refs_0_, f32[512,16]{1,0:T(8,128)} %get-tuple-element.58.refs_1_, bf16[272,1536]{1,0:T(8,128)(2,1)} %copy-done, bf16[272,1536]{1,0:T(8,128)(2,1)} %copy-done.2, ...), custom_call_target="tpu_custom_call" | custom-call | flops 1000 | bytes 1 | tf_op jit(solution)/shard_map/pallas_call | solution.py:390
  149.1 1.5 collective-permute-done.12
  151.2 2.6 %collective-permute-start.21 = (bf16[272,1536]{1,0:T(8,128)(2,1)S(1)}, bf16[272,1536]{1,0:T(8,128)(2,1)S(1)}, u32[]{:S(2)}, u32[]{:S(2)}) collective-permute-start(bf16[272,1536]{1,0:T(8,128)(2,1)S(1)} %pad_maximum_fusion.3), channel_id=1, source_target_pairs={{0,4},{1,5},{2,6},{3,7},{4,0},{5,1},{6,2},{7,3},{8,12},{9,13},{10,... | collective-permute-start | bytes 2506760 | tf_op jit(solution)/shard_map/ppermute | solution.py:424
  153.9 1.8 collective-permute-start.20
  156.1 17.8 %collective-permute-done.22 = bf16[256,1536]{1,0:T(8,128)(2,1)S(1)} collective-permute-done((bf16[256,1536]{1,0:T(8,128)(2,1)}, bf16[256,1536]{1,0:T(8,128)(2,1)S(1)}, u32[]{:S(2)}, u32[]{:S(2)}) %collective-permute-start.22) | collective-permute-done | bytes 786464 | tf_op jit(solution)/shard_map/ppermute | solution.py:424
  176.5 12.7 %collective-permute-done.23 = bf16[256,1536]{1,0:T(8,128)(2,1)S(1)} collective-permute-done((bf16[256,1536]{1,0:T(8,128)(2,1)}, bf16[256,1536]{1,0:T(8,128)(2,1)S(1)}, u32[]{:S(2)}, u32[]{:S(2)}) %collective-permute-start.23) | collective-permute-done | bytes 786464 | tf_op jit(solution)/shard_map/ppermute | solution.py:424
  189.3 1.4 add_bitcast_fusion
  (87 shorter events, 13.3 us)
Async XLA Ops:
  2.2 55.5 %collective-permute-start.8 = (bf16[512,1536]{1,0:T(8,128)(2,1)S(1)}, bf16[512,1536]{1,0:T(8,128)(2,1)}, u32[]{:S(2)}, u32[]{:S(2)}) collective-permute-start(bf16[512,1536]{1,0:T(8,128)(2,1)S(1)} %pad_maximum_fusion.1.refs_5_.refs_16_.refs_8_), channel_id=1, source_target_pairs={{0,2},{1,3},{2,0},{3,1},{4,6},{5,7},{6,4},{7,5},{8,10},{9,11},{10,... | collective-permute-start | bytes 4718600 | tf_op jit(solution)/shard_map/ppermute | solution.py:424
  5.5 21.6 %collective-permute-start = (bf16[272,1536]{1,0:T(8,128)(2,1)S(1)}, bf16[272,1536]{1,0:T(8,128)(2,1)S(1)}, u32[]{:S(2)}, u32[]{:S(2)}) collective-permute-start(bf16[272,1536]{1,0:T(8,128)(2,1)S(1)} %pad_maximum_fusion.2.refs_1_.refs_2_), channel_id=1, source_target_pairs={{0,16},{1,17},{2,18},{3,19},{4,20},{5,21},{6,22},{7,23},{8,24},{9,... | collective-permute-start | bytes 2506760 | tf_op jit(solution)/shard_map/ppermute | solution.py:424
  7.0 37.7 %collective-permute-start.1 = (bf16[272,1536]{1,0:T(8,128)(2,1)S(1)}, bf16[272,1536]{1,0:T(8,128)(2,1)S(1)}, u32[]{:S(2)}, u32[]{:S(2)}) collective-permute-start(bf16[272,1536]{1,0:T(8,128)(2,1)S(1)} %pad_maximum_fusion.2.refs_1_.refs_2_), channel_id=1, source_target_pairs={{0,1},{1,0},{2,3},{3,2},{4,5},{5,4},{6,7},{7,6},{8,9},{9,8},{10,11... | collective-permute-start | bytes 2506760 | tf_op jit(solution)/shard_map/ppermute | solution.py:424
  8.5 36.2 %collective-permute-start.2 = (bf16[272,1536]{1,0:T(8,128)(2,1)S(1)}, bf16[272,1536]{1,0:T(8,128)(2,1)S(1)}, u32[]{:S(2)}, u32[]{:S(2)}) collective-permute-start(bf16[272,1536]{1,0:T(8,128)(2,1)S(1)} %pad_maximum_fusion.2.refs_1_.refs_2_), channel_id=1, source_target_pairs={{0,17},{1,16},{2,19},{3,18},{4,21},{5,20},{6,23},{7,22},{8,25},{9,... | collective-permute-start | bytes 2506760 | tf_op jit(solution)/shard_map/ppermute | solution.py:424
  9.0 47.9 %collective-permute-start.3 = (bf16[272,1536]{1,0:T(8,128)(2,1)S(1)}, bf16[272,1536]{1,0:T(8,128)(2,1)}, u32[]{:S(2)}, u32[]{:S(2)}) collective-permute-start(bf16[272,1536]{1,0:T(8,128)(2,1)S(1)} %pad_maximum_fusion.2.refs_1_.refs_2_), channel_id=1, source_target_pairs={{0,4},{1,5},{2,6},{3,7},{4,0},{5,1},{6,2},{7,3},{8,12},{9,13},{10,... | collective-permute-start | bytes 2506760 | tf_op jit(solution)/shard_map/ppermute | solution.py:424
  56.9 41.5 %collective-permute-start.7 = (bf16[512,1536]{1,0:T(8,128)(2,1)S(1)}, bf16[512,1536]{1,0:T(8,128)(2,1)}, u32[]{:S(2)}, u32[]{:S(2)}) collective-permute-start(bf16[512,1536]{1,0:T(8,128)(2,1)S(1)} %pad_maximum_fusion.1.refs_5_.refs_16_.refs_8_), channel_id=1, source_target_pairs={{0,8},{1,9},{2,10},{3,11},{4,12},{5,13},{6,14},{7,15},{8,0},{9,1},... | collective-permute-start | bytes 4718600 | tf_op jit(solution)/shard_map/ppermute | solution.py:424
  57.7 41.2 %collective-permute-start.9 = (bf16[512,1536]{1,0:T(8,128)(2,1)}, bf16[512,1536]{1,0:T(8,128)(2,1)}, u32[]{:S(2)}, u32[]{:S(2)}) collective-permute-start(bf16[512,1536]{1,0:T(8,128)(2,1)} %collective-permute-done.8.refs_6_.refs_17_.refs_9_), channel_id=1, source_target_pairs={{0,8},{1,9},{2,10},{3,11},{4,12},{5,13},{6,14},{7,15},{8,0},{9,1},... | collective-permute-start | bytes 4718600 | tf_op jit(solution)/shard_map/ppermute | solution.py:424
  57.7 21.8 %collective-permute-start.4 = (bf16[272,1536]{1,0:T(8,128)(2,1)}, bf16[272,1536]{1,0:T(8,128)(2,1)}, u32[]{:S(2)}, u32[]{:S(2)}) collective-permute-start(bf16[272,1536]{1,0:T(8,128)(2,1)} %collective-permute-done.3.refs_1_.refs_5_), channel_id=1, source_target_pairs={{0,16},{1,17},{2,18},{3,19},{4,20},{5,21},{6,22},{7,23},{8,24},{9,... | collective-permute-start | bytes 2506760 | tf_op jit(solution)/shard_map/ppermute | solution.py:424
  59.5 38.9 %collective-permute-start.5 = (bf16[272,1536]{1,0:T(8,128)(2,1)}, bf16[272,1536]{1,0:T(8,128)(2,1)}, u32[]{:S(2)}, u32[]{:S(2)}) collective-permute-start(bf16[272,1536]{1,0:T(8,128)(2,1)} %collective-permute-done.3.refs_1_.refs_5_), channel_id=1, source_target_pairs={{0,1},{1,0},{2,3},{3,2},{4,5},{5,4},{6,7},{7,6},{8,9},{9,8},{10,11... | collective-permute-start | bytes 2506760 | tf_op jit(solution)/shard_map/ppermute | solution.py:424
  61.0 37.4 %collective-permute-start.6 = (bf16[272,1536]{1,0:T(8,128)(2,1)}, bf16[272,1536]{1,0:T(8,128)(2,1)}, u32[]{:S(2)}, u32[]{:S(2)}) collective-permute-start(bf16[272,1536]{1,0:T(8,128)(2,1)} %collective-permute-done.3.refs_1_.refs_5_), channel_id=1, source_target_pairs={{0,17},{1,16},{2,19},{3,18},{4,21},{5,20},{6,23},{7,22},{8,25},{9,... | collective-permute-start | bytes 2506760 | tf_op jit(solution)/shard_map/ppermute | solution.py:424
  79.5 35.0 %collective-permute-start.13 = (bf16[1088,1536]{1,0:T(8,128)(2,1)}, bf16[1088,1536]{1,0:T(8,128)(2,1)}, u32[]{:S(2)}, u32[]{:S(2)}) collective-permute-start(bf16[1088,1536]{1,0:T(8,128)(2,1)} %pad_maximum_fusion), channel_id=1, source_target_pairs={{0,8},{1,9},{2,10},{3,11},{4,12},{5,13},{6,14},{7,15},{8,0},{9,1},... | collective-permute-start | bytes 10027016 | tf_op jit(solution)/shard_map/ppermute | solution.py:424
  98.4 12.5 %collective-permute-start.14 = (bf16[272,1536]{1,0:T(8,128)(2,1)}, bf16[272,1536]{1,0:T(8,128)(2,1)S(1)}, u32[]{:S(2)}, u32[]{:S(2)}) collective-permute-start(bf16[272,1536]{1,0:T(8,128)(2,1)} %collective-permute-done.3.refs_1_.refs_5_), channel_id=1, source_target_pairs={{0,8},{1,9},{2,10},{3,11},{4,12},{5,13},{6,14},{7,15},{8,0},{9,1},... | collective-permute-start | bytes 2506760 | tf_op jit(solution)/shard_map/ppermute | solution.py:424
  98.4 13.9 %collective-permute-start.15 = (bf16[272,1536]{1,0:T(8,128)(2,1)}, bf16[272,1536]{1,0:T(8,128)(2,1)S(1)}, u32[]{:S(2)}, u32[]{:S(2)}) collective-permute-start(bf16[272,1536]{1,0:T(8,128)(2,1)} %collective-permute-done.4.refs_2_.refs_6_), channel_id=1, source_target_pairs={{0,8},{1,9},{2,10},{3,11},{4,12},{5,13},{6,14},{7,15},{8,0},{9,1},... | collective-permute-start | bytes 2506760 | tf_op jit(solution)/shard_map/ppermute | solution.py:424
  98.9 14.2 %collective-permute-start.16 = (bf16[272,1536]{1,0:T(8,128)(2,1)}, bf16[272,1536]{1,0:T(8,128)(2,1)S(1)}, u32[]{:S(2)}, u32[]{:S(2)}) collective-permute-start(bf16[272,1536]{1,0:T(8,128)(2,1)} %collective-permute-done.5.refs_3_.refs_7_), channel_id=1, source_target_pairs={{0,8},{1,9},{2,10},{3,11},{4,12},{5,13},{6,14},{7,15},{8,0},{9,1},... | collective-permute-start | bytes 2506760 | tf_op jit(solution)/shard_map/ppermute | solution.py:424
  98.9 15.5 %collective-permute-start.17 = (bf16[272,1536]{1,0:T(8,128)(2,1)}, bf16[272,1536]{1,0:T(8,128)(2,1)S(1)}, u32[]{:S(2)}, u32[]{:S(2)}) collective-permute-start(bf16[272,1536]{1,0:T(8,128)(2,1)} %collective-permute-done.6.refs_4_.refs_8_), channel_id=1, source_target_pairs={{0,8},{1,9},{2,10},{3,11},{4,12},{5,13},{6,14},{7,15},{8,0},{9,1},... | collective-permute-start | bytes 2506760 | tf_op jit(solution)/shard_map/ppermute | solution.py:424
  110.9 37.9 %collective-permute-start.10 = (bf16[272,1536]{1,0:T(8,128)(2,1)}, bf16[272,1536]{1,0:T(8,128)(2,1)S(1)}, u32[]{:S(2)}, u32[]{:S(2)}) collective-permute-start(bf16[272,1536]{1,0:T(8,128)(2,1)} %get-tuple-element.49), channel_id=1, source_target_pairs={{0,16},{1,17},{2,18},{3,19},{4,20},{5,21},{6,22},{7,23},{8,24},{9,... | collective-permute-start | bytes 2506760 | tf_op jit(solution)/shard_map/ppermute | solution.py:424
  112.2 36.9 %collective-permute-start.11 = (bf16[272,1536]{1,0:T(8,128)(2,1)}, bf16[272,1536]{1,0:T(8,128)(2,1)S(1)}, u32[]{:S(2)}, u32[]{:S(2)}) collective-permute-start(bf16[272,1536]{1,0:T(8,128)(2,1)} %get-tuple-element.50), channel_id=1, source_target_pairs={{0,1},{1,0},{2,3},{3,2},{4,5},{5,4},{6,7},{7,6},{8,9},{9,8},{10,11... | collective-permute-start | bytes 2506760 | tf_op jit(solution)/shard_map/ppermute | solution.py:424
  113.1 37.6 %collective-permute-start.12 = (bf16[272,1536]{1,0:T(8,128)(2,1)}, bf16[272,1536]{1,0:T(8,128)(2,1)S(1)}, u32[]{:S(2)}, u32[]{:S(2)}) collective-permute-start(bf16[272,1536]{1,0:T(8,128)(2,1)} %get-tuple-element.51), channel_id=1, source_target_pairs={{0,17},{1,16},{2,19},{3,18},{4,21},{5,20},{6,23},{7,22},{8,25},{9,... | collective-permute-start | bytes 2506760 | tf_op jit(solution)/shard_map/ppermute | solution.py:424
  134.6 39.3 %collective-permute-start.22 = (bf16[256,1536]{1,0:T(8,128)(2,1)}, bf16[256,1536]{1,0:T(8,128)(2,1)S(1)}, u32[]{:S(2)}, u32[]{:S(2)}) collective-permute-start(bf16[256,1536]{1,0:T(8,128)(2,1)} %get-tuple-element.65), channel_id=1, source_target_pairs={{0,2},{1,3},{2,0},{3,1},{4,6},{5,7},{6,4},{7,5},{8,10},{9,11},{10,... | collective-permute-start | bytes 2359304 | tf_op jit(solution)/shard_map/ppermute | solution.py:424
  137.4 51.9 %collective-permute-start.23 = (bf16[256,1536]{1,0:T(8,128)(2,1)}, bf16[256,1536]{1,0:T(8,128)(2,1)S(1)}, u32[]{:S(2)}, u32[]{:S(2)}) collective-permute-start(bf16[256,1536]{1,0:T(8,128)(2,1)} %get-tuple-element.66), channel_id=1, source_target_pairs={{0,2},{1,3},{2,0},{3,1},{4,6},{5,7},{6,4},{7,5},{8,10},{9,11},{10,... | collective-permute-start | bytes 2359304 | tf_op jit(solution)/shard_map/ppermute | solution.py:424
  151.2 39.4 %collective-permute-start.21 = (bf16[272,1536]{1,0:T(8,128)(2,1)S(1)}, bf16[272,1536]{1,0:T(8,128)(2,1)S(1)}, u32[]{:S(2)}, u32[]{:S(2)}) collective-permute-start(bf16[272,1536]{1,0:T(8,128)(2,1)S(1)} %pad_maximum_fusion.3), channel_id=1, source_target_pairs={{0,4},{1,5},{2,6},{3,7},{4,0},{5,1},{6,2},{7,3},{8,12},{9,13},{10,... | collective-permute-start | bytes 2506760 | tf_op jit(solution)/shard_map/ppermute | solution.py:424
  153.9 36.8 %collective-permute-start.20 = (bf16[272,1536]{1,0:T(8,128)(2,1)S(1)}, bf16[272,1536]{1,0:T(8,128)(2,1)S(1)}, u32[]{:S(2)}, u32[]{:S(2)}) collective-permute-start(bf16[272,1536]{1,0:T(8,128)(2,1)S(1)} %copy-done.16), channel_id=1, source_target_pairs={{0,17},{1,16},{2,19},{3,18},{4,21},{5,20},{6,23},{7,22},{8,25},{9,... | collective-permute-start | bytes 2506760 | tf_op jit(solution)/shard_map/ppermute | solution.py:424
  155.6 36.4 %collective-permute-start.19 = (bf16[272,1536]{1,0:T(8,128)(2,1)S(1)}, bf16[272,1536]{1,0:T(8,128)(2,1)S(1)}, u32[]{:S(2)}, u32[]{:S(2)}) collective-permute-start(bf16[272,1536]{1,0:T(8,128)(2,1)S(1)} %copy-done.15), channel_id=1, source_target_pairs={{0,1},{1,0},{2,3},{3,2},{4,5},{5,4},{6,7},{7,6},{8,9},{9,8},{10,11... | collective-permute-start | bytes 2506760 | tf_op jit(solution)/shard_map/ppermute | solution.py:424
  173.9 18.1 %collective-permute-start.18 = (bf16[272,1536]{1,0:T(8,128)(2,1)S(1)}, bf16[272,1536]{1,0:T(8,128)(2,1)S(1)}, u32[]{:S(2)}, u32[]{:S(2)}) collective-permute-start(bf16[272,1536]{1,0:T(8,128)(2,1)S(1)} %copy-done.14), channel_id=1, source_target_pairs={{0,16},{1,17},{2,18},{3,19},{4,20},{5,21},{6,22},{7,23},{8,24},{9,... | collective-permute-start | bytes 2506760 | tf_op jit(solution)/shard_map/ppermute | solution.py:424
  (21 other events, 307.2 us)

commit v4 on v3

--- a/solution.py
+++ b/solution.py
@@ -43,6 +43,21 @@
         copy.start()
         self.all.append(copy)
         return copy
+
+    def pair(self, sources, target):
+        hidden = target.shape[0] // 2
+        return Both(
+            [self.start(sources[k], target.at[pl.ds(k * hidden, hidden)]) for k in range(2)]
+        )
+
+
+class Both:
+    def __init__(self, copies):
+        self.copies = copies
+
+    def wait(self):
+        for copy in self.copies:
+            copy.wait()
 
 
 def hidden_part(tok, grad, weight, scale, act_ref, hid_ref, columns):
@@ -69,14 +84,14 @@
     count, rows = plan
     refs = list(refs)
     take = lambda number: [refs.pop(0) for _ in range(number)]
-    (first_ref,), pieces, weights_in = take(1), take(count), take(4)
+    (first_ref,), pieces, weights_in = take(1), take(count), [take(2) for _ in range(4)]
     (act_out, hid_out), pieces_out = take(2), take(count)
     (tok, grad, coded_rows, extra), values = take(4), take(2)
     weights, stages, (sems_in, sems_out) = take(4), take(2), take(2)
     hidden = weights[0].shape[0] // 2
     tile = 2 * rows
     loads, stores = Copies(sems_in), Copies(sems_out)
-    weight_ready, ready = [loads.start(weights_in[0], weights[0])], []
+    weight_ready, ready = [loads.pair(weights_in[0], weights[0])], []
 
     def load_tile(t):
         group = []
@@ -90,7 +105,7 @@
 
     load_tile(0)
     for i in range(1, 4):
-        weight_ready.append(loads.start(weights_in[i], weights[i]))
+        weight_ready.append(loads.pair(weights_in[i], weights[i]))
     for t in range(1, count // 2):
         load_tile(t)
     first = first_ref[0]
@@ -192,7 +207,8 @@
     take = lambda number: [refs.pop(0) for _ in range(number)]
     (first_ref,), near, far, (near_over,) = take(1), take(count), take(count), take(1)
     far_over, far_values = take(count), take(2)
-    weights_in, near_values, keep_out, near_sums, (score,) = take(2), take(2), take(2), take(2), take(1)
+    weights_in, near_values = [take(2) for _ in range(2)], take(2)
+    keep_out, near_sums, (score,) = take(2), take(2), take(1)
     tok, grad, coded_rows, acts, hids, totals, results = take(7)
     weights, (sems_in, sems_out) = take(2), take(2)
     group = 4
@@ -216,9 +232,9 @@
                 started.append(loads.start(source, target.at[n % 2]))
         return started
 
-    weight_ready = [loads.start(weights_in[0], weights[0])]
+    weight_ready = [loads.pair(weights_in[0], weights[0])]
     ready = load(0)
-    weight_ready.append(loads.start(weights_in[1], weights[1]))
+    weight_ready.append(loads.pair(weights_in[1], weights[1]))
     first = first_ref[0]
     saved = [[], []]
     for n, (kind, g, blocks) in enumerate(steps):
@@ -260,7 +276,8 @@
     count, rows = plan
     refs = list(refs)
     take = lambda number: [refs.pop(0) for _ in range(number)]
-    (first_ref, score), near, values_in, weights_in = take(2), take(count), take(2), take(4)
+    (first_ref, score), near, values_in = take(2), take(count), take(2)
+    weights_in = [take(2) for _ in range(4)]
     pieces_out = take(count)
     tok, grad, coded_rows, extra, acts, hids, others, outs = take(8)
     weights, (sems_in, sems_out) = take(4), take(2)
@@ -276,10 +293,10 @@
             started.append(loads.start(source.at[span], target.at[g % 2]))
         return started
 
-    weight_ready = {2: loads.start(weights_in[2], weights[2])}
+    weight_ready = {2: loads.pair(weights_in[2], weights[2])}
     ready = load(0)
     for i in (3, 0, 1):
-        weight_ready[i] = loads.start(weights_in[i], weights[i])
+        weight_ready[i] = loads.pair(weights_in[i], weights[i])
     first = first_ref[0]
     extra[...] = jnp.zeros_like(extra)
     out_copies = []
@@ -334,7 +351,7 @@
 
 def far_call(rows, first, pieces, weights):
     count, features = len(pieces), pieces[0].shape[1]
-    hidden = weights[0].shape[0] // 2
+    hidden = weights[0][0].shape[0]
     height = count * rows
     bf = jnp.bfloat16
     shape = jax.ShapeDtypeStruct
@@ -342,7 +359,7 @@
         functools.partial(far_kernel, (count, rows)),
         out_shape=[shape((height, 2 * hidden), bf)] * 2
         + [shape((2 * rows + SPARE, features), bf)] * count,
-        in_specs=[IN_SMEM] + [ANYWHERE] * (count + 4),
+        in_specs=[IN_SMEM] + [ANYWHERE] * (count + 8),
         out_specs=[ANYWHERE] * (2 + count),
         scratch_shapes=[pltpu.VMEM((height, features), bf)] * 2
         + [pltpu.VMEM((count, SPARE, 2 * rows), bf)]
@@ -350,15 +367,15 @@
         + [pltpu.VMEM((height, 4 * hidden), bf)] * 2
         + [pltpu.VMEM((2 * hidden, features), bf)] * 4
         + [pltpu.VMEM((2, 2 * rows, features), bf)] * 2
-        + [pltpu.SemaphoreType.DMA((3 * count + 4,)), pltpu.SemaphoreType.DMA((4 * count,))],
+        + [pltpu.SemaphoreType.DMA((3 * count + 8,)), pltpu.SemaphoreType.DMA((4 * count,))],
         **kernel_params(),
-    )(first, *pieces, *weights)
+    )(first, *pieces, *sum(weights, ()))
     return outs[:2], outs[2:]
 
 
 def sums_call(rows, first, near, far, near_over, far_over, far_values, weights):
     count, features = len(near), near[0].shape[1]
-    hidden = weights[0].shape[0] // 2
+    hidden = weights[0][0].shape[0]
     height, tile = count * rows, 4 * rows
     bf, f32 = jnp.bfloat16, jnp.float32
     shape = jax.ShapeDtypeStruct
@@ -368,7 +385,7 @@
         + [shape((hidden, features), f32)] * 2
         + [shape((hidden, features), bf)] * 2
         + [shape((height, SPARE), f32)],
-        in_specs=[IN_SMEM] + [ANYWHERE] * (3 * count + 5),
+        in_specs=[IN_SMEM] + [ANYWHERE] * (3 * count + 7),
         out_specs=[ANYWHERE] * 6 + [IN_VMEM],
         scratch_shapes=[pltpu.VMEM((2, tile, features), bf)] * 2
         + [pltpu.VMEM((2, 4, SPARE, 2 * rows), bf)]
@@ -376,21 +393,21 @@
         + [pltpu.VMEM((4, hidden, features), f32)]
         + [pltpu.VMEM((2, hidden, features), bf)]
         + [pltpu.VMEM((2 * hidden, features), bf)] * 2
-        + [pltpu.SemaphoreType.DMA((12 * count + 2,)), pltpu.SemaphoreType.DMA((count + 4,))],
+        + [pltpu.SemaphoreType.DMA((12 * count + 4,)), pltpu.SemaphoreType.DMA((count + 4,))],
         **kernel_params(),
-    )(first, *near, *far, near_over, *far_over, *far_values, *weights)
+    )(first, *near, *far, near_over, *far_over, *far_values, *sum(weights, ()))
     return outs[:2], outs[2:4], outs[4:6], outs[6]
 
 
 def near_call(rows, first, score, near, values, weights):
     count, features = len(near), near[0].shape[1]
-    hidden = weights[0].shape[0] // 2
+    hidden = weights[0][0].shape[0]
     tile = 4 * rows
     bf = jnp.bfloat16
     return pl.pallas_call(
         functools.partial(near_kernel, (count, rows)),
         out_shape=[jax.ShapeDtypeStruct((2 * rows + SPARE, features), bf)] * count,
-        in_specs=[IN_SMEM, IN_VMEM] + [ANYWHERE] * (count + 6),
+        in_specs=[IN_SMEM, IN_VMEM] + [ANYWHERE] * (count + 10),
         out_specs=[ANYWHERE] * count,
         scratch_shapes=[pltpu.VMEM((2, tile, features), bf)] * 2
         + [pltpu.VMEM((2, 4, SPARE, 2 * rows), bf)]
@@ -398,9 +415,9 @@
         + [pltpu.VMEM((2, tile, 2 * hidden), bf)] * 3
         + [pltpu.VMEM((2, tile, features), bf)]
         + [pltpu.VMEM((2 * hidden, features), bf)] * 4
-        + [pltpu.SemaphoreType.DMA((4 * count + 4,)), pltpu.SemaphoreType.DMA((3 * count,))],
+        + [pltpu.SemaphoreType.DMA((4 * count + 8,)), pltpu.SemaphoreType.DMA((3 * count,))],
         **kernel_params(1000),
-    )(first, score, *near, *values, *weights)
+    )(first, score, *near, *values, *sum(weights, ()))
 
 
 def coded(rows_of, features):
@@ -479,16 +496,15 @@
 
     own = jnp.concatenate([tokens, grad_y, coded(gate_rows, features)], axis=0)
     far = grid.swap_far(own)
-    own_weights = jnp.concatenate([w_in[0], w_out[0]], axis=0)
-    near_weights = grid.swap_near(own_weights)
+    own_pair = (w_in[0], w_out[0])
     near_pieces = [grid.spread(own, *step) for step in steps]
-    near_pieces, far, core_weights = tie(near_pieces, far, own_weights)
+    near_pieces, far, after_far = tie(near_pieces, far, own_pair)
+    near_pair = tuple(grid.swap_near(part) for part in after_far)
     far_pieces = [grid.spread(far, *step) for step in steps]
     near_over = grid.swap_core(jnp.concatenate(near_pieces, axis=0))
-    other_own = grid.swap_core(core_weights)
-    far_pieces, other_own = tie(far_pieces, other_own)
-    other_near = grid.swap_core(near_weights)
-    weights = [own_weights, near_weights, other_own, other_near]
+    other_own = tuple(grid.swap_core(part) for part in own_pair)
+    other_near = tuple(grid.swap_core(part) for part in near_pair)
+    weights = [own_pair, near_pair, other_own, other_near]
     far_values, far_out = far_call(rows, first, far_pieces, weights)
 
     far_home = [grid.collect(part, *step) for part, step in zip(far_out, steps)]

time: 194 us -> 183 us (0.943)
  waiting for transfers between devices: 111 us -> 102 us
  other arithmetic: 11.6 us -> 8.21 us
    ppermute x24 -> x27, waiting for transfers between devices: 111 us -> 102 us  [move(): return lax.ppermute(array, AXES, pairs)]
    concatenate x1, other arithmetic: 5.69 us -> 1.92 us  [shards(): near_over = grid.swap_core(jnp.concatenate(near_pieces, axis=0))]
    ppermute x24 -> x27, starting transfers between devices: 26.3 us -> 27.8 us  [move(): return lax.ppermute(array, AXES, pairs)]
  transfers between devices with their start and end apart: 24 -> 27, of which waited for: 11 -> 11; matrix products, arithmetic and copies ran while one was open for 5% -> 3% of each run, Pallas kernels for 22% -> 23%
where the time goes in v4:
time: 183 us
  waiting for transfers between devices  102 us (56%)
  Pallas kernels  42.2 us (23%)
  starting transfers between devices  27.8 us (15%)
  other arithmetic  8.21 us (4%)
  local copies, waits for them, and re-layouts  1.97 us (1%)
    ppermute x27, waiting for transfers between devices, move(): return lax.ppermute(array, AXES, pairs)  102 us
    ppermute x27, starting transfers between devices, move(): return lax.ppermute(array, AXES, pairs)  27.8 us
    pallas_call x1, Pallas kernels, sums_call(): pl.pallas_call(functools.partial(sums_kernel, (count, rows)), out_shape=[...  19.1 us
    pallas_call x1, Pallas kernels, far_call(): pl.pallas_call(functools.partial(far_kernel, (count, rows)), out_shape=[s...  11.6 us
    pallas_call x1, Pallas kernels, near_call(): pl.pallas_call(functools.partial(near_kernel, (count, rows)), out_shape=[...  11.4 us
  transfers between devices with their start and end apart: 27, of which 11 were waited for; matrix products, arithmetic and copies ran while one was open for 3% of the time, Pallas kernels for 23%

profile of v4, /device:TPU:0, one launch (start us, length us, event | category | flops | bytes accessed | tf_op | source)
XLA Modules:
  0.0 183.2 jit_solution(6863070372722883711)
XLA Ops:
  2.7 3.0 %collective-permute-start = (bf16[272,1536]{1,0:T(8,128)(2,1)S(1)}, bf16[272,1536]{1,0:T(8,128)(2,1)S(1)}, u32[]{:S(2)}, u32[]{:S(2)}) collective-permute-start(bf16[272,1536]{1,0:T(8,128)(2,1)S(1)} %pad_maximum_fusion.1.refs_1_.refs_2_), channel_id=1, source_target_pairs={{0,16},{1,17},{2,18},{3,19},{4,20},{5,21},{6,22},{7,23},{8,24},{9,... | collective-permute-start | bytes 2506760 | tf_op jit(solution)/shard_map/ppermute | solution.py:441
  5.7 1.5 collective-permute-start.1
  7.2 3.0 %collective-permute-start.3 = (bf16[272,1536]{1,0:T(8,128)(2,1)S(1)}, bf16[272,1536]{1,0:T(8,128)(2,1)}, u32[]{:S(2)}, u32[]{:S(2)}) collective-permute-start(bf16[272,1536]{1,0:T(8,128)(2,1)S(1)} %pad_maximum_fusion.1.refs_1_.refs_2_), channel_id=1, source_target_pairs={{0,4},{1,5},{2,6},{3,7},{4,0},{5,1},{6,2},{7,3},{8,12},{9,13},{10,... | collective-permute-start | bytes 2506760 | tf_op jit(solution)/shard_map/ppermute | solution.py:441
  10.3 14.8 %collective-permute-done.refs_2_.refs_3_ = bf16[272,1536]{1,0:T(8,128)(2,1)S(1)} collective-permute-done((bf16[272,1536]{1,0:T(8,128)(2,1)S(1)}, bf16[272,1536]{1,0:T(8,128)(2,1)S(1)}, u32[]{:S(2)}, u32[]{:S(2)}) %collective-permute-start) | collective-permute-done | bytes 835616 | tf_op jit(solution)/shard_map/ppermute | solution.py:441
  25.1 18.5 %collective-permute-done.1.refs_3_.refs_4_ = bf16[272,1536]{1,0:T(8,128)(2,1)S(1)} collective-permute-done((bf16[272,1536]{1,0:T(8,128)(2,1)S(1)}, bf16[272,1536]{1,0:T(8,128)(2,1)S(1)}, u32[]{:S(2)}, u32[]{:S(2)}) %collective-permute-start.1) | collective-permute-done | bytes 835616 | tf_op jit(solution)/shard_map/ppermute | solution.py:441
  43.7 2.4 %collective-permute-done.3.refs_1_.refs_5_ = bf16[272,1536]{1,0:T(8,128)(2,1)} collective-permute-done((bf16[272,1536]{1,0:T(8,128)(2,1)S(1)}, bf16[272,1536]{1,0:T(8,128)(2,1)}, u32[]{:S(2)}, u32[]{:S(2)}) %collective-permute-start.3) | collective-permute-done | bytes 835616 | tf_op jit(solution)/shard_map/ppermute | solution.py:441
  48.1 1.5 collective-permute-start.4
  49.6 1.5 collective-permute-start.5
  51.6 15.1 %collective-permute-done.7.refs_7_.refs_18_.refs_10_ = bf16[256,1536]{1,0:T(8,128)(2,1)} collective-permute-done((bf16[256,1536]{1,0:T(8,128)(2,1)S(1)}, bf16[256,1536]{1,0:T(8,128)(2,1)}, u32[]{:S(2)}, u32[]{:S(2)}) %collective-permute-start.7) | collective-permute-done | bytes 786464 | tf_op jit(solution)/shard_map/ppermute | solution.py:441
  66.6 14.7 %collective-permute-done.8.refs_8_.refs_19_.refs_11_ = bf16[256,1536]{1,0:T(8,128)(2,1)} collective-permute-done((bf16[256,1536]{1,0:T(8,128)(2,1)S(1)}, bf16[256,1536]{1,0:T(8,128)(2,1)}, u32[]{:S(2)}, u32[]{:S(2)}) %collective-permute-start.8) | collective-permute-done | bytes 786464 | tf_op jit(solution)/shard_map/ppermute | solution.py:441
  81.4 1.9 %pad_maximum_fusion = bf16[1088,1536]{1,0:T(8,128)(2,1)} fusion(bf16[272,1536]{1,0:T(8,128)(2,1)S(1)} %collective-permute-done.2.refs_4_.refs_5_, bf16[272,1536]{1,0:T(8,128)(2,1)S(1)} %collective-permute-done.1.refs_3_.refs_4_, bf16[272,1536]{1,0:T(8,128)(2,1)S(1)} %collective-permute-done.refs_2_.refs_3_, ...), kind=kLoop, calls=%fused_computation | loop fusion | flops 13369344 | bytes 6684672 | tf_op jit(solution)/shard_map/concatenate | solution.py:504
  83.8 2.6 %collective-permute-done.5.refs_3_.refs_7_ = bf16[272,1536]{1,0:T(8,128)(2,1)} collective-permute-done((bf16[272,1536]{1,0:T(8,128)(2,1)}, bf16[272,1536]{1,0:T(8,128)(2,1)}, u32[]{:S(2)}, u32[]{:S(2)}) %collective-permute-start.5) | collective-permute-done | bytes 835616 | tf_op jit(solution)/shard_map/ppermute | solution.py:441
  87.5 11.6 %shard_map.101 = (bf16[512,512]{1,0:T(8,128)(2,1)}, bf16[512,512]{1,0:T(8,128)(2,1)}, bf16[272,1536]{1,0:T(8,128)(2,1)}, bf16[272,1536]{1,0:T(8,128)(2,1)}, bf16...) custom-call(s32[1]{0:T(128)} %bitcast.refs_0_, bf16[272,1536]{1,0:T(8,128)(2,1)} %collective-permute-done.3.refs_1_.refs_5_, ...), custom_call_target="tpu_custom_call" | custom-call | flops 99999997952 | bytes 100000000 | tf_op jit(solution)/shard_map/pallas_call | solution.py:358
  101.3 1.4 collective-permute-start.15
  103.6 19.1 %shard_map.102 = (bf16[512,512]{1,0:T(8,128)(2,1)}, bf16[512,512]{1,0:T(8,128)(2,1)}, f32[256,1536]{1,0:T(8,128)}, f32[256,1536]{1,0:T(8,128)}, bf16[256,1536]{1...) custom-call(s32[1]{0:T(128)} %bitcast.refs_0_, bf16[272,1536]{1,0:T(8,128)(2,1)} %copy-done, ...), custom_call_target="tpu_custom_call" | custom-call | flops 99999997952 | bytes 100000000 | tf_op jit(solution)/shard_map/pallas_call | solution.py:382
  122.7 1.7 collective-permute-start.25
  124.8 11.4 %shard_map.103 = (bf16[272,1536]{1,0:T(8,128)(2,1)}, bf16[272,1536]{1,0:T(8,128)(2,1)}, bf16[272,1536]{1,0:T(8,128)(2,1)}, bf16[272,1536]{1,0:T(8,128)(2,1)}) custom-call(s32[1]{0:T(128)} %bitcast.refs_0_, f32[512,16]{1,0:T(8,128)} %get-tuple-element.50.refs_1_, bf16[272,1536]{1,0:T(8,128)(2,1)} %copy-done, bf16[272,1536]{1,0:T(8,128)(2,1)} %copy-done.1, ...), custom_call_target="tpu_custom_call" | custom-call | flops 1000 | bytes 1 | tf_op jit(solution)/shard_map/pallas_call | solution.py:407
  137.3 1.5 collective-permute-done.15
  139.5 3.5 %collective-permute-start.24 = (bf16[272,1536]{1,0:T(8,128)(2,1)S(1)}, bf16[272,1536]{1,0:T(8,128)(2,1)S(1)}, u32[]{:S(2)}, u32[]{:S(2)}) collective-permute-start(bf16[272,1536]{1,0:T(8,128)(2,1)S(1)} %pad_maximum_fusion.2), channel_id=1, source_target_pairs={{0,4},{1,5},{2,6},{3,7},{4,0},{5,1},{6,2},{7,3},{8,12},{9,13},{10,... | collective-permute-start | bytes 2506760 | tf_op jit(solution)/shard_map/ppermute | solution.py:441
  142.9 1.8 collective-permute-start.23
  145.2 15.3 %collective-permute-done.25 = bf16[256,1536]{1,0:T(8,128)(2,1)S(1)} collective-permute-done((bf16[256,1536]{1,0:T(8,128)(2,1)}, bf16[256,1536]{1,0:T(8,128)(2,1)S(1)}, u32[]{:S(2)}, u32[]{:S(2)}) %collective-permute-start.25) | collective-permute-done | bytes 786464 | tf_op jit(solution)/shard_map/ppermute | solution.py:441
  160.5 1.7 collective-permute-start.21
  163.6 12.9 %collective-permute-done.26 = bf16[256,1536]{1,0:T(8,128)(2,1)S(1)} collective-permute-done((bf16[256,1536]{1,0:T(8,128)(2,1)}, bf16[256,1536]{1,0:T(8,128)(2,1)S(1)}, u32[]{:S(2)}, u32[]{:S(2)}) %collective-permute-start.26) | collective-permute-done | bytes 786464 | tf_op jit(solution)/shard_map/ppermute | solution.py:441
  177.8 3.3 %collective-permute-done.22 = bf16[272,1536]{1,0:T(8,128)(2,1)S(1)} collective-permute-done((bf16[272,1536]{1,0:T(8,128)(2,1)S(1)}, bf16[272,1536]{1,0:T(8,128)(2,1)S(1)}, u32[]{:S(2)}, u32[]{:S(2)}) %collective-permute-start.22) | collective-permute-done | bytes 835616 | tf_op jit(solution)/shard_map/ppermute | solution.py:441
  (90 shorter events, 16.4 us)
Async XLA Ops:
  2.7 22.4 %collective-permute-start = (bf16[272,1536]{1,0:T(8,128)(2,1)S(1)}, bf16[272,1536]{1,0:T(8,128)(2,1)S(1)}, u32[]{:S(2)}, u32[]{:S(2)}) collective-permute-start(bf16[272,1536]{1,0:T(8,128)(2,1)S(1)} %pad_maximum_fusion.1.refs_1_.refs_2_), channel_id=1, source_target_pairs={{0,16},{1,17},{2,18},{3,19},{4,20},{5,21},{6,22},{7,23},{8,24},{9,... | collective-permute-start | bytes 2506760 | tf_op jit(solution)/shard_map/ppermute | solution.py:441
  5.7 38.0 %collective-permute-start.1 = (bf16[272,1536]{1,0:T(8,128)(2,1)S(1)}, bf16[272,1536]{1,0:T(8,128)(2,1)S(1)}, u32[]{:S(2)}, u32[]{:S(2)}) collective-permute-start(bf16[272,1536]{1,0:T(8,128)(2,1)S(1)} %pad_maximum_fusion.1.refs_1_.refs_2_), channel_id=1, source_target_pairs={{0,1},{1,0},{2,3},{3,2},{4,5},{5,4},{6,7},{7,6},{8,9},{9,8},{10,11... | collective-permute-start | bytes 2506760 | tf_op jit(solution)/shard_map/ppermute | solution.py:441
  7.2 36.4 %collective-permute-start.2 = (bf16[272,1536]{1,0:T(8,128)(2,1)S(1)}, bf16[272,1536]{1,0:T(8,128)(2,1)S(1)}, u32[]{:S(2)}, u32[]{:S(2)}) collective-permute-start(bf16[272,1536]{1,0:T(8,128)(2,1)S(1)} %pad_maximum_fusion.1.refs_1_.refs_2_), channel_id=1, source_target_pairs={{0,17},{1,16},{2,19},{3,18},{4,21},{5,20},{6,23},{7,22},{8,25},{9,... | collective-permute-start | bytes 2506760 | tf_op jit(solution)/shard_map/ppermute | solution.py:441
  7.2 38.8 %collective-permute-start.3 = (bf16[272,1536]{1,0:T(8,128)(2,1)S(1)}, bf16[272,1536]{1,0:T(8,128)(2,1)}, u32[]{:S(2)}, u32[]{:S(2)}) collective-permute-start(bf16[272,1536]{1,0:T(8,128)(2,1)S(1)} %pad_maximum_fusion.1.refs_1_.refs_2_), channel_id=1, source_target_pairs={{0,4},{1,5},{2,6},{3,7},{4,0},{5,1},{6,2},{7,3},{8,12},{9,13},{10,... | collective-permute-start | bytes 2506760 | tf_op jit(solution)/shard_map/ppermute | solution.py:441
  10.3 39.3 %collective-permute-start.9 = (bf16[256,1536]{1,0:T(8,128)(2,1)S(1)}, bf16[256,1536]{1,0:T(8,128)(2,1)S(1)}, u32[]{:S(2)}, u32[]{:S(2)}) collective-permute-start(bf16[256,1536]{1,0:T(8,128)(2,1)S(1)} %bitcast.13), channel_id=1, source_target_pairs={{0,8},{1,9},{2,10},{3,11},{4,12},{5,13},{6,14},{7,15},{8,0},{9,1},... | collective-permute-start | bytes 2359304 | tf_op jit(solution)/shard_map/ppermute | solution.py:441
  25.1 26.0 %collective-permute-start.10 = (bf16[256,1536]{1,0:T(8,128)(2,1)S(1)}, bf16[256,1536]{1,0:T(8,128)(2,1)S(1)}, u32[]{:S(2)}, u32[]{:S(2)}) collective-permute-start(bf16[256,1536]{1,0:T(8,128)(2,1)S(1)} %bitcast.18), channel_id=1, source_target_pairs={{0,8},{1,9},{2,10},{3,11},{4,12},{5,13},{6,14},{7,15},{8,0},{9,1},... | collective-permute-start | bytes 2359304 | tf_op jit(solution)/shard_map/ppermute | solution.py:441
  46.0 20.6 %collective-permute-start.7 = (bf16[256,1536]{1,0:T(8,128)(2,1)S(1)}, bf16[256,1536]{1,0:T(8,128)(2,1)}, u32[]{:S(2)}, u32[]{:S(2)}) collective-permute-start(bf16[256,1536]{1,0:T(8,128)(2,1)S(1)} %bitcast.14), channel_id=1, source_target_pairs={{0,2},{1,3},{2,0},{3,1},{4,6},{5,7},{6,4},{7,5},{8,10},{9,11},{10,... | collective-permute-start | bytes 2359304 | tf_op jit(solution)/shard_map/ppermute | solution.py:441
  46.7 34.7 %collective-permute-start.8 = (bf16[256,1536]{1,0:T(8,128)(2,1)S(1)}, bf16[256,1536]{1,0:T(8,128)(2,1)}, u32[]{:S(2)}, u32[]{:S(2)}) collective-permute-start(bf16[256,1536]{1,0:T(8,128)(2,1)S(1)} %bitcast.19), channel_id=1, source_target_pairs={{0,2},{1,3},{2,0},{3,1},{4,6},{5,7},{6,4},{7,5},{8,10},{9,11},{10,... | collective-permute-start | bytes 2359304 | tf_op jit(solution)/shard_map/ppermute | solution.py:441
  48.1 35.2 %collective-permute-start.4 = (bf16[272,1536]{1,0:T(8,128)(2,1)}, bf16[272,1536]{1,0:T(8,128)(2,1)}, u32[]{:S(2)}, u32[]{:S(2)}) collective-permute-start(bf16[272,1536]{1,0:T(8,128)(2,1)} %collective-permute-done.3.refs_1_.refs_5_), channel_id=1, source_target_pairs={{0,16},{1,17},{2,18},{3,19},{4,20},{5,21},{6,22},{7,23},{8,24},{9,... | collective-permute-start | bytes 2506760 | tf_op jit(solution)/shard_map/ppermute | solution.py:441
  49.6 36.8 %collective-permute-start.5 = (bf16[272,1536]{1,0:T(8,128)(2,1)}, bf16[272,1536]{1,0:T(8,128)(2,1)}, u32[]{:S(2)}, u32[]{:S(2)}) collective-permute-start(bf16[272,1536]{1,0:T(8,128)(2,1)} %collective-permute-done.3.refs_1_.refs_5_), channel_id=1, source_target_pairs={{0,1},{1,0},{2,3},{3,2},{4,5},{5,4},{6,7},{7,6},{8,9},{9,8},{10,11... | collective-permute-start | bytes 2506760 | tf_op jit(solution)/shard_map/ppermute | solution.py:441
  51.1 35.3 %collective-permute-start.6 = (bf16[272,1536]{1,0:T(8,128)(2,1)}, bf16[272,1536]{1,0:T(8,128)(2,1)}, u32[]{:S(2)}, u32[]{:S(2)}) collective-permute-start(bf16[272,1536]{1,0:T(8,128)(2,1)} %collective-permute-done.3.refs_1_.refs_5_), channel_id=1, source_target_pairs={{0,17},{1,16},{2,19},{3,18},{4,21},{5,20},{6,23},{7,22},{8,25},{9,... | collective-permute-start | bytes 2506760 | tf_op jit(solution)/shard_map/ppermute | solution.py:441
  66.6 20.3 %collective-permute-start.11 = (bf16[256,1536]{1,0:T(8,128)(2,1)}, bf16[256,1536]{1,0:T(8,128)(2,1)}, u32[]{:S(2)}, u32[]{:S(2)}) collective-permute-start(bf16[256,1536]{1,0:T(8,128)(2,1)} %collective-permute-done.7.refs_7_.refs_18_.refs_10_), channel_id=1, source_target_pairs={{0,8},{1,9},{2,10},{3,11},{4,12},{5,13},{6,14},{7,15},{8,0},{9,1},... | collective-permute-start | bytes 2359304 | tf_op jit(solution)/shard_map/ppermute | solution.py:441
  83.3 15.8 %collective-permute-start.17 = (bf16[272,1536]{1,0:T(8,128)(2,1)}, bf16[272,1536]{1,0:T(8,128)(2,1)S(1)}, u32[]{:S(2)}, u32[]{:S(2)}) collective-permute-start(bf16[272,1536]{1,0:T(8,128)(2,1)} %collective-permute-done.3.refs_1_.refs_5_), channel_id=1, source_target_pairs={{0,8},{1,9},{2,10},{3,11},{4,12},{5,13},{6,14},{7,15},{8,0},{9,1},... | collective-permute-start | bytes 2506760 | tf_op jit(solution)/shard_map/ppermute | solution.py:441
  86.4 16.3 %collective-permute-start.16 = (bf16[1088,1536]{1,0:T(8,128)(2,1)}, bf16[1088,1536]{1,0:T(8,128)(2,1)}, u32[]{:S(2)}, u32[]{:S(2)}) collective-permute-start(bf16[1088,1536]{1,0:T(8,128)(2,1)} %pad_maximum_fusion), channel_id=1, source_target_pairs={{0,8},{1,9},{2,10},{3,11},{4,12},{5,13},{6,14},{7,15},{8,0},{9,1},... | collective-permute-start | bytes 10027016 | tf_op jit(solution)/shard_map/ppermute | solution.py:441
  87.0 15.7 %collective-permute-start.20 = (bf16[272,1536]{1,0:T(8,128)(2,1)}, bf16[272,1536]{1,0:T(8,128)(2,1)S(1)}, u32[]{:S(2)}, u32[]{:S(2)}) collective-permute-start(bf16[272,1536]{1,0:T(8,128)(2,1)} %collective-permute-done.6.refs_4_.refs_8_), channel_id=1, source_target_pairs={{0,8},{1,9},{2,10},{3,11},{4,12},{5,13},{6,14},{7,15},{8,0},{9,1},... | collective-permute-start | bytes 2506760 | tf_op jit(solution)/shard_map/ppermute | solution.py:441
  99.1 37.1 %collective-permute-start.13 = (bf16[272,1536]{1,0:T(8,128)(2,1)}, bf16[272,1536]{1,0:T(8,128)(2,1)S(1)}, u32[]{:S(2)}, u32[]{:S(2)}) collective-permute-start(bf16[272,1536]{1,0:T(8,128)(2,1)} %get-tuple-element.41), channel_id=1, source_target_pairs={{0,16},{1,17},{2,18},{3,19},{4,20},{5,21},{6,22},{7,23},{8,24},{9,... | collective-permute-start | bytes 2506760 | tf_op jit(solution)/shard_map/ppermute | solution.py:441
  100.0 37.3 %collective-permute-start.14 = (bf16[272,1536]{1,0:T(8,128)(2,1)}, bf16[272,1536]{1,0:T(8,128)(2,1)S(1)}, u32[]{:S(2)}, u32[]{:S(2)}) collective-permute-start(bf16[272,1536]{1,0:T(8,128)(2,1)} %get-tuple-element.42), channel_id=1, source_target_pairs={{0,1},{1,0},{2,3},{3,2},{4,5},{5,4},{6,7},{7,6},{8,9},{9,8},{10,11... | collective-permute-start | bytes 2506760 | tf_op jit(solution)/shard_map/ppermute | solution.py:441
  101.3 37.6 %collective-permute-start.15 = (bf16[272,1536]{1,0:T(8,128)(2,1)}, bf16[272,1536]{1,0:T(8,128)(2,1)S(1)}, u32[]{:S(2)}, u32[]{:S(2)}) collective-permute-start(bf16[272,1536]{1,0:T(8,128)(2,1)} %get-tuple-element.43), channel_id=1, source_target_pairs={{0,17},{1,16},{2,19},{3,18},{4,21},{5,20},{6,23},{7,22},{8,25},{9,... | collective-permute-start | bytes 2506760 | tf_op jit(solution)/shard_map/ppermute | solution.py:441
  122.7 37.7 %collective-permute-start.25 = (bf16[256,1536]{1,0:T(8,128)(2,1)}, bf16[256,1536]{1,0:T(8,128)(2,1)S(1)}, u32[]{:S(2)}, u32[]{:S(2)}) collective-permute-start(bf16[256,1536]{1,0:T(8,128)(2,1)} %get-tuple-element.57), channel_id=1, source_target_pairs={{0,2},{1,3},{2,0},{3,1},{4,6},{5,7},{6,4},{7,5},{8,10},{9,11},{10,... | collective-permute-start | bytes 2359304 | tf_op jit(solution)/shard_map/ppermute | solution.py:441
  124.5 52.0 %collective-permute-start.26 = (bf16[256,1536]{1,0:T(8,128)(2,1)}, bf16[256,1536]{1,0:T(8,128)(2,1)S(1)}, u32[]{:S(2)}, u32[]{:S(2)}) collective-permute-start(bf16[256,1536]{1,0:T(8,128)(2,1)} %get-tuple-element.58), channel_id=1, source_target_pairs={{0,2},{1,3},{2,0},{3,1},{4,6},{5,7},{6,4},{7,5},{8,10},{9,11},{10,... | collective-permute-start | bytes 2359304 | tf_op jit(solution)/shard_map/ppermute | solution.py:441
  139.5 38.4 %collective-permute-start.24 = (bf16[272,1536]{1,0:T(8,128)(2,1)S(1)}, bf16[272,1536]{1,0:T(8,128)(2,1)S(1)}, u32[]{:S(2)}, u32[]{:S(2)}) collective-permute-start(bf16[272,1536]{1,0:T(8,128)(2,1)S(1)} %pad_maximum_fusion.2), channel_id=1, source_target_pairs={{0,4},{1,5},{2,6},{3,7},{4,0},{5,1},{6,2},{7,3},{8,12},{9,13},{10,... | collective-permute-start | bytes 2506760 | tf_op jit(solution)/shard_map/ppermute | solution.py:441
  142.9 34.9 %collective-permute-start.23 = (bf16[272,1536]{1,0:T(8,128)(2,1)S(1)}, bf16[272,1536]{1,0:T(8,128)(2,1)S(1)}, u32[]{:S(2)}, u32[]{:S(2)}) collective-permute-start(bf16[272,1536]{1,0:T(8,128)(2,1)S(1)} %copy-done.15), channel_id=1, source_target_pairs={{0,17},{1,16},{2,19},{3,18},{4,21},{5,20},{6,23},{7,22},{8,25},{9,... | collective-permute-start | bytes 2506760 | tf_op jit(solution)/shard_map/ppermute | solution.py:441
  144.7 36.5 %collective-permute-start.22 = (bf16[272,1536]{1,0:T(8,128)(2,1)S(1)}, bf16[272,1536]{1,0:T(8,128)(2,1)S(1)}, u32[]{:S(2)}, u32[]{:S(2)}) collective-permute-start(bf16[272,1536]{1,0:T(8,128)(2,1)S(1)} %copy-done.14), channel_id=1, source_target_pairs={{0,1},{1,0},{2,3},{3,2},{4,5},{5,4},{6,7},{7,6},{8,9},{9,8},{10,11... | collective-permute-start | bytes 2506760 | tf_op jit(solution)/shard_map/ppermute | solution.py:441
  160.5 20.7 %collective-permute-start.21 = (bf16[272,1536]{1,0:T(8,128)(2,1)S(1)}, bf16[272,1536]{1,0:T(8,128)(2,1)S(1)}, u32[]{:S(2)}, u32[]{:S(2)}) collective-permute-start(bf16[272,1536]{1,0:T(8,128)(2,1)S(1)} %copy-done.13), channel_id=1, source_target_pairs={{0,16},{1,17},{2,18},{3,19},{4,20},{5,21},{6,22},{7,23},{8,24},{9,... | collective-permute-start | bytes 2506760 | tf_op jit(solution)/shard_map/ppermute | solution.py:441
  (23 other events, 447.9 us)

commit v5 on v4

--- a/solution.py
+++ b/solution.py
@@ -498,8 +498,8 @@
     far = grid.swap_far(own)
     own_pair = (w_in[0], w_out[0])
     near_pieces = [grid.spread(own, *step) for step in steps]
-    near_pieces, far, after_far = tie(near_pieces, far, own_pair)
-    near_pair = tuple(grid.swap_near(part) for part in after_far)
+    near_pieces, far = tie(near_pieces, far)
+    near_pair = tuple(grid.swap_near(part) for part in own_pair)
     far_pieces = [grid.spread(far, *step) for step in steps]
     near_over = grid.swap_core(jnp.concatenate(near_pieces, axis=0))
     other_own = tuple(grid.swap_core(part) for part in own_pair)

time: 183 us -> 180 us (0.984)
  waiting for transfers between devices: 102 us -> 95.2 us
    ppermute x27, waiting for transfers between devices: 102 us -> 95.2 us  [move(): return lax.ppermute(array, AXES, pairs)]
  transfers between devices with their start and end apart: 27 -> 27, of which waited for: 11 -> 11; matrix products, arithmetic and copies ran while one was open for 3% -> 3% of each run, Pallas kernels for 23% -> 24%
where the time goes in v5:
time: 180 us; the launch traced here: 179 us
  waiting for transfers between devices  95.2 us (53%)
  Pallas kernels  42.2 us (23%)
  starting transfers between devices  28.7 us (16%)
  other arithmetic  8.19 us (5%)
  local copies, waits for them, and re-layouts  3.75 us (2%)
    ppermute x27, waiting for transfers between devices, move(): return lax.ppermute(array, AXES, pairs)  95.2 us
    ppermute x27, starting transfers between devices, move(): return lax.ppermute(array, AXES, pairs)  28.7 us
    pallas_call x1, Pallas kernels, sums_call(): pl.pallas_call(functools.partial(sums_kernel, (count, rows)), out_shape=[...  19.1 us
    pallas_call x1, Pallas kernels, far_call(): pl.pallas_call(functools.partial(far_kernel, (count, rows)), out_shape=[s...  11.6 us
    pallas_call x1, Pallas kernels, near_call(): pl.pallas_call(functools.partial(near_kernel, (count, rows)), out_shape=[...  11.4 us
  transfers between devices with their start and end apart: 27, of which 11 were waited for; matrix products, arithmetic and copies ran while one was open for 3% of the time, Pallas kernels for 24%

profile of v5, /device:TPU:0, one launch (start us, length us, event | category | flops | bytes accessed | tf_op | source)
XLA Modules:
  0.0 179.0 jit_solution(1471774381701299709)
XLA Ops:
  2.7 3.0 %collective-permute-start = (bf16[272,1536]{1,0:T(8,128)(2,1)S(1)}, bf16[272,1536]{1,0:T(8,128)(2,1)S(1)}, u32[]{:S(2)}, u32[]{:S(2)}) collective-permute-start(bf16[272,1536]{1,0:T(8,128)(2,1)S(1)} %pad_maximum_fusion.1.refs_1_.refs_2_), channel_id=1, source_target_pairs={{0,16},{1,17},{2,18},{3,19},{4,20},{5,21},{6,22},{7,23},{8,24},{9,... | collective-permute-start | bytes 2506760 | tf_op jit(solution)/shard_map/ppermute | solution.py:441
  5.7 1.5 collective-permute-start.1
  7.2 3.0 %collective-permute-start.3 = (bf16[272,1536]{1,0:T(8,128)(2,1)S(1)}, bf16[272,1536]{1,0:T(8,128)(2,1)}, u32[]{:S(2)}, u32[]{:S(2)}) collective-permute-start(bf16[272,1536]{1,0:T(8,128)(2,1)S(1)} %pad_maximum_fusion.1.refs_1_.refs_2_), channel_id=1, source_target_pairs={{0,4},{1,5},{2,6},{3,7},{4,0},{5,1},{6,2},{7,3},{8,12},{9,13},{10,... | collective-permute-start | bytes 2506760 | tf_op jit(solution)/shard_map/ppermute | solution.py:441
  10.3 1.6 collective-permute-start.7
  11.9 13.3 %collective-permute-done.refs_2_.refs_3_ = bf16[272,1536]{1,0:T(8,128)(2,1)S(1)} collective-permute-done((bf16[272,1536]{1,0:T(8,128)(2,1)S(1)}, bf16[272,1536]{1,0:T(8,128)(2,1)S(1)}, u32[]{:S(2)}, u32[]{:S(2)}) %collective-permute-start) | collective-permute-done | bytes 835616 | tf_op jit(solution)/shard_map/ppermute | solution.py:441
  25.1 2.1 %collective-permute-start.8 = (bf16[256,1536]{1,0:T(8,128)(2,1)S(1)}, bf16[256,1536]{1,0:T(8,128)(2,1)}, u32[]{:S(2)}, u32[]{:S(2)}) collective-permute-start(bf16[256,1536]{1,0:T(8,128)(2,1)S(1)} %bitcast.18), channel_id=1, source_target_pairs={{0,2},{1,3},{2,0},{3,1},{4,6},{5,7},{6,4},{7,5},{8,10},{9,11},{10,... | collective-permute-start | bytes 2359304 | tf_op jit(solution)/shard_map/ppermute | solution.py:441
  27.3 16.4 %collective-permute-done.1.refs_3_.refs_4_ = bf16[272,1536]{1,0:T(8,128)(2,1)S(1)} collective-permute-done((bf16[272,1536]{1,0:T(8,128)(2,1)S(1)}, bf16[272,1536]{1,0:T(8,128)(2,1)S(1)}, u32[]{:S(2)}, u32[]{:S(2)}) %collective-permute-start.1) | collective-permute-done | bytes 835616 | tf_op jit(solution)/shard_map/ppermute | solution.py:441
  44.2 2.0 %collective-permute-done.3.refs_1_.refs_5_ = bf16[272,1536]{1,0:T(8,128)(2,1)} collective-permute-done((bf16[272,1536]{1,0:T(8,128)(2,1)S(1)}, bf16[272,1536]{1,0:T(8,128)(2,1)}, u32[]{:S(2)}, u32[]{:S(2)}) %collective-permute-start.3) | collective-permute-done | bytes 835616 | tf_op jit(solution)/shard_map/ppermute | solution.py:441
  46.1 1.5 collective-permute-start.4
  47.7 1.5 collective-permute-start.5
  49.2 12.9 %collective-permute-done.8.refs_8_.refs_19_.refs_11_ = bf16[256,1536]{1,0:T(8,128)(2,1)} collective-permute-done((bf16[256,1536]{1,0:T(8,128)(2,1)S(1)}, bf16[256,1536]{1,0:T(8,128)(2,1)}, u32[]{:S(2)}, u32[]{:S(2)}) %collective-permute-start.8) | collective-permute-done | bytes 786464 | tf_op jit(solution)/shard_map/ppermute | solution.py:441
  62.1 2.5 %collective-permute-start.6 = (bf16[272,1536]{1,0:T(8,128)(2,1)}, bf16[272,1536]{1,0:T(8,128)(2,1)}, u32[]{:S(2)}, u32[]{:S(2)}) collective-permute-start(bf16[272,1536]{1,0:T(8,128)(2,1)} %collective-permute-done.3.refs_1_.refs_5_), channel_id=1, source_target_pairs={{0,17},{1,16},{2,19},{3,18},{4,21},{5,20},{6,23},{7,22},{8,25},{9,... | collective-permute-start | bytes 2506760 | tf_op jit(solution)/shard_map/ppermute | solution.py:441
  66.4 1.9 %pad_maximum_fusion = bf16[1088,1536]{1,0:T(8,128)(2,1)} fusion(bf16[272,1536]{1,0:T(8,128)(2,1)S(1)} %collective-permute-done.2.refs_4_.refs_5_, bf16[272,1536]{1,0:T(8,128)(2,1)S(1)} %collective-permute-done.1.refs_3_.refs_4_, bf16[272,1536]{1,0:T(8,128)(2,1)S(1)} %collective-permute-done.refs_2_.refs_3_, ...), kind=kLoop, calls=%fused_computation | loop fusion | flops 13369344 | bytes 6684672 | tf_op jit(solution)/shard_map/concatenate | solution.py:504
  69.0 16.0 %collective-permute-done.5.refs_3_.refs_7_ = bf16[272,1536]{1,0:T(8,128)(2,1)} collective-permute-done((bf16[272,1536]{1,0:T(8,128)(2,1)}, bf16[272,1536]{1,0:T(8,128)(2,1)}, u32[]{:S(2)}, u32[]{:S(2)}) %collective-permute-start.5) | collective-permute-done | bytes 835616 | tf_op jit(solution)/shard_map/ppermute | solution.py:441
  85.5 11.6 %shard_map.101 = (bf16[512,512]{1,0:T(8,128)(2,1)}, bf16[512,512]{1,0:T(8,128)(2,1)}, bf16[272,1536]{1,0:T(8,128)(2,1)}, bf16[272,1536]{1,0:T(8,128)(2,1)}, bf16...) custom-call(s32[1]{0:T(128)} %bitcast.refs_0_, bf16[272,1536]{1,0:T(8,128)(2,1)} %collective-permute-done.3.refs_1_.refs_5_, ...), custom_call_target="tpu_custom_call" | custom-call | flops 99999997952 | bytes 100000000 | tf_op jit(solution)/shard_map/pallas_call | solution.py:358
  99.3 1.4 collective-permute-start.15
  101.7 19.1 %shard_map.102 = (bf16[512,512]{1,0:T(8,128)(2,1)}, bf16[512,512]{1,0:T(8,128)(2,1)}, f32[256,1536]{1,0:T(8,128)}, f32[256,1536]{1,0:T(8,128)}, bf16[256,1536]{1...) custom-call(s32[1]{0:T(128)} %bitcast.refs_0_, bf16[272,1536]{1,0:T(8,128)(2,1)} %copy-done, ...), custom_call_target="tpu_custom_call" | custom-call | flops 99999997952 | bytes 100000000 | tf_op jit(solution)/shard_map/pallas_call | solution.py:382
  120.8 1.7 collective-permute-start.25
  122.9 11.4 %shard_map.103 = (bf16[272,1536]{1,0:T(8,128)(2,1)}, bf16[272,1536]{1,0:T(8,128)(2,1)}, bf16[272,1536]{1,0:T(8,128)(2,1)}, bf16[272,1536]{1,0:T(8,128)(2,1)}) custom-call(s32[1]{0:T(128)} %bitcast.refs_0_, f32[512,16]{1,0:T(8,128)} %get-tuple-element.46.refs_1_, bf16[272,1536]{1,0:T(8,128)(2,1)} %copy-done, bf16[272,1536]{1,0:T(8,128)(2,1)} %copy-done.1, ...), custom_call_target="tpu_custom_call" | custom-call | flops 1000 | bytes 1 | tf_op jit(solution)/shard_map/pallas_call | solution.py:407
  135.3 1.5 collective-permute-done.15
  138.6 1.5 collective-permute-start.23
  141.3 18.2 %collective-permute-done.25 = bf16[256,1536]{1,0:T(8,128)(2,1)S(1)} collective-permute-done((bf16[256,1536]{1,0:T(8,128)(2,1)}, bf16[256,1536]{1,0:T(8,128)(2,1)S(1)}, u32[]{:S(2)}, u32[]{:S(2)}) %collective-permute-start.25) | collective-permute-done | bytes 786464 | tf_op jit(solution)/shard_map/ppermute | solution.py:441
  161.6 12.9 %collective-permute-done.26 = bf16[256,1536]{1,0:T(8,128)(2,1)S(1)} collective-permute-done((bf16[256,1536]{1,0:T(8,128)(2,1)}, bf16[256,1536]{1,0:T(8,128)(2,1)S(1)}, u32[]{:S(2)}, u32[]{:S(2)}) %collective-permute-start.26) | collective-permute-done | bytes 786464 | tf_op jit(solution)/shard_map/ppermute | solution.py:441
  174.5 1.4 add_bitcast_fusion
  (90 shorter events, 18.0 us)
Async XLA Ops:
  2.7 22.4 %collective-permute-start = (bf16[272,1536]{1,0:T(8,128)(2,1)S(1)}, bf16[272,1536]{1,0:T(8,128)(2,1)S(1)}, u32[]{:S(2)}, u32[]{:S(2)}) collective-permute-start(bf16[272,1536]{1,0:T(8,128)(2,1)S(1)} %pad_maximum_fusion.1.refs_1_.refs_2_), channel_id=1, source_target_pairs={{0,16},{1,17},{2,18},{3,19},{4,20},{5,21},{6,22},{7,23},{8,24},{9,... | collective-permute-start | bytes 2506760 | tf_op jit(solution)/shard_map/ppermute | solution.py:441
  5.7 38.0 %collective-permute-start.1 = (bf16[272,1536]{1,0:T(8,128)(2,1)S(1)}, bf16[272,1536]{1,0:T(8,128)(2,1)S(1)}, u32[]{:S(2)}, u32[]{:S(2)}) collective-permute-start(bf16[272,1536]{1,0:T(8,128)(2,1)S(1)} %pad_maximum_fusion.1.refs_1_.refs_2_), channel_id=1, source_target_pairs={{0,1},{1,0},{2,3},{3,2},{4,5},{5,4},{6,7},{7,6},{8,9},{9,8},{10,11... | collective-permute-start | bytes 2506760 | tf_op jit(solution)/shard_map/ppermute | solution.py:441
  7.2 36.4 %collective-permute-start.2 = (bf16[272,1536]{1,0:T(8,128)(2,1)S(1)}, bf16[272,1536]{1,0:T(8,128)(2,1)S(1)}, u32[]{:S(2)}, u32[]{:S(2)}) collective-permute-start(bf16[272,1536]{1,0:T(8,128)(2,1)S(1)} %pad_maximum_fusion.1.refs_1_.refs_2_), channel_id=1, source_target_pairs={{0,17},{1,16},{2,19},{3,18},{4,21},{5,20},{6,23},{7,22},{8,25},{9,... | collective-permute-start | bytes 2506760 | tf_op jit(solution)/shard_map/ppermute | solution.py:441
  7.2 38.9 %collective-permute-start.3 = (bf16[272,1536]{1,0:T(8,128)(2,1)S(1)}, bf16[272,1536]{1,0:T(8,128)(2,1)}, u32[]{:S(2)}, u32[]{:S(2)}) collective-permute-start(bf16[272,1536]{1,0:T(8,128)(2,1)S(1)} %pad_maximum_fusion.1.refs_1_.refs_2_), channel_id=1, source_target_pairs={{0,4},{1,5},{2,6},{3,7},{4,0},{5,1},{6,2},{7,3},{8,12},{9,13},{10,... | collective-permute-start | bytes 2506760 | tf_op jit(solution)/shard_map/ppermute | solution.py:441
  10.3 37.4 %collective-permute-start.7 = (bf16[256,1536]{1,0:T(8,128)(2,1)S(1)}, bf16[256,1536]{1,0:T(8,128)(2,1)}, u32[]{:S(2)}, u32[]{:S(2)}) collective-permute-start(bf16[256,1536]{1,0:T(8,128)(2,1)S(1)} %bitcast.13), channel_id=1, source_target_pairs={{0,2},{1,3},{2,0},{3,1},{4,6},{5,7},{6,4},{7,5},{8,10},{9,11},{10,... | collective-permute-start | bytes 2359304 | tf_op jit(solution)/shard_map/ppermute | solution.py:441
  25.1 37.0 %collective-permute-start.8 = (bf16[256,1536]{1,0:T(8,128)(2,1)S(1)}, bf16[256,1536]{1,0:T(8,128)(2,1)}, u32[]{:S(2)}, u32[]{:S(2)}) collective-permute-start(bf16[256,1536]{1,0:T(8,128)(2,1)S(1)} %bitcast.18), channel_id=1, source_target_pairs={{0,2},{1,3},{2,0},{3,1},{4,6},{5,7},{6,4},{7,5},{8,10},{9,11},{10,... | collective-permute-start | bytes 2359304 | tf_op jit(solution)/shard_map/ppermute | solution.py:441
  43.6 21.0 %collective-permute-start.9 = (bf16[256,1536]{1,0:T(8,128)(2,1)S(1)}, bf16[256,1536]{1,0:T(8,128)(2,1)S(1)}, u32[]{:S(2)}, u32[]{:S(2)}) collective-permute-start(bf16[256,1536]{1,0:T(8,128)(2,1)S(1)} %bitcast.14), channel_id=1, source_target_pairs={{0,8},{1,9},{2,10},{3,11},{4,12},{5,13},{6,14},{7,15},{8,0},{9,1},... | collective-permute-start | bytes 2359304 | tf_op jit(solution)/shard_map/ppermute | solution.py:441
  43.7 21.0 %collective-permute-start.10 = (bf16[256,1536]{1,0:T(8,128)(2,1)S(1)}, bf16[256,1536]{1,0:T(8,128)(2,1)S(1)}, u32[]{:S(2)}, u32[]{:S(2)}) collective-permute-start(bf16[256,1536]{1,0:T(8,128)(2,1)S(1)} %bitcast.19), channel_id=1, source_target_pairs={{0,8},{1,9},{2,10},{3,11},{4,12},{5,13},{6,14},{7,15},{8,0},{9,1},... | collective-permute-start | bytes 2359304 | tf_op jit(solution)/shard_map/ppermute | solution.py:441
  46.1 22.8 %collective-permute-start.4 = (bf16[272,1536]{1,0:T(8,128)(2,1)}, bf16[272,1536]{1,0:T(8,128)(2,1)}, u32[]{:S(2)}, u32[]{:S(2)}) collective-permute-start(bf16[272,1536]{1,0:T(8,128)(2,1)} %collective-permute-done.3.refs_1_.refs_5_), channel_id=1, source_target_pairs={{0,16},{1,17},{2,18},{3,19},{4,20},{5,21},{6,22},{7,23},{8,24},{9,... | collective-permute-start | bytes 2506760 | tf_op jit(solution)/shard_map/ppermute | solution.py:441
  47.7 37.3 %collective-permute-start.5 = (bf16[272,1536]{1,0:T(8,128)(2,1)}, bf16[272,1536]{1,0:T(8,128)(2,1)}, u32[]{:S(2)}, u32[]{:S(2)}) collective-permute-start(bf16[272,1536]{1,0:T(8,128)(2,1)} %collective-permute-done.3.refs_1_.refs_5_), channel_id=1, source_target_pairs={{0,1},{1,0},{2,3},{3,2},{4,5},{5,4},{6,7},{7,6},{8,9},{9,8},{10,11... | collective-permute-start | bytes 2506760 | tf_op jit(solution)/shard_map/ppermute | solution.py:441
  62.1 22.9 %collective-permute-start.6 = (bf16[272,1536]{1,0:T(8,128)(2,1)}, bf16[272,1536]{1,0:T(8,128)(2,1)}, u32[]{:S(2)}, u32[]{:S(2)}) collective-permute-start(bf16[272,1536]{1,0:T(8,128)(2,1)} %collective-permute-done.3.refs_1_.refs_5_), channel_id=1, source_target_pairs={{0,17},{1,16},{2,19},{3,18},{4,21},{5,20},{6,23},{7,22},{8,25},{9,... | collective-permute-start | bytes 2506760 | tf_op jit(solution)/shard_map/ppermute | solution.py:441
  68.4 28.8 %collective-permute-start.17 = (bf16[272,1536]{1,0:T(8,128)(2,1)}, bf16[272,1536]{1,0:T(8,128)(2,1)S(1)}, u32[]{:S(2)}, u32[]{:S(2)}) collective-permute-start(bf16[272,1536]{1,0:T(8,128)(2,1)} %collective-permute-done.3.refs_1_.refs_5_), channel_id=1, source_target_pairs={{0,8},{1,9},{2,10},{3,11},{4,12},{5,13},{6,14},{7,15},{8,0},{9,1},... | collective-permute-start | bytes 2506760 | tf_op jit(solution)/shard_map/ppermute | solution.py:441
  68.5 32.3 %collective-permute-start.16 = (bf16[1088,1536]{1,0:T(8,128)(2,1)}, bf16[1088,1536]{1,0:T(8,128)(2,1)}, u32[]{:S(2)}, u32[]{:S(2)}) collective-permute-start(bf16[1088,1536]{1,0:T(8,128)(2,1)} %pad_maximum_fusion), channel_id=1, source_target_pairs={{0,8},{1,9},{2,10},{3,11},{4,12},{5,13},{6,14},{7,15},{8,0},{9,1},... | collective-permute-start | bytes 10027016 | tf_op jit(solution)/shard_map/ppermute | solution.py:441
  69.0 29.0 %collective-permute-start.18 = (bf16[272,1536]{1,0:T(8,128)(2,1)}, bf16[272,1536]{1,0:T(8,128)(2,1)S(1)}, u32[]{:S(2)}, u32[]{:S(2)}) collective-permute-start(bf16[272,1536]{1,0:T(8,128)(2,1)} %collective-permute-done.4.refs_2_.refs_6_), channel_id=1, source_target_pairs={{0,8},{1,9},{2,10},{3,11},{4,12},{5,13},{6,14},{7,15},{8,0},{9,1},... | collective-permute-start | bytes 2506760 | tf_op jit(solution)/shard_map/ppermute | solution.py:441
  85.0 15.7 %collective-permute-start.20 = (bf16[272,1536]{1,0:T(8,128)(2,1)}, bf16[272,1536]{1,0:T(8,128)(2,1)S(1)}, u32[]{:S(2)}, u32[]{:S(2)}) collective-permute-start(bf16[272,1536]{1,0:T(8,128)(2,1)} %collective-permute-done.6.refs_4_.refs_8_), channel_id=1, source_target_pairs={{0,8},{1,9},{2,10},{3,11},{4,12},{5,13},{6,14},{7,15},{8,0},{9,1},... | collective-permute-start | bytes 2506760 | tf_op jit(solution)/shard_map/ppermute | solution.py:441
  97.2 37.1 %collective-permute-start.13 = (bf16[272,1536]{1,0:T(8,128)(2,1)}, bf16[272,1536]{1,0:T(8,128)(2,1)S(1)}, u32[]{:S(2)}, u32[]{:S(2)}) collective-permute-start(bf16[272,1536]{1,0:T(8,128)(2,1)} %get-tuple-element.37), channel_id=1, source_target_pairs={{0,16},{1,17},{2,18},{3,19},{4,20},{5,21},{6,22},{7,23},{8,24},{9,... | collective-permute-start | bytes 2506760 | tf_op jit(solution)/shard_map/ppermute | solution.py:441
  98.0 37.3 %collective-permute-start.14 = (bf16[272,1536]{1,0:T(8,128)(2,1)}, bf16[272,1536]{1,0:T(8,128)(2,1)S(1)}, u32[]{:S(2)}, u32[]{:S(2)}) collective-permute-start(bf16[272,1536]{1,0:T(8,128)(2,1)} %get-tuple-element.38), channel_id=1, source_target_pairs={{0,1},{1,0},{2,3},{3,2},{4,5},{5,4},{6,7},{7,6},{8,9},{9,8},{10,11... | collective-permute-start | bytes 2506760 | tf_op jit(solution)/shard_map/ppermute | solution.py:441
  99.3 37.5 %collective-permute-start.15 = (bf16[272,1536]{1,0:T(8,128)(2,1)}, bf16[272,1536]{1,0:T(8,128)(2,1)S(1)}, u32[]{:S(2)}, u32[]{:S(2)}) collective-permute-start(bf16[272,1536]{1,0:T(8,128)(2,1)} %get-tuple-element.39), channel_id=1, source_target_pairs={{0,17},{1,16},{2,19},{3,18},{4,21},{5,20},{6,23},{7,22},{8,25},{9,... | collective-permute-start | bytes 2506760 | tf_op jit(solution)/shard_map/ppermute | solution.py:441
  120.8 38.7 %collective-permute-start.25 = (bf16[256,1536]{1,0:T(8,128)(2,1)}, bf16[256,1536]{1,0:T(8,128)(2,1)S(1)}, u32[]{:S(2)}, u32[]{:S(2)}) collective-permute-start(bf16[256,1536]{1,0:T(8,128)(2,1)} %get-tuple-element.53), channel_id=1, source_target_pairs={{0,2},{1,3},{2,0},{3,1},{4,6},{5,7},{6,4},{7,5},{8,10},{9,11},{10,... | collective-permute-start | bytes 2359304 | tf_op jit(solution)/shard_map/ppermute | solution.py:441
  122.5 52.0 %collective-permute-start.26 = (bf16[256,1536]{1,0:T(8,128)(2,1)}, bf16[256,1536]{1,0:T(8,128)(2,1)S(1)}, u32[]{:S(2)}, u32[]{:S(2)}) collective-permute-start(bf16[256,1536]{1,0:T(8,128)(2,1)} %get-tuple-element.54), channel_id=1, source_target_pairs={{0,2},{1,3},{2,0},{3,1},{4,6},{5,7},{6,4},{7,5},{8,10},{9,11},{10,... | collective-permute-start | bytes 2359304 | tf_op jit(solution)/shard_map/ppermute | solution.py:441
  137.4 38.4 %collective-permute-start.24 = (bf16[272,1536]{1,0:T(8,128)(2,1)S(1)}, bf16[272,1536]{1,0:T(8,128)(2,1)S(1)}, u32[]{:S(2)}, u32[]{:S(2)}) collective-permute-start(bf16[272,1536]{1,0:T(8,128)(2,1)S(1)} %pad_maximum_fusion.2), channel_id=1, source_target_pairs={{0,4},{1,5},{2,6},{3,7},{4,0},{5,1},{6,2},{7,3},{8,12},{9,13},{10,... | collective-permute-start | bytes 2506760 | tf_op jit(solution)/shard_map/ppermute | solution.py:441
  138.6 37.3 %collective-permute-start.23 = (bf16[272,1536]{1,0:T(8,128)(2,1)S(1)}, bf16[272,1536]{1,0:T(8,128)(2,1)S(1)}, u32[]{:S(2)}, u32[]{:S(2)}) collective-permute-start(bf16[272,1536]{1,0:T(8,128)(2,1)S(1)} %copy-done.15), channel_id=1, source_target_pairs={{0,17},{1,16},{2,19},{3,18},{4,21},{5,20},{6,23},{7,22},{8,25},{9,... | collective-permute-start | bytes 2506760 | tf_op jit(solution)/shard_map/ppermute | solution.py:441
  140.1 36.5 %collective-permute-start.22 = (bf16[272,1536]{1,0:T(8,128)(2,1)S(1)}, bf16[272,1536]{1,0:T(8,128)(2,1)S(1)}, u32[]{:S(2)}, u32[]{:S(2)}) collective-permute-start(bf16[272,1536]{1,0:T(8,128)(2,1)S(1)} %copy-done.14), channel_id=1, source_target_pairs={{0,1},{1,0},{2,3},{3,2},{4,5},{5,4},{6,7},{7,6},{8,9},{9,8},{10,11... | collective-permute-start | bytes 2506760 | tf_op jit(solution)/shard_map/ppermute | solution.py:441
  159.5 17.4 %collective-permute-start.21 = (bf16[272,1536]{1,0:T(8,128)(2,1)S(1)}, bf16[272,1536]{1,0:T(8,128)(2,1)S(1)}, u32[]{:S(2)}, u32[]{:S(2)}) collective-permute-start(bf16[272,1536]{1,0:T(8,128)(2,1)S(1)} %copy-done.13), channel_id=1, source_target_pairs={{0,16},{1,17},{2,18},{3,19},{4,20},{5,21},{6,22},{7,23},{8,24},{9,... | collective-permute-start | bytes 2506760 | tf_op jit(solution)/shard_map/ppermute | solution.py:441
  (23 other events, 306.9 us)

commit v6 on v5

--- a/solution.py
+++ b/solution.py
@@ -495,10 +495,10 @@
     gate_rows = jnp.sum(jnp.where(named, gates.T[None], 0.0), axis=1)
 
     own = jnp.concatenate([tokens, grad_y, coded(gate_rows, features)], axis=0)
-    far = grid.swap_far(own)
     own_pair = (w_in[0], w_out[0])
     near_pieces = [grid.spread(own, *step) for step in steps]
-    near_pieces, far = tie(near_pieces, far)
+    far = grid.swap_far(own)
+    far, near_pieces = tie(far, near_pieces)
     near_pair = tuple(grid.swap_near(part) for part in own_pair)
     far_pieces = [grid.spread(far, *step) for step in steps]
     near_over = grid.swap_core(jnp.concatenate(near_pieces, axis=0))
@@ -513,8 +513,10 @@
         rows, first, near_pieces, far_pieces, near_over, far_over, far_values, weights[:2]
     )
     near_out = near_call(rows, first, score, near_pieces, near_values, weights)
-    far_home, near_out, _ = tie(far_home, near_out, near_sums)
+    far_home, _ = tie(far_home, near_sums)
     near_sums = [grid.swap_near(part) for part in near_sums]
+    last_out, near_sums[0] = tie(near_out[-1], near_sums[0])
+    near_out = [*near_out[:-1], last_out]
     far_home = total(far_home)
 
     def score_of(home):

time: 180 us -> 178 us (0.989)
  transfers between devices with their start and end apart: 27 -> 27, of which waited for: 11 -> 12; matrix products, arithmetic and copies ran while one was open for 3% -> 3% of each run, Pallas kernels for 24% -> 24%
where the time goes in v6:
time: 178 us
  waiting for transfers between devices  94.7 us (53%)
  Pallas kernels  42.1 us (24%)
  starting transfers between devices  29.9 us (17%)
  other arithmetic  8.2 us (5%)
  local copies, waits for them, and re-layouts  1.96 us (1%)
    ppermute x27, waiting for transfers between devices, move(): return lax.ppermute(array, AXES, pairs)  94.7 us
    ppermute x27, starting transfers between devices, move(): return lax.ppermute(array, AXES, pairs)  29.9 us
    pallas_call x1, Pallas kernels, sums_call(): pl.pallas_call(functools.partial(sums_kernel, (count, rows)), out_shape=[...  19.1 us
    pallas_call x1, Pallas kernels, far_call(): pl.pallas_call(functools.partial(far_kernel, (count, rows)), out_shape=[s...  11.6 us
    pallas_call x1, Pallas kernels, near_call(): pl.pallas_call(functools.partial(near_kernel, (count, rows)), out_shape=[...  11.4 us
  transfers between devices with their start and end apart: 27, of which 12 were waited for; matrix products, arithmetic and copies ran while one was open for 3% of the time, Pallas kernels for 24%

profile of v6, /device:TPU:0, one launch (start us, length us, event | category | flops | bytes accessed | tf_op | source)
XLA Modules:
  0.0 177.7 jit_solution(12696352279796602527)
XLA Ops:
  2.7 4.0 %collective-permute-start.3 = (bf16[272,1536]{1,0:T(8,128)(2,1)S(1)}, bf16[272,1536]{1,0:T(8,128)(2,1)S(1)}, u32[]{:S(2)}, u32[]{:S(2)}) collective-permute-start(bf16[272,1536]{1,0:T(8,128)(2,1)S(1)} %pad_maximum_fusion.1.refs_1_.refs_2_), channel_id=1, source_target_pairs={{0,17},{1,16},{2,19},{3,18},{4,21},{5,20},{6,23},{7,22},{8,25},{9,... | collective-permute-start | bytes 2506760 | tf_op jit(solution)/shard_map/ppermute | solution.py:441
  7.3 3.0 %collective-permute-start = (bf16[272,1536]{1,0:T(8,128)(2,1)S(1)}, bf16[272,1536]{1,0:T(8,128)(2,1)}, u32[]{:S(2)}, u32[]{:S(2)}) collective-permute-start(bf16[272,1536]{1,0:T(8,128)(2,1)S(1)} %pad_maximum_fusion.1.refs_1_.refs_2_), channel_id=1, source_target_pairs={{0,4},{1,5},{2,6},{3,7},{4,0},{5,1},{6,2},{7,3},{8,12},{9,13},{10,... | collective-permute-start | bytes 2506760 | tf_op jit(solution)/shard_map/ppermute | solution.py:441
  10.3 15.8 %collective-permute-done.3.refs_4_.refs_5_ = bf16[272,1536]{1,0:T(8,128)(2,1)S(1)} collective-permute-done((bf16[272,1536]{1,0:T(8,128)(2,1)S(1)}, bf16[272,1536]{1,0:T(8,128)(2,1)S(1)}, u32[]{:S(2)}, u32[]{:S(2)}) %collective-permute-start.3) | collective-permute-done | bytes 835616 | tf_op jit(solution)/shard_map/ppermute | solution.py:441
  26.1 2.1 %collective-permute-start.12 = (bf16[256,1536]{1,0:T(8,128)(2,1)S(1)}, bf16[256,1536]{1,0:T(8,128)(2,1)}, u32[]{:S(2)}, u32[]{:S(2)}) collective-permute-start(bf16[256,1536]{1,0:T(8,128)(2,1)S(1)} %bitcast.14), channel_id=1, source_target_pairs={{0,2},{1,3},{2,0},{3,1},{4,6},{5,7},{6,4},{7,5},{8,10},{9,11},{10,... | collective-permute-start | bytes 2359304 | tf_op jit(solution)/shard_map/ppermute | solution.py:441
  28.2 14.9 %collective-permute-done.2.refs_3_.refs_4_ = bf16[272,1536]{1,0:T(8,128)(2,1)S(1)} collective-permute-done((bf16[272,1536]{1,0:T(8,128)(2,1)S(1)}, bf16[272,1536]{1,0:T(8,128)(2,1)S(1)}, u32[]{:S(2)}, u32[]{:S(2)}) %collective-permute-start.2) | collective-permute-done | bytes 835616 | tf_op jit(solution)/shard_map/ppermute | solution.py:441
  43.4 1.6 collective-permute-start.13
  46.1 2.5 %collective-permute-start.6 = (bf16[272,1536]{1,0:T(8,128)(2,1)}, bf16[272,1536]{1,0:T(8,128)(2,1)}, u32[]{:S(2)}, u32[]{:S(2)}) collective-permute-start(bf16[272,1536]{1,0:T(8,128)(2,1)} %collective-permute-done.refs_1_.refs_5_), channel_id=1, source_target_pairs={{0,17},{1,16},{2,19},{3,18},{4,21},{5,20},{6,23},{7,22},{8,25},{9,... | collective-permute-start | bytes 2506760 | tf_op jit(solution)/shard_map/ppermute | solution.py:441
  49.2 13.9 %collective-permute-done.12.refs_7_.refs_18_.refs_10_ = bf16[256,1536]{1,0:T(8,128)(2,1)} collective-permute-done((bf16[256,1536]{1,0:T(8,128)(2,1)S(1)}, bf16[256,1536]{1,0:T(8,128)(2,1)}, u32[]{:S(2)}, u32[]{:S(2)}) %collective-permute-start.12) | collective-permute-done | bytes 786464 | tf_op jit(solution)/shard_map/ppermute | solution.py:441
  63.1 1.5 collective-permute-start.4
  64.6 13.1 %collective-permute-done.13.refs_8_.refs_19_.refs_11_ = bf16[256,1536]{1,0:T(8,128)(2,1)} collective-permute-done((bf16[256,1536]{1,0:T(8,128)(2,1)S(1)}, bf16[256,1536]{1,0:T(8,128)(2,1)}, u32[]{:S(2)}, u32[]{:S(2)}) %collective-permute-start.13) | collective-permute-done | bytes 786464 | tf_op jit(solution)/shard_map/ppermute | solution.py:441
  77.7 1.9 %pad_maximum_fusion = bf16[1088,1536]{1,0:T(8,128)(2,1)} fusion(bf16[272,1536]{1,0:T(8,128)(2,1)S(1)} %collective-permute-done.3.refs_4_.refs_5_, bf16[272,1536]{1,0:T(8,128)(2,1)S(1)} %collective-permute-done.2.refs_3_.refs_4_, bf16[272,1536]{1,0:T(8,128)(2,1)S(1)} %collective-permute-done.1.refs_2_.refs_3_, ...), kind=kLoop, calls=%fused_computation | loop fusion | flops 13369344 | bytes 6684672 | tf_op jit(solution)/shard_map/concatenate | solution.py:504
  80.9 3.9 %collective-permute-done.5.refs_3_.refs_7_ = bf16[272,1536]{1,0:T(8,128)(2,1)} collective-permute-done((bf16[272,1536]{1,0:T(8,128)(2,1)}, bf16[272,1536]{1,0:T(8,128)(2,1)}, u32[]{:S(2)}, u32[]{:S(2)}) %collective-permute-start.5) | collective-permute-done | bytes 835616 | tf_op jit(solution)/shard_map/ppermute | solution.py:441
  85.3 11.6 %shard_map.101 = (bf16[512,512]{1,0:T(8,128)(2,1)}, bf16[512,512]{1,0:T(8,128)(2,1)}, bf16[272,1536]{1,0:T(8,128)(2,1)}, bf16[272,1536]{1,0:T(8,128)(2,1)}, bf16...) custom-call(s32[1]{0:T(128)} %bitcast.refs_0_, bf16[272,1536]{1,0:T(8,128)(2,1)} %collective-permute-done.refs_1_.refs_5_, ...), custom_call_target="tpu_custom_call" | custom-call | flops 99999997952 | bytes 100000000 | tf_op jit(solution)/shard_map/pallas_call | solution.py:358
  96.9 1.6 collective-permute-start.22
  101.4 19.1 %shard_map.102 = (bf16[512,512]{1,0:T(8,128)(2,1)}, bf16[512,512]{1,0:T(8,128)(2,1)}, f32[256,1536]{1,0:T(8,128)}, f32[256,1536]{1,0:T(8,128)}, bf16[256,1536]{1...) custom-call(s32[1]{0:T(128)} %bitcast.refs_0_, bf16[272,1536]{1,0:T(8,128)(2,1)} %copy-done, ...), custom_call_target="tpu_custom_call" | custom-call | flops 99999997952 | bytes 100000000 | tf_op jit(solution)/shard_map/pallas_call | solution.py:382
  120.5 1.6 collective-permute-start.20
  122.6 11.4 %shard_map.103 = (bf16[272,1536]{1,0:T(8,128)(2,1)}, bf16[272,1536]{1,0:T(8,128)(2,1)}, bf16[272,1536]{1,0:T(8,128)(2,1)}, bf16[272,1536]{1,0:T(8,128)(2,1)}) custom-call(s32[1]{0:T(128)} %bitcast.refs_0_, f32[512,16]{1,0:T(8,128)} %get-tuple-element.40.refs_1_, bf16[272,1536]{1,0:T(8,128)(2,1)} %copy-done, bf16[272,1536]{1,0:T(8,128)(2,1)} %copy-done.3, ...), custom_call_target="tpu_custom_call" | custom-call | flops 1000 | bytes 1 | tf_op jit(solution)/shard_map/pallas_call | solution.py:407
  134.0 1.6 collective-permute-start.18
  138.3 2.6 %collective-permute-start.25 = (bf16[272,1536]{1,0:T(8,128)(2,1)S(1)}, bf16[272,1536]{1,0:T(8,128)(2,1)S(1)}, u32[]{:S(2)}, u32[]{:S(2)}) collective-permute-start(bf16[272,1536]{1,0:T(8,128)(2,1)S(1)} %pad_maximum_fusion.2), channel_id=1, source_target_pairs={{0,4},{1,5},{2,6},{3,7},{4,0},{5,1},{6,2},{7,3},{8,12},{9,13},{10,... | collective-permute-start | bytes 2506760 | tf_op jit(solution)/shard_map/ppermute | solution.py:441
  140.9 18.3 %collective-permute-done.20 = bf16[256,1536]{1,0:T(8,128)(2,1)S(1)} collective-permute-done((bf16[256,1536]{1,0:T(8,128)(2,1)}, bf16[256,1536]{1,0:T(8,128)(2,1)S(1)}, u32[]{:S(2)}, u32[]{:S(2)}) %collective-permute-start.20) | collective-permute-done | bytes 786464 | tf_op jit(solution)/shard_map/ppermute | solution.py:441
  159.2 1.8 collective-permute-start.21
  161.0 1.4 add_bitcast_fusion.1
  162.3 11.9 %collective-permute-done.26 = bf16[256,1536]{1,0:T(8,128)(2,1)S(1)} collective-permute-done((bf16[256,1536]{1,0:T(8,128)(2,1)}, bf16[256,1536]{1,0:T(8,128)(2,1)S(1)}, u32[]{:S(2)}, u32[]{:S(2)}) %collective-permute-start.26) | collective-permute-done | bytes 786464 | tf_op jit(solution)/shard_map/ppermute | solution.py:441
  174.3 1.4 add_bitcast_fusion
  (86 shorter events, 14.3 us)
Async XLA Ops:
  2.7 23.4 %collective-permute-start.3 = (bf16[272,1536]{1,0:T(8,128)(2,1)S(1)}, bf16[272,1536]{1,0:T(8,128)(2,1)S(1)}, u32[]{:S(2)}, u32[]{:S(2)}) collective-permute-start(bf16[272,1536]{1,0:T(8,128)(2,1)S(1)} %pad_maximum_fusion.1.refs_1_.refs_2_), channel_id=1, source_target_pairs={{0,17},{1,16},{2,19},{3,18},{4,21},{5,20},{6,23},{7,22},{8,25},{9,... | collective-permute-start | bytes 2506760 | tf_op jit(solution)/shard_map/ppermute | solution.py:441
  6.6 36.5 %collective-permute-start.2 = (bf16[272,1536]{1,0:T(8,128)(2,1)S(1)}, bf16[272,1536]{1,0:T(8,128)(2,1)S(1)}, u32[]{:S(2)}, u32[]{:S(2)}) collective-permute-start(bf16[272,1536]{1,0:T(8,128)(2,1)S(1)} %pad_maximum_fusion.1.refs_1_.refs_2_), channel_id=1, source_target_pairs={{0,1},{1,0},{2,3},{3,2},{4,5},{5,4},{6,7},{7,6},{8,9},{9,8},{10,11... | collective-permute-start | bytes 2506760 | tf_op jit(solution)/shard_map/ppermute | solution.py:441
  7.1 36.3 %collective-permute-start.1 = (bf16[272,1536]{1,0:T(8,128)(2,1)S(1)}, bf16[272,1536]{1,0:T(8,128)(2,1)S(1)}, u32[]{:S(2)}, u32[]{:S(2)}) collective-permute-start(bf16[272,1536]{1,0:T(8,128)(2,1)S(1)} %pad_maximum_fusion.1.refs_1_.refs_2_), channel_id=1, source_target_pairs={{0,16},{1,17},{2,18},{3,19},{4,20},{5,21},{6,22},{7,23},{8,24},{9,... | collective-permute-start | bytes 2506760 | tf_op jit(solution)/shard_map/ppermute | solution.py:441
  7.3 38.9 %collective-permute-start = (bf16[272,1536]{1,0:T(8,128)(2,1)S(1)}, bf16[272,1536]{1,0:T(8,128)(2,1)}, u32[]{:S(2)}, u32[]{:S(2)}) collective-permute-start(bf16[272,1536]{1,0:T(8,128)(2,1)S(1)} %pad_maximum_fusion.1.refs_1_.refs_2_), channel_id=1, source_target_pairs={{0,4},{1,5},{2,6},{3,7},{4,0},{5,1},{6,2},{7,3},{8,12},{9,13},{10,... | collective-permute-start | bytes 2506760 | tf_op jit(solution)/shard_map/ppermute | solution.py:441
  10.3 38.4 %collective-permute-start.14 = (bf16[256,1536]{1,0:T(8,128)(2,1)S(1)}, bf16[256,1536]{1,0:T(8,128)(2,1)S(1)}, u32[]{:S(2)}, u32[]{:S(2)}) collective-permute-start(bf16[256,1536]{1,0:T(8,128)(2,1)S(1)} %bitcast.13), channel_id=1, source_target_pairs={{0,8},{1,9},{2,10},{3,11},{4,12},{5,13},{6,14},{7,15},{8,0},{9,1},... | collective-permute-start | bytes 2359304 | tf_op jit(solution)/shard_map/ppermute | solution.py:441
  26.1 36.9 %collective-permute-start.12 = (bf16[256,1536]{1,0:T(8,128)(2,1)S(1)}, bf16[256,1536]{1,0:T(8,128)(2,1)}, u32[]{:S(2)}, u32[]{:S(2)}) collective-permute-start(bf16[256,1536]{1,0:T(8,128)(2,1)S(1)} %bitcast.14), channel_id=1, source_target_pairs={{0,2},{1,3},{2,0},{3,1},{4,6},{5,7},{6,4},{7,5},{8,10},{9,11},{10,... | collective-permute-start | bytes 2359304 | tf_op jit(solution)/shard_map/ppermute | solution.py:441
  43.1 21.4 %collective-permute-start.15 = (bf16[256,1536]{1,0:T(8,128)(2,1)S(1)}, bf16[256,1536]{1,0:T(8,128)(2,1)S(1)}, u32[]{:S(2)}, u32[]{:S(2)}) collective-permute-start(bf16[256,1536]{1,0:T(8,128)(2,1)S(1)} %bitcast.18), channel_id=1, source_target_pairs={{0,8},{1,9},{2,10},{3,11},{4,12},{5,13},{6,14},{7,15},{8,0},{9,1},... | collective-permute-start | bytes 2359304 | tf_op jit(solution)/shard_map/ppermute | solution.py:441
  43.4 34.3 %collective-permute-start.13 = (bf16[256,1536]{1,0:T(8,128)(2,1)S(1)}, bf16[256,1536]{1,0:T(8,128)(2,1)}, u32[]{:S(2)}, u32[]{:S(2)}) collective-permute-start(bf16[256,1536]{1,0:T(8,128)(2,1)S(1)} %bitcast.19), channel_id=1, source_target_pairs={{0,2},{1,3},{2,0},{3,1},{4,6},{5,7},{6,4},{7,5},{8,10},{9,11},{10,... | collective-permute-start | bytes 2359304 | tf_op jit(solution)/shard_map/ppermute | solution.py:441
  46.1 34.3 %collective-permute-start.6 = (bf16[272,1536]{1,0:T(8,128)(2,1)}, bf16[272,1536]{1,0:T(8,128)(2,1)}, u32[]{:S(2)}, u32[]{:S(2)}) collective-permute-start(bf16[272,1536]{1,0:T(8,128)(2,1)} %collective-permute-done.refs_1_.refs_5_), channel_id=1, source_target_pairs={{0,17},{1,16},{2,19},{3,18},{4,21},{5,20},{6,23},{7,22},{8,25},{9,... | collective-permute-start | bytes 2506760 | tf_op jit(solution)/shard_map/ppermute | solution.py:441
  48.7 36.1 %collective-permute-start.5 = (bf16[272,1536]{1,0:T(8,128)(2,1)}, bf16[272,1536]{1,0:T(8,128)(2,1)}, u32[]{:S(2)}, u32[]{:S(2)}) collective-permute-start(bf16[272,1536]{1,0:T(8,128)(2,1)} %collective-permute-done.refs_1_.refs_5_), channel_id=1, source_target_pairs={{0,1},{1,0},{2,3},{3,2},{4,5},{5,4},{6,7},{7,6},{8,9},{9,8},{10,11... | collective-permute-start | bytes 2506760 | tf_op jit(solution)/shard_map/ppermute | solution.py:441
  63.1 21.8 %collective-permute-start.4 = (bf16[272,1536]{1,0:T(8,128)(2,1)}, bf16[272,1536]{1,0:T(8,128)(2,1)}, u32[]{:S(2)}, u32[]{:S(2)}) collective-permute-start(bf16[272,1536]{1,0:T(8,128)(2,1)} %collective-permute-done.refs_1_.refs_5_), channel_id=1, source_target_pairs={{0,16},{1,17},{2,18},{3,19},{4,20},{5,21},{6,22},{7,23},{8,24},{9,... | collective-permute-start | bytes 2506760 | tf_op jit(solution)/shard_map/ppermute | solution.py:441
  79.7 17.2 %collective-permute-start.8 = (bf16[272,1536]{1,0:T(8,128)(2,1)}, bf16[272,1536]{1,0:T(8,128)(2,1)S(1)}, u32[]{:S(2)}, u32[]{:S(2)}) collective-permute-start(bf16[272,1536]{1,0:T(8,128)(2,1)} %collective-permute-done.refs_1_.refs_5_), channel_id=1, source_target_pairs={{0,8},{1,9},{2,10},{3,11},{4,12},{5,13},{6,14},{7,15},{8,0},{9,1},... | collective-permute-start | bytes 2506760 | tf_op jit(solution)/shard_map/ppermute | solution.py:441
  80.3 20.2 %collective-permute-start.7 = (bf16[1088,1536]{1,0:T(8,128)(2,1)}, bf16[1088,1536]{1,0:T(8,128)(2,1)}, u32[]{:S(2)}, u32[]{:S(2)}) collective-permute-start(bf16[1088,1536]{1,0:T(8,128)(2,1)} %pad_maximum_fusion), channel_id=1, source_target_pairs={{0,8},{1,9},{2,10},{3,11},{4,12},{5,13},{6,14},{7,15},{8,0},{9,1},... | collective-permute-start | bytes 10027016 | tf_op jit(solution)/shard_map/ppermute | solution.py:441
  80.5 18.0 %collective-permute-start.11 = (bf16[272,1536]{1,0:T(8,128)(2,1)}, bf16[272,1536]{1,0:T(8,128)(2,1)S(1)}, u32[]{:S(2)}, u32[]{:S(2)}) collective-permute-start(bf16[272,1536]{1,0:T(8,128)(2,1)} %collective-permute-done.6.refs_4_.refs_8_), channel_id=1, source_target_pairs={{0,8},{1,9},{2,10},{3,11},{4,12},{5,13},{6,14},{7,15},{8,0},{9,1},... | collective-permute-start | bytes 2506760 | tf_op jit(solution)/shard_map/ppermute | solution.py:441
  84.9 15.6 %collective-permute-start.9 = (bf16[272,1536]{1,0:T(8,128)(2,1)}, bf16[272,1536]{1,0:T(8,128)(2,1)S(1)}, u32[]{:S(2)}, u32[]{:S(2)}) collective-permute-start(bf16[272,1536]{1,0:T(8,128)(2,1)} %collective-permute-done.4.refs_2_.refs_6_), channel_id=1, source_target_pairs={{0,8},{1,9},{2,10},{3,11},{4,12},{5,13},{6,14},{7,15},{8,0},{9,1},... | collective-permute-start | bytes 2506760 | tf_op jit(solution)/shard_map/ppermute | solution.py:441
  96.9 37.1 %collective-permute-start.22 = (bf16[272,1536]{1,0:T(8,128)(2,1)}, bf16[272,1536]{1,0:T(8,128)(2,1)S(1)}, u32[]{:S(2)}, u32[]{:S(2)}) collective-permute-start(bf16[272,1536]{1,0:T(8,128)(2,1)} %get-tuple-element.50), channel_id=1, source_target_pairs={{0,16},{1,17},{2,18},{3,19},{4,20},{5,21},{6,22},{7,23},{8,24},{9,... | collective-permute-start | bytes 2506760 | tf_op jit(solution)/shard_map/ppermute | solution.py:441
  98.5 38.4 %collective-permute-start.23 = (bf16[272,1536]{1,0:T(8,128)(2,1)}, bf16[272,1536]{1,0:T(8,128)(2,1)S(1)}, u32[]{:S(2)}, u32[]{:S(2)}) collective-permute-start(bf16[272,1536]{1,0:T(8,128)(2,1)} %get-tuple-element.51), channel_id=1, source_target_pairs={{0,1},{1,0},{2,3},{3,2},{4,5},{5,4},{6,7},{7,6},{8,9},{9,8},{10,11... | collective-permute-start | bytes 2506760 | tf_op jit(solution)/shard_map/ppermute | solution.py:441
  99.3 38.4 %collective-permute-start.24 = (bf16[272,1536]{1,0:T(8,128)(2,1)}, bf16[272,1536]{1,0:T(8,128)(2,1)S(1)}, u32[]{:S(2)}, u32[]{:S(2)}) collective-permute-start(bf16[272,1536]{1,0:T(8,128)(2,1)} %get-tuple-element.52), channel_id=1, source_target_pairs={{0,17},{1,16},{2,19},{3,18},{4,21},{5,20},{6,23},{7,22},{8,25},{9,... | collective-permute-start | bytes 2506760 | tf_op jit(solution)/shard_map/ppermute | solution.py:441
  120.5 38.7 %collective-permute-start.20 = (bf16[256,1536]{1,0:T(8,128)(2,1)}, bf16[256,1536]{1,0:T(8,128)(2,1)S(1)}, u32[]{:S(2)}, u32[]{:S(2)}) collective-permute-start(bf16[256,1536]{1,0:T(8,128)(2,1)} %get-tuple-element.47), channel_id=1, source_target_pairs={{0,2},{1,3},{2,0},{3,1},{4,6},{5,7},{6,4},{7,5},{8,10},{9,11},{10,... | collective-permute-start | bytes 2359304 | tf_op jit(solution)/shard_map/ppermute | solution.py:441
  122.2 52.1 %collective-permute-start.26 = (bf16[256,1536]{1,0:T(8,128)(2,1)}, bf16[256,1536]{1,0:T(8,128)(2,1)S(1)}, u32[]{:S(2)}, u32[]{:S(2)}) collective-permute-start(bf16[256,1536]{1,0:T(8,128)(2,1)} %get-tuple-element.53), channel_id=1, source_target_pairs={{0,2},{1,3},{2,0},{3,1},{4,6},{5,7},{6,4},{7,5},{8,10},{9,11},{10,... | collective-permute-start | bytes 2359304 | tf_op jit(solution)/shard_map/ppermute | solution.py:441
  134.0 41.6 %collective-permute-start.18 = (bf16[272,1536]{1,0:T(8,128)(2,1)}, bf16[272,1536]{1,0:T(8,128)(2,1)S(1)}, u32[]{:S(2)}, u32[]{:S(2)}) collective-permute-start(bf16[272,1536]{1,0:T(8,128)(2,1)} %get-tuple-element.44), channel_id=1, source_target_pairs={{0,16},{1,17},{2,18},{3,19},{4,20},{5,21},{6,22},{7,23},{8,24},{9,... | collective-permute-start | bytes 2506760 | tf_op jit(solution)/shard_map/ppermute | solution.py:441
  136.9 38.8 %collective-permute-start.19 = (bf16[272,1536]{1,0:T(8,128)(2,1)}, bf16[272,1536]{1,0:T(8,128)(2,1)S(1)}, u32[]{:S(2)}, u32[]{:S(2)}) collective-permute-start(bf16[272,1536]{1,0:T(8,128)(2,1)} %get-tuple-element.45), channel_id=1, source_target_pairs={{0,1},{1,0},{2,3},{3,2},{4,5},{5,4},{6,7},{7,6},{8,9},{9,8},{10,11... | collective-permute-start | bytes 2506760 | tf_op jit(solution)/shard_map/ppermute | solution.py:441
  138.3 37.4 %collective-permute-start.25 = (bf16[272,1536]{1,0:T(8,128)(2,1)S(1)}, bf16[272,1536]{1,0:T(8,128)(2,1)S(1)}, u32[]{:S(2)}, u32[]{:S(2)}) collective-permute-start(bf16[272,1536]{1,0:T(8,128)(2,1)S(1)} %pad_maximum_fusion.2), channel_id=1, source_target_pairs={{0,4},{1,5},{2,6},{3,7},{4,0},{5,1},{6,2},{7,3},{8,12},{9,13},{10,... | collective-permute-start | bytes 2506760 | tf_op jit(solution)/shard_map/ppermute | solution.py:441
  159.2 16.5 %collective-permute-start.21 = (bf16[272,1536]{1,0:T(8,128)(2,1)S(1)}, bf16[272,1536]{1,0:T(8,128)(2,1)S(1)}, u32[]{:S(2)}, u32[]{:S(2)}) collective-permute-start(bf16[272,1536]{1,0:T(8,128)(2,1)S(1)} %copy-done.13), channel_id=1, source_target_pairs={{0,17},{1,16},{2,19},{3,18},{4,21},{5,20},{6,23},{7,22},{8,25},{9,... | collective-permute-start | bytes 2506760 | tf_op jit(solution)/shard_map/ppermute | solution.py:441
  (21 other events, 412.7 us)

commit v7 on v6

--- a/solution.py
+++ b/solution.py
@@ -120,9 +120,10 @@
         for e in range(2):
             here, scale = gate_of(gate, first ^ e)
             part = 0.0
+            if t == 0:
+                weight_ready[2 * e].wait()
+                weight_ready[2 * e + 1].wait()
             for i in (2 * e, 2 * e + 1):
-                if t == 0:
-                    weight_ready[i].wait()
                 part = part + hidden_part(
                     tok[span, :],
                     grad[span, :],
@@ -250,9 +251,10 @@
             gate = jnp.concatenate([decode(coded_rows[slot, k], rows) for k in range(group)], axis=0)
             here, scale = gate_of(gate, first)
             part = 0.0
+            if n == 0:
+                weight_ready[0].wait()
+                weight_ready[1].wait()
             for k in range(2):
-                if n == 0:
-                    weight_ready[k].wait()
                 columns = slice(k * hidden, (k + 1) * hidden)
                 part = part + hidden_part(
                     tok[slot], grad[slot], weights[k], scale, acts.at[slot], hids.at[slot], columns

time: 178 us -> 177 us (level)
  no operation moved by 1% of the time
where the time goes in v7:
time: 177 us
  waiting for transfers between devices  94.7 us (54%)
  Pallas kernels  41.7 us (24%)
  starting transfers between devices  29.8 us (17%)
  other arithmetic  8.2 us (5%)
  local copies, waits for them, and re-layouts  1.96 us (1%)
    ppermute x27, waiting for transfers between devices, move(): return lax.ppermute(array, AXES, pairs)  94.7 us
    ppermute x27, starting transfers between devices, move(): return lax.ppermute(array, AXES, pairs)  29.8 us
    pallas_call x1, Pallas kernels, sums_call(): pl.pallas_call(functools.partial(sums_kernel, (count, rows)), out_shape=[...  19.1 us
    pallas_call x1, Pallas kernels, near_call(): pl.pallas_call(functools.partial(near_kernel, (count, rows)), out_shape=[...  11.4 us
    pallas_call x1, Pallas kernels, far_call(): pl.pallas_call(functools.partial(far_kernel, (count, rows)), out_shape=[s...  11.2 us
  transfers between devices with their start and end apart: 27, of which 12 were waited for; matrix products, arithmetic and copies ran while one was open for 3% of the time, Pallas kernels for 24%

profile of v7, /device:TPU:0, one launch (start us, length us, event | category | flops | bytes accessed | tf_op | source)
XLA Modules:
  0.0 177.3 jit_solution(8477308726804108056)
XLA Ops:
  2.7 4.0 %collective-permute-start.3 = (bf16[272,1536]{1,0:T(8,128)(2,1)S(1)}, bf16[272,1536]{1,0:T(8,128)(2,1)S(1)}, u32[]{:S(2)}, u32[]{:S(2)}) collective-permute-start(bf16[272,1536]{1,0:T(8,128)(2,1)S(1)} %pad_maximum_fusion.1.refs_1_.refs_2_), channel_id=1, source_target_pairs={{0,17},{1,16},{2,19},{3,18},{4,21},{5,20},{6,23},{7,22},{8,25},{9,... | collective-permute-start | bytes 2506760 | tf_op jit(solution)/shard_map/ppermute | solution.py:443
  7.3 3.0 %collective-permute-start = (bf16[272,1536]{1,0:T(8,128)(2,1)S(1)}, bf16[272,1536]{1,0:T(8,128)(2,1)}, u32[]{:S(2)}, u32[]{:S(2)}) collective-permute-start(bf16[272,1536]{1,0:T(8,128)(2,1)S(1)} %pad_maximum_fusion.1.refs_1_.refs_2_), channel_id=1, source_target_pairs={{0,4},{1,5},{2,6},{3,7},{4,0},{5,1},{6,2},{7,3},{8,12},{9,13},{10,... | collective-permute-start | bytes 2506760 | tf_op jit(solution)/shard_map/ppermute | solution.py:443
  10.3 15.8 %collective-permute-done.3.refs_4_.refs_5_ = bf16[272,1536]{1,0:T(8,128)(2,1)S(1)} collective-permute-done((bf16[272,1536]{1,0:T(8,128)(2,1)S(1)}, bf16[272,1536]{1,0:T(8,128)(2,1)S(1)}, u32[]{:S(2)}, u32[]{:S(2)}) %collective-permute-start.3) | collective-permute-done | bytes 835616 | tf_op jit(solution)/shard_map/ppermute | solution.py:443
  26.1 2.1 %collective-permute-start.12 = (bf16[256,1536]{1,0:T(8,128)(2,1)S(1)}, bf16[256,1536]{1,0:T(8,128)(2,1)}, u32[]{:S(2)}, u32[]{:S(2)}) collective-permute-start(bf16[256,1536]{1,0:T(8,128)(2,1)S(1)} %bitcast.14), channel_id=1, source_target_pairs={{0,2},{1,3},{2,0},{3,1},{4,6},{5,7},{6,4},{7,5},{8,10},{9,11},{10,... | collective-permute-start | bytes 2359304 | tf_op jit(solution)/shard_map/ppermute | solution.py:443
  28.2 14.9 %collective-permute-done.2.refs_3_.refs_4_ = bf16[272,1536]{1,0:T(8,128)(2,1)S(1)} collective-permute-done((bf16[272,1536]{1,0:T(8,128)(2,1)S(1)}, bf16[272,1536]{1,0:T(8,128)(2,1)S(1)}, u32[]{:S(2)}, u32[]{:S(2)}) %collective-permute-start.2) | collective-permute-done | bytes 835616 | tf_op jit(solution)/shard_map/ppermute | solution.py:443
  43.4 1.6 collective-permute-start.13
  46.1 2.5 %collective-permute-start.6 = (bf16[272,1536]{1,0:T(8,128)(2,1)}, bf16[272,1536]{1,0:T(8,128)(2,1)}, u32[]{:S(2)}, u32[]{:S(2)}) collective-permute-start(bf16[272,1536]{1,0:T(8,128)(2,1)} %collective-permute-done.refs_1_.refs_5_), channel_id=1, source_target_pairs={{0,17},{1,16},{2,19},{3,18},{4,21},{5,20},{6,23},{7,22},{8,25},{9,... | collective-permute-start | bytes 2506760 | tf_op jit(solution)/shard_map/ppermute | solution.py:443
  49.2 13.9 %collective-permute-done.12.refs_7_.refs_18_.refs_10_ = bf16[256,1536]{1,0:T(8,128)(2,1)} collective-permute-done((bf16[256,1536]{1,0:T(8,128)(2,1)S(1)}, bf16[256,1536]{1,0:T(8,128)(2,1)}, u32[]{:S(2)}, u32[]{:S(2)}) %collective-permute-start.12) | collective-permute-done | bytes 786464 | tf_op jit(solution)/shard_map/ppermute | solution.py:443
  63.1 1.5 collective-permute-start.4
  64.6 13.1 %collective-permute-done.13.refs_8_.refs_19_.refs_11_ = bf16[256,1536]{1,0:T(8,128)(2,1)} collective-permute-done((bf16[256,1536]{1,0:T(8,128)(2,1)S(1)}, bf16[256,1536]{1,0:T(8,128)(2,1)}, u32[]{:S(2)}, u32[]{:S(2)}) %collective-permute-start.13) | collective-permute-done | bytes 786464 | tf_op jit(solution)/shard_map/ppermute | solution.py:443
  77.7 1.9 %pad_maximum_fusion = bf16[1088,1536]{1,0:T(8,128)(2,1)} fusion(bf16[272,1536]{1,0:T(8,128)(2,1)S(1)} %collective-permute-done.3.refs_4_.refs_5_, bf16[272,1536]{1,0:T(8,128)(2,1)S(1)} %collective-permute-done.2.refs_3_.refs_4_, bf16[272,1536]{1,0:T(8,128)(2,1)S(1)} %collective-permute-done.1.refs_2_.refs_3_, ...), kind=kLoop, calls=%fused_computation | loop fusion | flops 13369344 | bytes 6684672 | tf_op jit(solution)/shard_map/concatenate | solution.py:506
  80.9 3.9 %collective-permute-done.5.refs_3_.refs_7_ = bf16[272,1536]{1,0:T(8,128)(2,1)} collective-permute-done((bf16[272,1536]{1,0:T(8,128)(2,1)}, bf16[272,1536]{1,0:T(8,128)(2,1)}, u32[]{:S(2)}, u32[]{:S(2)}) %collective-permute-start.5) | collective-permute-done | bytes 835616 | tf_op jit(solution)/shard_map/ppermute | solution.py:443
  85.3 11.2 %shard_map.101 = (bf16[512,512]{1,0:T(8,128)(2,1)}, bf16[512,512]{1,0:T(8,128)(2,1)}, bf16[272,1536]{1,0:T(8,128)(2,1)}, bf16[272,1536]{1,0:T(8,128)(2,1)}, bf16...) custom-call(s32[1]{0:T(128)} %bitcast.refs_0_, bf16[272,1536]{1,0:T(8,128)(2,1)} %collective-permute-done.refs_1_.refs_5_, ...), custom_call_target="tpu_custom_call" | custom-call | flops 99999997952 | bytes 100000000 | tf_op jit(solution)/shard_map/pallas_call | solution.py:360
  96.5 1.6 collective-permute-start.22
  101.0 19.1 %shard_map.102 = (bf16[512,512]{1,0:T(8,128)(2,1)}, bf16[512,512]{1,0:T(8,128)(2,1)}, f32[256,1536]{1,0:T(8,128)}, f32[256,1536]{1,0:T(8,128)}, bf16[256,1536]{1...) custom-call(s32[1]{0:T(128)} %bitcast.refs_0_, bf16[272,1536]{1,0:T(8,128)(2,1)} %copy-done, ...), custom_call_target="tpu_custom_call" | custom-call | flops 99999997952 | bytes 100000000 | tf_op jit(solution)/shard_map/pallas_call | solution.py:384
  120.1 1.6 collective-permute-start.20
  122.2 11.4 %shard_map.103 = (bf16[272,1536]{1,0:T(8,128)(2,1)}, bf16[272,1536]{1,0:T(8,128)(2,1)}, bf16[272,1536]{1,0:T(8,128)(2,1)}, bf16[272,1536]{1,0:T(8,128)(2,1)}) custom-call(s32[1]{0:T(128)} %bitcast.refs_0_, f32[512,16]{1,0:T(8,128)} %get-tuple-element.40.refs_1_, bf16[272,1536]{1,0:T(8,128)(2,1)} %copy-done, bf16[272,1536]{1,0:T(8,128)(2,1)} %copy-done.3, ...), custom_call_target="tpu_custom_call" | custom-call | flops 1000 | bytes 1 | tf_op jit(solution)/shard_map/pallas_call | solution.py:409
  133.6 1.5 collective-permute-start.18
  135.1 1.4 collective-permute-done.23
  138.0 2.6 %collective-permute-start.25 = (bf16[272,1536]{1,0:T(8,128)(2,1)S(1)}, bf16[272,1536]{1,0:T(8,128)(2,1)S(1)}, u32[]{:S(2)}, u32[]{:S(2)}) collective-permute-start(bf16[272,1536]{1,0:T(8,128)(2,1)S(1)} %pad_maximum_fusion.2), channel_id=1, source_target_pairs={{0,4},{1,5},{2,6},{3,7},{4,0},{5,1},{6,2},{7,3},{8,12},{9,13},{10,... | collective-permute-start | bytes 2506760 | tf_op jit(solution)/shard_map/ppermute | solution.py:443
  140.5 18.2 %collective-permute-done.20 = bf16[256,1536]{1,0:T(8,128)(2,1)S(1)} collective-permute-done((bf16[256,1536]{1,0:T(8,128)(2,1)}, bf16[256,1536]{1,0:T(8,128)(2,1)S(1)}, u32[]{:S(2)}, u32[]{:S(2)}) %collective-permute-start.20) | collective-permute-done | bytes 786464 | tf_op jit(solution)/shard_map/ppermute | solution.py:443
  158.7 1.8 collective-permute-start.21
  161.9 11.9 %collective-permute-done.26 = bf16[256,1536]{1,0:T(8,128)(2,1)S(1)} collective-permute-done((bf16[256,1536]{1,0:T(8,128)(2,1)}, bf16[256,1536]{1,0:T(8,128)(2,1)S(1)}, u32[]{:S(2)}, u32[]{:S(2)}) %collective-permute-start.26) | collective-permute-done | bytes 786464 | tf_op jit(solution)/shard_map/ppermute | solution.py:443
  173.8 1.4 add_bitcast_fusion
  (86 shorter events, 14.5 us)
Async XLA Ops:
  2.7 23.4 %collective-permute-start.3 = (bf16[272,1536]{1,0:T(8,128)(2,1)S(1)}, bf16[272,1536]{1,0:T(8,128)(2,1)S(1)}, u32[]{:S(2)}, u32[]{:S(2)}) collective-permute-start(bf16[272,1536]{1,0:T(8,128)(2,1)S(1)} %pad_maximum_fusion.1.refs_1_.refs_2_), channel_id=1, source_target_pairs={{0,17},{1,16},{2,19},{3,18},{4,21},{5,20},{6,23},{7,22},{8,25},{9,... | collective-permute-start | bytes 2506760 | tf_op jit(solution)/shard_map/ppermute | solution.py:443
  6.6 36.5 %collective-permute-start.2 = (bf16[272,1536]{1,0:T(8,128)(2,1)S(1)}, bf16[272,1536]{1,0:T(8,128)(2,1)S(1)}, u32[]{:S(2)}, u32[]{:S(2)}) collective-permute-start(bf16[272,1536]{1,0:T(8,128)(2,1)S(1)} %pad_maximum_fusion.1.refs_1_.refs_2_), channel_id=1, source_target_pairs={{0,1},{1,0},{2,3},{3,2},{4,5},{5,4},{6,7},{7,6},{8,9},{9,8},{10,11... | collective-permute-start | bytes 2506760 | tf_op jit(solution)/shard_map/ppermute | solution.py:443
  7.1 36.3 %collective-permute-start.1 = (bf16[272,1536]{1,0:T(8,128)(2,1)S(1)}, bf16[272,1536]{1,0:T(8,128)(2,1)S(1)}, u32[]{:S(2)}, u32[]{:S(2)}) collective-permute-start(bf16[272,1536]{1,0:T(8,128)(2,1)S(1)} %pad_maximum_fusion.1.refs_1_.refs_2_), channel_id=1, source_target_pairs={{0,16},{1,17},{2,18},{3,19},{4,20},{5,21},{6,22},{7,23},{8,24},{9,... | collective-permute-start | bytes 2506760 | tf_op jit(solution)/shard_map/ppermute | solution.py:443
  7.3 38.9 %collective-permute-start = (bf16[272,1536]{1,0:T(8,128)(2,1)S(1)}, bf16[272,1536]{1,0:T(8,128)(2,1)}, u32[]{:S(2)}, u32[]{:S(2)}) collective-permute-start(bf16[272,1536]{1,0:T(8,128)(2,1)S(1)} %pad_maximum_fusion.1.refs_1_.refs_2_), channel_id=1, source_target_pairs={{0,4},{1,5},{2,6},{3,7},{4,0},{5,1},{6,2},{7,3},{8,12},{9,13},{10,... | collective-permute-start | bytes 2506760 | tf_op jit(solution)/shard_map/ppermute | solution.py:443
  10.3 38.4 %collective-permute-start.14 = (bf16[256,1536]{1,0:T(8,128)(2,1)S(1)}, bf16[256,1536]{1,0:T(8,128)(2,1)S(1)}, u32[]{:S(2)}, u32[]{:S(2)}) collective-permute-start(bf16[256,1536]{1,0:T(8,128)(2,1)S(1)} %bitcast.13), channel_id=1, source_target_pairs={{0,8},{1,9},{2,10},{3,11},{4,12},{5,13},{6,14},{7,15},{8,0},{9,1},... | collective-permute-start | bytes 2359304 | tf_op jit(solution)/shard_map/ppermute | solution.py:443
  26.1 36.9 %collective-permute-start.12 = (bf16[256,1536]{1,0:T(8,128)(2,1)S(1)}, bf16[256,1536]{1,0:T(8,128)(2,1)}, u32[]{:S(2)}, u32[]{:S(2)}) collective-permute-start(bf16[256,1536]{1,0:T(8,128)(2,1)S(1)} %bitcast.14), channel_id=1, source_target_pairs={{0,2},{1,3},{2,0},{3,1},{4,6},{5,7},{6,4},{7,5},{8,10},{9,11},{10,... | collective-permute-start | bytes 2359304 | tf_op jit(solution)/shard_map/ppermute | solution.py:443
  43.1 21.4 %collective-permute-start.15 = (bf16[256,1536]{1,0:T(8,128)(2,1)S(1)}, bf16[256,1536]{1,0:T(8,128)(2,1)S(1)}, u32[]{:S(2)}, u32[]{:S(2)}) collective-permute-start(bf16[256,1536]{1,0:T(8,128)(2,1)S(1)} %bitcast.18), channel_id=1, source_target_pairs={{0,8},{1,9},{2,10},{3,11},{4,12},{5,13},{6,14},{7,15},{8,0},{9,1},... | collective-permute-start | bytes 2359304 | tf_op jit(solution)/shard_map/ppermute | solution.py:443
  43.4 34.3 %collective-permute-start.13 = (bf16[256,1536]{1,0:T(8,128)(2,1)S(1)}, bf16[256,1536]{1,0:T(8,128)(2,1)}, u32[]{:S(2)}, u32[]{:S(2)}) collective-permute-start(bf16[256,1536]{1,0:T(8,128)(2,1)S(1)} %bitcast.19), channel_id=1, source_target_pairs={{0,2},{1,3},{2,0},{3,1},{4,6},{5,7},{6,4},{7,5},{8,10},{9,11},{10,... | collective-permute-start | bytes 2359304 | tf_op jit(solution)/shard_map/ppermute | solution.py:443
  46.1 34.3 %collective-permute-start.6 = (bf16[272,1536]{1,0:T(8,128)(2,1)}, bf16[272,1536]{1,0:T(8,128)(2,1)}, u32[]{:S(2)}, u32[]{:S(2)}) collective-permute-start(bf16[272,1536]{1,0:T(8,128)(2,1)} %collective-permute-done.refs_1_.refs_5_), channel_id=1, source_target_pairs={{0,17},{1,16},{2,19},{3,18},{4,21},{5,20},{6,23},{7,22},{8,25},{9,... | collective-permute-start | bytes 2506760 | tf_op jit(solution)/shard_map/ppermute | solution.py:443
  48.7 36.1 %collective-permute-start.5 = (bf16[272,1536]{1,0:T(8,128)(2,1)}, bf16[272,1536]{1,0:T(8,128)(2,1)}, u32[]{:S(2)}, u32[]{:S(2)}) collective-permute-start(bf16[272,1536]{1,0:T(8,128)(2,1)} %collective-permute-done.refs_1_.refs_5_), channel_id=1, source_target_pairs={{0,1},{1,0},{2,3},{3,2},{4,5},{5,4},{6,7},{7,6},{8,9},{9,8},{10,11... | collective-permute-start | bytes 2506760 | tf_op jit(solution)/shard_map/ppermute | solution.py:443
  63.1 21.8 %collective-permute-start.4 = (bf16[272,1536]{1,0:T(8,128)(2,1)}, bf16[272,1536]{1,0:T(8,128)(2,1)}, u32[]{:S(2)}, u32[]{:S(2)}) collective-permute-start(bf16[272,1536]{1,0:T(8,128)(2,1)} %collective-permute-done.refs_1_.refs_5_), channel_id=1, source_target_pairs={{0,16},{1,17},{2,18},{3,19},{4,20},{5,21},{6,22},{7,23},{8,24},{9,... | collective-permute-start | bytes 2506760 | tf_op jit(solution)/shard_map/ppermute | solution.py:443
  79.7 16.9 %collective-permute-start.8 = (bf16[272,1536]{1,0:T(8,128)(2,1)}, bf16[272,1536]{1,0:T(8,128)(2,1)S(1)}, u32[]{:S(2)}, u32[]{:S(2)}) collective-permute-start(bf16[272,1536]{1,0:T(8,128)(2,1)} %collective-permute-done.refs_1_.refs_5_), channel_id=1, source_target_pairs={{0,8},{1,9},{2,10},{3,11},{4,12},{5,13},{6,14},{7,15},{8,0},{9,1},... | collective-permute-start | bytes 2506760 | tf_op jit(solution)/shard_map/ppermute | solution.py:443
  80.3 19.8 %collective-permute-start.7 = (bf16[1088,1536]{1,0:T(8,128)(2,1)}, bf16[1088,1536]{1,0:T(8,128)(2,1)}, u32[]{:S(2)}, u32[]{:S(2)}) collective-permute-start(bf16[1088,1536]{1,0:T(8,128)(2,1)} %pad_maximum_fusion), channel_id=1, source_target_pairs={{0,8},{1,9},{2,10},{3,11},{4,12},{5,13},{6,14},{7,15},{8,0},{9,1},... | collective-permute-start | bytes 10027016 | tf_op jit(solution)/shard_map/ppermute | solution.py:443
  80.5 17.6 %collective-permute-start.11 = (bf16[272,1536]{1,0:T(8,128)(2,1)}, bf16[272,1536]{1,0:T(8,128)(2,1)S(1)}, u32[]{:S(2)}, u32[]{:S(2)}) collective-permute-start(bf16[272,1536]{1,0:T(8,128)(2,1)} %collective-permute-done.6.refs_4_.refs_8_), channel_id=1, source_target_pairs={{0,8},{1,9},{2,10},{3,11},{4,12},{5,13},{6,14},{7,15},{8,0},{9,1},... | collective-permute-start | bytes 2506760 | tf_op jit(solution)/shard_map/ppermute | solution.py:443
  84.9 15.2 %collective-permute-start.9 = (bf16[272,1536]{1,0:T(8,128)(2,1)}, bf16[272,1536]{1,0:T(8,128)(2,1)S(1)}, u32[]{:S(2)}, u32[]{:S(2)}) collective-permute-start(bf16[272,1536]{1,0:T(8,128)(2,1)} %collective-permute-done.4.refs_2_.refs_6_), channel_id=1, source_target_pairs={{0,8},{1,9},{2,10},{3,11},{4,12},{5,13},{6,14},{7,15},{8,0},{9,1},... | collective-permute-start | bytes 2506760 | tf_op jit(solution)/shard_map/ppermute | solution.py:443
  96.5 37.0 %collective-permute-start.22 = (bf16[272,1536]{1,0:T(8,128)(2,1)}, bf16[272,1536]{1,0:T(8,128)(2,1)S(1)}, u32[]{:S(2)}, u32[]{:S(2)}) collective-permute-start(bf16[272,1536]{1,0:T(8,128)(2,1)} %get-tuple-element.50), channel_id=1, source_target_pairs={{0,16},{1,17},{2,18},{3,19},{4,20},{5,21},{6,22},{7,23},{8,24},{9,... | collective-permute-start | bytes 2506760 | tf_op jit(solution)/shard_map/ppermute | solution.py:443
  98.1 38.4 %collective-permute-start.23 = (bf16[272,1536]{1,0:T(8,128)(2,1)}, bf16[272,1536]{1,0:T(8,128)(2,1)S(1)}, u32[]{:S(2)}, u32[]{:S(2)}) collective-permute-start(bf16[272,1536]{1,0:T(8,128)(2,1)} %get-tuple-element.51), channel_id=1, source_target_pairs={{0,1},{1,0},{2,3},{3,2},{4,5},{5,4},{6,7},{7,6},{8,9},{9,8},{10,11... | collective-permute-start | bytes 2506760 | tf_op jit(solution)/shard_map/ppermute | solution.py:443
  98.9 38.4 %collective-permute-start.24 = (bf16[272,1536]{1,0:T(8,128)(2,1)}, bf16[272,1536]{1,0:T(8,128)(2,1)S(1)}, u32[]{:S(2)}, u32[]{:S(2)}) collective-permute-start(bf16[272,1536]{1,0:T(8,128)(2,1)} %get-tuple-element.52), channel_id=1, source_target_pairs={{0,17},{1,16},{2,19},{3,18},{4,21},{5,20},{6,23},{7,22},{8,25},{9,... | collective-permute-start | bytes 2506760 | tf_op jit(solution)/shard_map/ppermute | solution.py:443
  120.1 38.7 %collective-permute-start.20 = (bf16[256,1536]{1,0:T(8,128)(2,1)}, bf16[256,1536]{1,0:T(8,128)(2,1)S(1)}, u32[]{:S(2)}, u32[]{:S(2)}) collective-permute-start(bf16[256,1536]{1,0:T(8,128)(2,1)} %get-tuple-element.47), channel_id=1, source_target_pairs={{0,2},{1,3},{2,0},{3,1},{4,6},{5,7},{6,4},{7,5},{8,10},{9,11},{10,... | collective-permute-start | bytes 2359304 | tf_op jit(solution)/shard_map/ppermute | solution.py:443
  121.7 52.1 %collective-permute-start.26 = (bf16[256,1536]{1,0:T(8,128)(2,1)}, bf16[256,1536]{1,0:T(8,128)(2,1)S(1)}, u32[]{:S(2)}, u32[]{:S(2)}) collective-permute-start(bf16[256,1536]{1,0:T(8,128)(2,1)} %get-tuple-element.53), channel_id=1, source_target_pairs={{0,2},{1,3},{2,0},{3,1},{4,6},{5,7},{6,4},{7,5},{8,10},{9,11},{10,... | collective-permute-start | bytes 2359304 | tf_op jit(solution)/shard_map/ppermute | solution.py:443
  133.6 41.6 %collective-permute-start.18 = (bf16[272,1536]{1,0:T(8,128)(2,1)}, bf16[272,1536]{1,0:T(8,128)(2,1)S(1)}, u32[]{:S(2)}, u32[]{:S(2)}) collective-permute-start(bf16[272,1536]{1,0:T(8,128)(2,1)} %get-tuple-element.44), channel_id=1, source_target_pairs={{0,16},{1,17},{2,18},{3,19},{4,20},{5,21},{6,22},{7,23},{8,24},{9,... | collective-permute-start | bytes 2506760 | tf_op jit(solution)/shard_map/ppermute | solution.py:443
  136.5 38.7 %collective-permute-start.19 = (bf16[272,1536]{1,0:T(8,128)(2,1)}, bf16[272,1536]{1,0:T(8,128)(2,1)S(1)}, u32[]{:S(2)}, u32[]{:S(2)}) collective-permute-start(bf16[272,1536]{1,0:T(8,128)(2,1)} %get-tuple-element.45), channel_id=1, source_target_pairs={{0,1},{1,0},{2,3},{3,2},{4,5},{5,4},{6,7},{7,6},{8,9},{9,8},{10,11... | collective-permute-start | bytes 2506760 | tf_op jit(solution)/shard_map/ppermute | solution.py:443
  138.0 37.2 %collective-permute-start.25 = (bf16[272,1536]{1,0:T(8,128)(2,1)S(1)}, bf16[272,1536]{1,0:T(8,128)(2,1)S(1)}, u32[]{:S(2)}, u32[]{:S(2)}) collective-permute-start(bf16[272,1536]{1,0:T(8,128)(2,1)S(1)} %pad_maximum_fusion.2), channel_id=1, source_target_pairs={{0,4},{1,5},{2,6},{3,7},{4,0},{5,1},{6,2},{7,3},{8,12},{9,13},{10,... | collective-permute-start | bytes 2506760 | tf_op jit(solution)/shard_map/ppermute | solution.py:443
  158.7 16.4 %collective-permute-start.21 = (bf16[272,1536]{1,0:T(8,128)(2,1)S(1)}, bf16[272,1536]{1,0:T(8,128)(2,1)S(1)}, u32[]{:S(2)}, u32[]{:S(2)}) collective-permute-start(bf16[272,1536]{1,0:T(8,128)(2,1)S(1)} %copy-done.13), channel_id=1, source_target_pairs={{0,17},{1,16},{2,19},{3,18},{4,21},{5,20},{6,23},{7,22},{8,25},{9,... | collective-permute-start | bytes 2506760 | tf_op jit(solution)/shard_map/ppermute | solution.py:443
  (21 other events, 412.2 us)
